TPU v7x, 128 devices: a whole 4x4x4 slice. The times are simulated.
128 devices in a mesh: row: 8 (over y_lo, z), col: 8 (over x, y_hi), depth: 2 (over core).
Axes of the slice: x: 4, y: 4 (y_hi: 2, y_lo: 2; y = y_hi * 2 + y_lo), z: 4, core: 2. Of those that a mesh axis runs over, the one named last changes fastest.
Arguments:
- quant_codes: int32 [12288, 6144], P(('row', 'depth'), 'col'), may hold values from 0 to 15
- block_scales: float32 [96, 12288], P('col', ('row', 'depth')), may hold values from 0.14 to 0.3
Outputs:
- rectified: bfloat16 [12288, 6144], P(('row', 'depth'), 'col')
- gram_matrix: bfloat16 [6144, 6144], P(('row', 'depth'), 'col')
All inputs are finite; a program needn't handle non-finite values.
Results may differ from a plain program's by a relative error of at most 0.0059.
Values may be sent and summed in bfloat16 or wider, within the bound.
No kernel may reach another device: no remote copies, remote signals or barrier semaphores. Data moves between devices by JAX's collectives and lax.ppermute only.
A program may use at most 128 MiB of HBM per device.

v0:
```python
import jax
import jax.numpy as jnp
from jax import lax
from jax.sharding import PartitionSpec as P

N = 12288
BLOCK = 64


def body(quant_codes, block_scales):
    row_count, col_count = quant_codes.shape
    levels = quant_codes.astype(jnp.float32).reshape(row_count, col_count // BLOCK, BLOCK) - 7.5
    factor = jnp.transpose(block_scales)
    basis_tile = (levels * factor[:, :, None]).reshape(row_count, col_count).astype(jnp.bfloat16)
    row_panel = lax.all_gather(basis_tile, "col", axis=1, tiled=True)
    columns = row_panel
    gram_sum = lax.psum_scatter(
        lax.dot_general(
            columns, basis_tile, (((0,), (0,)), ((), ())), preferred_element_type=jnp.float32
        ),
        ("row", "depth"),
        scatter_dimension=0,
        tiled=True,
    )
    gram_owned = (gram_sum * (1.0 / N)).astype(jnp.bfloat16)
    columns = row_panel
    product = jnp.dot(
        columns,
        lax.all_gather(gram_owned, ("row", "depth"), axis=0, tiled=True),
        preferred_element_type=jnp.float32,
    )
    rectified = (1.5 * basis_tile.astype(jnp.float32) - 0.5 * product).astype(jnp.bfloat16)
    return (rectified, gram_owned)


def solution(mesh):
    return jax.shard_map(
        body,
        mesh=mesh,
        in_specs=(P(("row", "depth"), "col"), P("col", ("row", "depth"))),
        out_specs=(P(("row", "depth"), "col"), P(("row", "depth"), "col")),
        check_vma=False,
    )
```

profile of v0, /device:TPU:1, one launch (start us, length us, event | category | flops | bytes accessed | tf_op | source)
XLA Modules:
  0.0 334.5 jit_solution(17455816664108170384)
XLA Ops:
  7.2 0.0 all-gather.3.cloned.1.call-start
  7.2 1.0 mul.29
  8.2 2.0 copy.5
  10.2 3.7 %multiply_convert_fusion = bf16[768,768]{1,0:T(8,128)(2,1)} fusion(f32[768,768]{1,0:T(8,128)} %copy.5, s32[768,768]{1,0:T(8,128)} %param.2), kind=kLoop, calls=%fused_computation.1 | loop fusion | flops 2359296 | bytes 5898240 | tf_op jit(solution)/shard_map/convert_element_type | solution.py:14
  13.9 0.0 all-gather.3.cloned.1.call-update
  13.9 0.0 reduce-scatter.2.cloned.1.call-start
  13.9 120.3 %all-gather.3.cloned.1.call-done = bf16[768,6144]{1,0:T(8,128)(2,1)} async-done(((bf16[768,768]{1,0:T(8,128)(2,1)}), bf16[768,6144]{1,0:T(8,128)(2,1)}) %all-gather.3.cloned.1.call-update) | async-done | bytes 9437200 | tf_op jit(solution)/shard_map/all_gather | solution.py:15
  134.2 14.2 %fusion = f32[6144,768]{1,0:T(8,128)} fusion(bf16[768,6144]{1,0:T(8,128)(2,1)} %all-gather.3.cloned.1.call-done, bf16[768,768]{1,0:T(8,128)(2,1)} %multiply_convert_fusion), kind=kOutput, calls=%fused_computation.3 | convolution fusion | flops 7247757312 | bytes 29491200 | tf_op jit(solution)/shard_map/dot_general | solution.py:18
  148.4 0.0 reduce-scatter.2.cloned.1.call-update
  148.4 0.0 copy-start
  148.4 0.0 all-gather.5.cloned.1.call-start
  148.5 105.9 %reduce-scatter.2.cloned.1.call-done = f32[384,768]{1,0:T(8,128)} async-done(((f32[6144,768]{1,0:T(8,128)}), f32[384,768]{1,0:T(8,128)}) %reduce-scatter.2.cloned.1.call-update) | async-done | bytes 1179664 | tf_op jit(solution)/shard_map/reduce_scatter | solution.py:17
  254.4 2.2 multiply_convert_fusion.1
  256.6 0.0 all-gather.5.cloned.1.call-update
  256.6 57.8 %all-gather.5.cloned.1.call-done = bf16[6144,768]{1,0:T(8,128)(2,1)} async-done(((bf16[384,768]{1,0:T(8,128)(2,1)}), bf16[6144,768]{1,0:T(8,128)(2,1)}) %all-gather.5.cloned.1.call-update) | async-done | bytes 9437200 | tf_op jit(solution)/shard_map/all_gather | solution.py:29
  314.4 0.0 copy-done
  314.4 13.6 %subtract_convert_fusion = bf16[768,768]{1,0:T(8,128)(2,1)} fusion(bf16[768,768]{1,0:T(8,128)(2,1)S(1)} %copy-done, bf16[768,6144]{1,0:T(8,128)(2,1)} %all-gather.3.cloned.1.call-done, bf16[6144,768]{1,0:T(8,128)(2,1)} %all-gather.5.cloned.1.call-done), kind=kOutput, calls=%fused_computation | convolution fusion | flops 7250706432 | bytes 21233664 | tf_op jit(solution)/shard_map/dot_general | solution.py:27
Async XLA Ops:
  7.2 127.1 %all-gather.3.cloned.1.call-start = ((), (), s32[]{:S(2)}) async-start(), calls=%async_computation.1 | async-start | bytes 10616832 | tf_op jit(solution)/shard_map/all_gather | solution.py:15
  13.9 240.5 %reduce-scatter.2.cloned.1.call-start = ((), (), s32[]{:S(2)}) async-start(), calls=%async_computation.2 | async-start | bytes 20054016 | tf_op jit(solution)/shard_map/reduce_scatter | solution.py:17
  148.4 166.0 %copy-start = (bf16[768,768]{1,0:T(8,128)(2,1)S(1)}, bf16[768,768]{1,0:T(8,128)(2,1)}, u32[]{:S(2)}) copy-start(bf16[768,768]{1,0:T(8,128)(2,1)} %multiply_convert_fusion) | copy-start | bytes 3538948
  148.4 166.0 %all-gather.5.cloned.1.call-start = ((), (), s32[]{:S(2)}) async-start(), calls=%async_computation.3 | async-start | bytes 10027008 | tf_op jit(solution)/shard_map/all_gather | solution.py:29
Sparse Core Ops, SparseCore 0:
  14.0 120.1 all-gather.2
  148.5 105.8 reduce-scatter.1
  256.7 57.6 all-gather.4
where the time goes:
time: 335 us
  waiting for transfers between devices  284 us (85%)
  matrix products  27.7 us (8%)
  between operations  13.8 us (4%)
  other arithmetic  5.88 us (2%)
    all_gather x1, waiting for transfers between devices, body(): row_panel = lax.all_gather(basis_tile, 'col', axis=1, tiled=True)  120 us
    reduce_scatter x1, waiting for transfers between devices, body(): lax.psum_scatter(lax.dot_general(columns, basis_tile, (((0,), (0,)), ((),...  106 us
    all_gather x1, waiting for transfers between devices, body(): lax.all_gather(gram_owned, ('row', 'depth'), axis=0, tiled=True)  57.8 us
    dot_general x1, matrix products, body(): lax.dot_general(columns, basis_tile, (((0,), (0,)), ((), ())), preferred_...  14.2 us
    dot_general x1, matrix products, body(): jnp.dot(columns, lax.all_gather(gram_owned, ('row', 'depth'), axis=0, til...  13.6 us
  transfers between devices with their start and end apart: 3, of which 3 were waited for; matrix products, arithmetic and copies ran while one was open for 0% of the time, Pallas kernels for 0%

commit v1 on v0

v1 whole, which is shorter than its diff:
```python
import functools

import jax
import jax.numpy as jnp
from jax import lax
from jax.experimental import pallas as pl
from jax.experimental.pallas import tpu as pltpu
from jax.sharding import Mesh, PartitionSpec as P

N = 12288
BLOCK = 64
AXES = ("yl", "z", "x", "yh", "core")
F32, BF16 = jnp.float32, jnp.bfloat16
T = 768
H = T // 2
S = 48
VMEM = pl.BlockSpec(memory_space=pltpu.VMEM)
ANY = pl.BlockSpec(memory_space=pl.ANY)


def ring(axis, step):
    return lambda a: lax.ppermute(a, axis, [(i, (i + step) % 4) for i in range(4)])


def swap(axis):
    return lambda a: lax.ppermute(a, axis, [(0, 1), (1, 0)])


def tdot(a, b):
    return lax.dot_general(a, b, (((0,), (0,)), ((), ())), preferred_element_type=F32)


def dot(a, b):
    return jnp.dot(a, b, preferred_element_type=F32)


def dot_t(a, b):
    return lax.dot_general(a, b, (((1,), (1,)), ((), ())), preferred_element_type=F32)


def params(mib):
    return pltpu.CompilerParams(vmem_limit_bytes=mib << 20)


def cost(flops, size):
    return pl.CostEstimate(flops=flops, bytes_accessed=size, transcendentals=0)


def dequant_kernel(codes, scales, out):
    factor = scales[...].T
    lane = lax.broadcasted_iota(jnp.int32, (T, 128), 1)
    for g in range(T // 128):
        both = jnp.where(lane < BLOCK, factor[:, 2 * g : 2 * g + 1], factor[:, 2 * g + 1 : 2 * g + 2])
        levels = codes[:, 128 * g : 128 * (g + 1)].astype(F32) - 7.5
        out[:, 128 * g : 128 * (g + 1)] = (levels * both).astype(BF16)


def dequant(codes, scales):
    return pl.pallas_call(
        dequant_kernel,
        out_shape=jax.ShapeDtypeStruct((T, T), BF16),
        in_specs=[VMEM, VMEM],
        out_specs=VMEM,
        compiler_params=params(24),
        cost_estimate=cost(2 * T * T, 6 * T * T),
    )(codes, scales)


def cut(full, first, count, keep, send):
    z, k = lax.axis_index("z"), lax.axis_index("core")
    for half in range(count):
        for j in range(4):
            at = half * H + lax.rem(z + j, 4) * S
            to = pl.ds((first + half) * S, S)
            keep[j, to, :] = full[pl.ds(pl.multiple_of(at + k * (4 * S), 16), S), :].astype(BF16)
            send[j, to, :] = full[pl.ds(pl.multiple_of(at + (1 - k) * (4 * S), 16), S), :].astype(BF16)


def gram_kernel0(own, keep, send, full):
    full[...] = tdot(own[...], own[...])
    cut(full, 0, 2, keep, send)


def gram_kernel1(own, near1, far, keep, send, full):
    turned = near1[...].T
    full[...] = dot(turned, own[...])
    cut(full, 0, 2, keep, send)
    full[...] = dot(turned, far[...])
    cut(full, 2, 2, keep, send)
    h = lax.axis_index("yh")

    @pl.when(h == 0)
    def _():
        full[0:H, :] = tdot(far[:, 0:H], own[...])

    @pl.when(h != 0)
    def _():
        full[0:H, :] = tdot(own[:, H:T], far[...])

    cut(full, 4, 1, keep, send)


def gram_kernel2(own, far, near2a, near2b, keep, send, full):
    low = lax.axis_index("x") < 2
    for i, other in enumerate((own, far)):

        @pl.when(low)
        def _():
            full[0:H, :] = tdot(near2a[:, 0:H], other[0:H, :]) + tdot(near2b[:, 0:H], other[H:T, :])

        @pl.when(jnp.logical_not(low))
        def _():
            full[0:H, :] = tdot(other[0:H, H:T], near2a[...]) + tdot(other[H:T, H:T], near2b[...])

        cut(full, i, 1, keep, send)


def gram(kernel, halves, *tiles):
    out = jax.ShapeDtypeStruct((4, halves * S, T), BF16)
    return pl.pallas_call(
        kernel,
        out_shape=(out, out),
        in_specs=[VMEM] * len(tiles),
        out_specs=(VMEM, VMEM),
        scratch_shapes=[pltpu.VMEM((T, T), F32)],
        compiler_params=params(32),
        cost_estimate=cost(halves * T * T * T, 6 * T * T),
    )(*tiles)


PIECES = (2, 10, 4)


def product_kernel(*refs):
    own, near1, near3, far3, far1, far, near2a, near2b, far2a, far2b = refs[:10]
    slices = refs[10 : 10 + 24]
    out, gram_out = refs[34:36]
    a, g, acc, a_sem, g_sem = refs[36:]
    z, k, h = lax.axis_index("z"), lax.axis_index("core"), lax.axis_index("yh")
    x, yl = lax.axis_index("x"), lax.axis_index("yl")
    low = x < 2

    a_copies = []
    for i, src in enumerate((own, near1, near3, far3, far1, far)):
        a_copies.append([pltpu.make_async_copy(src, a.at[i], a_sem.at[i])])
    for i, (top, bottom) in ((6, (near2a, near2b)), (7, (far2a, far2b))):
        a_copies.append(
            [
                pltpu.make_async_copy(top, a.at[i, pl.ds(0, H)], a_sem.at[i]),
                pltpu.make_async_copy(bottom, a.at[i, pl.ds(H, H)], a_sem.at[i + 2]),
            ]
        )
    g_copies, first = [], 0
    for p, count in enumerate(PIECES):
        piece = []
        for c in range(2):
            for j in range(4):
                src = slices[p * 8 + c * 4 + j]
                core = k if c == 0 else 1 - k
                at = pl.multiple_of(core * (4 * S) + lax.rem(z + j, 4) * S, 16)
                piece.append(
                    pltpu.make_async_copy(src, g.at[pl.ds(first, count), pl.ds(at, S)], g_sem.at[p * 8 + c * 4 + j])
                )
        g_copies.append(piece)
        first += count
    for group in a_copies + g_copies:
        for copy in group:
            copy.start()

    def tile(t):
        return g[2 * t : 2 * t + 2].reshape(T, T)

    def add(t, turn):
        for copy in a_copies[t]:
            copy.wait()
        if isinstance(turn, bool):
            acc[...] += dot_t(a[t], tile(t)) if turn else dot(a[t], tile(t))
            return

        @pl.when(turn)
        def _():
            acc[...] += dot_t(a[t], tile(t))

        @pl.when(jnp.logical_not(turn))
        def _():
            acc[...] += dot(a[t], tile(t))

    for copy in g_copies[0]:
        copy.wait()
    for copy in a_copies[0]:
        copy.wait()
    acc[...] = dot(a[0], tile(0))
    for copy in g_copies[1]:
        copy.wait()
    add(1, False)
    add(2, True)
    add(3, True)
    add(4, False)
    add(5, h != 0)
    for copy in g_copies[2]:
        copy.wait()
    add(6, x >= 2)
    add(7, x >= 2)
    out[...] = (1.5 * a[0].astype(F32) - 0.5 * acc[...]).astype(BF16)

    line = yl * 4 + z
    dx, dh = lax.rem(line // 2 - x + 4, 4), lax.rem(lax.rem(line, 2) + h, 2)
    where = ((0, 5), (1, 4), (6, 7), (2, 3))
    which = jnp.int32(0)
    for i, pair in enumerate(where):
        for j, t in enumerate(pair):
            which = jnp.where((dx == i) & (dh == j), t, which)
    turn = (which == 2) | (which == 3) | ((which == 5) & (h != 0)) | ((which >= 6) & (x >= 2))

    @pl.when(jnp.logical_not(turn))
    def _():
        gram_out[...] = g[2 * which + k]

    for side in range(2):

        @pl.when(turn & (k == side))
        def _():
            columns = g[pl.ds(2 * which, 2), :, side * H : (side + 1) * H].reshape(T, H)
            gram_out[...] = columns.T


def product(tiles, slices):
    return pl.pallas_call(
        product_kernel,
        out_shape=(jax.ShapeDtypeStruct((T, T), BF16), jax.ShapeDtypeStruct((H, T), BF16)),
        in_specs=[ANY] * (len(tiles) + len(slices)),
        out_specs=(VMEM, VMEM),
        scratch_shapes=[
            pltpu.VMEM((8, T, T), BF16),
            pltpu.VMEM((16, H, T), BF16),
            pltpu.VMEM((T, T), F32),
            pltpu.SemaphoreType.DMA((10,)),
            pltpu.SemaphoreType.DMA((24,)),
        ],
        compiler_params=params(40),
        cost_estimate=cost(16 * T * T * T, 36 * T * T),
    )(*tiles, *slices)


def reduce(keep, send):
    other = swap("core")(send)
    sums = [keep[j].astype(F32) + other[j].astype(F32) for j in range(4)]
    got = [ring("z", j)(sums[j].astype(BF16)) for j in (1, 3, 2)]
    total = sums[0]
    for piece in got:
        total = total + piece.astype(F32)
    total = total.astype(BF16)
    total = total.astype(F32) + swap("yl")(total).astype(F32)
    return (total * (1.0 / N)).astype(BF16)


def spread(*parts):
    shard = jnp.concatenate(parts).reshape(-1, S, T)
    mine = [shard] + [ring("z", -j)(shard) for j in (1, 2, 3)]
    return mine + [swap("core")(a) for a in mine]


def body(quant_codes, block_scales):
    h, low = lax.axis_index("yh"), lax.axis_index("x") < 2
    own = dequant(quant_codes, block_scales)

    near1 = ring("x", -1)(own)
    near3 = ring("x", 1)(own)
    far = swap("yh")(own)
    shard0 = reduce(*gram(gram_kernel0, 2, own))
    slices0 = spread(shard0)
    near2 = [ring("x", -1)(near1[:H]), ring("x", 1)(near3[H:])]

    keep, send = gram(gram_kernel1, 5, own, near1, far)
    shard = reduce(keep, send)
    later, _, _ = lax.optimization_barrier((far, near2[0], near2[1]))
    far1 = ring("x", -1)(later)
    far3 = ring("x", 1)(later)
    far2 = [ring("x", -1)(far1[:H]), ring("x", 1)(far3[H:])]
    mine = shard[4 * S :]
    from_x = ring("x", 1)(shard[: 4 * S])
    from_y = swap("yh")(shard[2 * S :])
    theirs = from_y[2 * S :]
    slices1 = spread(
        shard[: 2 * S], from_x, from_y[: 2 * S], jnp.where(h == 0, mine, theirs), jnp.where(h == 0, theirs, mine)
    )

    shard = reduce(*gram(gram_kernel2, 2, own, far, *near2))
    from_x = ring("x", 2)(shard)
    from_y = swap("yh")(shard[S:])
    mine, theirs = jnp.concatenate([shard[:S], from_y]), from_x
    first, second = jnp.where(low, mine, theirs), jnp.where(low, theirs, mine)
    slices2 = spread(first[:S], second[:S], first[S:], second[S:])

    return product([own, near1, near3, far3, far1, far] + near2 + far2, slices0 + slices1 + slices2)


def solution(mesh):
    split = Mesh(mesh.devices.reshape(2, 4, 4, 2, 2), AXES)
    line, side = ("yl", "z", "core"), ("x", "yh")
    return jax.shard_map(
        body,
        mesh=split,
        in_specs=(P(line, side), P(side, line)),
        out_specs=(P(line, side), P(line, side)),
        check_vma=False,
    )
```

time: 335 us -> 231 us (0.69)
  waiting for transfers between devices: 284 us -> 122 us
  starting transfers between devices: 0.12 us -> 69.3 us
  matrix products: 27.7 us -> 0 us
  Pallas kernels: 0 us -> 25.4 us
  between operations: 13.8 us -> 1.13 us
    all_gather x2 -> x0, waiting for transfers between devices: 178 us -> none  [the longest x1 120 us: body(): row_panel = lax.all_gather(basis_tile, 'col', axis=1, tiled=True)]
    ppermute x0 -> x49, waiting for transfers between devices: none -> 122 us  [the longest x28 115 us: ring(): lax.ppermute(a, axis, [(i, (i + step) % 4) for i in range(4)])]
    reduce_scatter x1 -> x0, waiting for transfers between devices: 106 us -> none  [body(): lax.psum_scatter(lax.dot_general(columns, basis_tile, (((0,), (0,)), ((),...]
    ppermute x0 -> x49, starting transfers between devices: none -> 69.3 us  [the longest x28 42.2 us: ring(): lax.ppermute(a, axis, [(i, (i + step) % 4) for i in range(4)])]
    dot_general x2 -> x0, matrix products: 27.7 us -> none  [the longest x1 14.2 us: body(): lax.dot_general(columns, basis_tile, (((0,), (0,)), ((), ())), preferred_...]
    pallas_call x0 -> x5, Pallas kernels: none -> 25.4 us  [the longest x1 15.1 us: product(): pl.pallas_call(product_kernel, out_shape=(jax.ShapeDtypeStruct((T, T), BF...]
    unnamed x2 -> x31, local copies, waits for them, and re-layouts: 0.01 us -> 4.73 us
    convert_element_type x2 -> x9, other arithmetic: 5.88 us -> 7.6 us  [the longest x3 4.05 us: reduce(): got = [ring('z', j)(sums[j].astype(BF16)) for j in (1, 3, 2)]]
  transfers between devices with their start and end apart: 3 -> 49, of which waited for: 3 -> 19; matrix products, arithmetic and copies ran while one was open for 0% -> 3% of each run, Pallas kernels for 0% -> 4%
where the time goes in v1:
time: 231 us
  waiting for transfers between devices  122 us (53%)
  starting transfers between devices  69.3 us (30%)
  Pallas kernels  25.4 us (11%)
  other arithmetic  7.71 us (3%)
  local copies, waits for them, and re-layouts  4.96 us (2%)
    ppermute x28, waiting for transfers between devices, ring(): lax.ppermute(a, axis, [(i, (i + step) % 4) for i in range(4)])  115 us
    ppermute x28, starting transfers between devices, ring(): lax.ppermute(a, axis, [(i, (i + step) % 4) for i in range(4)])  42.2 us
    ppermute x21, starting transfers between devices, swap(): return lambda a: lax.ppermute(a, axis, [(0, 1), (1, 0)])  27 us
    pallas_call x1, Pallas kernels, product(): pl.pallas_call(product_kernel, out_shape=(jax.ShapeDtypeStruct((T, T), BF...  15.1 us
    pallas_call x3, Pallas kernels, gram(): pl.pallas_call(kernel, out_shape=(out, out), in_specs=[VMEM] * len(tiles)...  8.84 us
    ppermute x21, waiting for transfers between devices, swap(): return lambda a: lax.ppermute(a, axis, [(0, 1), (1, 0)])  7.75 us
    unnamed x31, local copies, waits for them, and re-layouts  4.73 us
  transfers between devices with their start and end apart: 49, of which 19 were waited for; matrix products, arithmetic and copies ran while one was open for 3% of the time, Pallas kernels for 4%

profile of v1, /device:TPU:1, one launch (start us, length us, event | category | flops | bytes accessed | tf_op | source)
XLA Modules:
  0.0 230.9 jit_solution(13631184852047121558)
XLA Ops:
  4.5 2.1 collective-permute-start.1
  8.0 3.0 %collective-permute-start.2 = (bf16[768,768]{1,0:T(8,128)(2,1)S(1)}, bf16[768,768]{1,0:T(8,128)(2,1)S(1)}, u32[]{:S(2)}, u32[]{:S(2)}) collective-permute-start(bf16[768,768]{1,0:T(8,128)(2,1)S(1)} %shard_map.41.own.refs_0_), channel_id=1, source_target_pairs={{0,2},{2,0},{1,3},{3,1},{4,6},{6,4},{5,7},{7,5},{8,10},{10,8},{9,1... | collective-permute-start | bytes 3538952 | tf_op jit(solution)/shard_map/ppermute | solution.py:26
  11.0 22.1 %collective-permute-done.1.refs_2_ = bf16[768,768]{1,0:T(8,128)(2,1)S(1)} collective-permute-done((bf16[768,768]{1,0:T(8,128)(2,1)S(1)}, bf16[768,768]{1,0:T(8,128)(2,1)S(1)}, u32[]{:S(2)}, u32[]{:S(2)}) %collective-permute-start.1) | collective-permute-done | bytes 1179680 | tf_op jit(solution)/shard_map/ppermute | solution.py:22
  36.1 2.1 shard_map.42
  38.9 2.2 collective-permute-start.9
  41.2 4.1 %shard_map.43 = (bf16[4,240,768]{2,1,0:T(8,128)(2,1)S(1)}, bf16[4,240,768]{2,1,0:T(8,128)(2,1)}) custom-call(bf16[768,768]{1,0:T(8,128)(2,1)S(1)} %shard_map.41.own.refs_0_, bf16[768,768]{1,0:T(8,128)(2,1)S(1)} %collective-permute-done.near1.refs_1_, bf16[768,768]{1,0:T(8,128)(2,1)S(1)} %collective-permute-done.2.far.refs_5_), custom_call_target="tpu_custom_call" | custom-call | flops 2264924160 | bytes 3538944 | tf_op jit(solution)/shard_map/pallas_call | solution.py:120
  45.3 2.3 collective-permute-done.4.near2b.refs_7_
  47.7 2.7 %shard_map.44 = (bf16[4,96,768]{2,1,0:T(8,128)(2,1)S(1)}, bf16[4,96,768]{2,1,0:T(8,128)(2,1)}) custom-call(bf16[768,768]{1,0:T(8,128)(2,1)S(1)} %shard_map.41.own.refs_0_, bf16[768,768]{1,0:T(8,128)(2,1)S(1)} %collective-permute-done.2.far.refs_5_, bf16[384,768]{1,0:T(8,128)(2,1)S(1)} %collective-permute-done.3.near2a.refs_6_, ...), custom_call_target="tpu_custom_call" | custom-call | flops 905969664 | bytes 3538944 | tf_op jit(solution)/shard_map/pallas_call | solution.py:120
  51.1 2.6 %collective-permute-start.35 = (bf16[4,96,768]{2,1,0:T(8,128)(2,1)}, bf16[4,96,768]{2,1,0:T(8,128)(2,1)}, u32[]{:S(2)}, u32[]{:S(2)}) collective-permute-start(bf16[4,96,768]{2,1,0:T(8,128)(2,1)} %get-tuple-element.15), channel_id=1, source_target_pairs={{0,1},{1,0},{2,3},{3,2},{4,5},{5,4},{6,7},{7,6},{8,9},{9,8},{10,11... | collective-permute-start | bytes 1769480 | tf_op jit(solution)/shard_map/ppermute | solution.py:26
  55.1 2.0 collective-permute-start.10
  57.1 3.3 %collective-permute-start.12 = (bf16[96,768]{1,0:T(8,128)(2,1)S(1)}, bf16[96,768]{1,0:T(8,128)(2,1)S(1)}, u32[]{:S(2)}, u32[]{:S(2)}) collective-permute-start(bf16[96,768]{1,0:T(8,128)(2,1)S(1)} %get-tuple-element.23), channel_id=1, source_target_pairs={{0,32},{16,48},{32,0},{48,16},{1,33},{17,49},{33,1},{49,17},{2,34}... | collective-permute-start | bytes 442376 | tf_op jit(solution)/shard_map/ppermute | solution.py:22
  64.6 3.0 %collective-permute-done.12 = bf16[96,768]{1,0:T(8,128)(2,1)S(1)} collective-permute-done((bf16[96,768]{1,0:T(8,128)(2,1)S(1)}, bf16[96,768]{1,0:T(8,128)(2,1)S(1)}, u32[]{:S(2)}, u32[]{:S(2)}) %collective-permute-start.12) | collective-permute-done | bytes 147488 | tf_op jit(solution)/shard_map/ppermute | solution.py:22
  71.3 2.6 %collective-permute-done.38 = bf16[96,768]{1,0:T(8,128)(2,1)S(1)} collective-permute-done((bf16[96,768]{1,0:T(8,128)(2,1)S(1)}, bf16[96,768]{1,0:T(8,128)(2,1)S(1)}, u32[]{:S(2)}, u32[]{:S(2)}) %collective-permute-start.38) | collective-permute-done | bytes 147488 | tf_op jit(solution)/shard_map/ppermute | solution.py:22
  78.7 2.5 %collective-permute-start.24 = (bf16[240,768]{1,0:T(8,128)(2,1)S(1)}, bf16[240,768]{1,0:T(8,128)(2,1)S(1)}, u32[]{:S(2)}, u32[]{:S(2)}) collective-permute-start(bf16[240,768]{1,0:T(8,128)(2,1)S(1)} %get-tuple-element.17), channel_id=1, source_target_pairs={{0,32},{16,48},{32,0},{48,16},{1,33},{17,49},{33,1},{49,17},{2,34}... | collective-permute-start | bytes 1105928 | tf_op jit(solution)/shard_map/ppermute | solution.py:22
  82.7 5.4 %collective-permute-done.22 = bf16[240,768]{1,0:T(8,128)(2,1)S(1)} collective-permute-done((bf16[240,768]{1,0:T(8,128)(2,1)S(1)}, bf16[240,768]{1,0:T(8,128)(2,1)S(1)}, u32[]{:S(2)}, u32[]{:S(2)}) %collective-permute-start.22) | collective-permute-done | bytes 368672 | tf_op jit(solution)/shard_map/ppermute | solution.py:22
  88.1 2.6 %collective-permute-start.40 = (bf16[48,768]{1,0:T(8,128)(2,1)S(1)}, bf16[48,768]{1,0:T(8,128)(2,1)S(1)}, u32[]{:S(2)}, u32[]{:S(2)}) collective-permute-start(bf16[48,768]{1,0:T(8,128)(2,1)S(1)} %get-tuple-element.32), channel_id=1, source_target_pairs={{0,2},{2,0},{1,3},{3,1},{4,6},{6,4},{5,7},{7,5},{8,10},{10,8},{9,1... | collective-permute-start | bytes 221192 | tf_op jit(solution)/shard_map/ppermute | solution.py:26
  90.7 6.2 %collective-permute-done.24 = bf16[240,768]{1,0:T(8,128)(2,1)S(1)} collective-permute-done((bf16[240,768]{1,0:T(8,128)(2,1)S(1)}, bf16[240,768]{1,0:T(8,128)(2,1)S(1)}, u32[]{:S(2)}, u32[]{:S(2)}) %collective-permute-start.24) | collective-permute-done | bytes 368672 | tf_op jit(solution)/shard_map/ppermute | solution.py:22
  101.1 2.8 %collective-permute-start.6 = (bf16[768,768]{1,0:T(8,128)(2,1)S(1)}, bf16[768,768]{1,0:T(8,128)(2,1)S(1)}, u32[]{:S(2)}, u32[]{:S(2)}) collective-permute-start(bf16[768,768]{1,0:T(8,128)(2,1)S(1)} %copy-done.2), channel_id=1, source_target_pairs={{0,12},{4,0},{8,4},{12,8},{1,13},{5,1},{9,5},{13,9},{2,14},{6,2},{... | collective-permute-start | bytes 3538952 | tf_op jit(solution)/shard_map/ppermute | solution.py:22
  103.9 3.0 %collective-permute-done.25 = bf16[240,768]{1,0:T(8,128)(2,1)S(1)} collective-permute-done((bf16[240,768]{1,0:T(8,128)(2,1)S(1)}, bf16[240,768]{1,0:T(8,128)(2,1)S(1)}, u32[]{:S(2)}, u32[]{:S(2)}) %collective-permute-start.25) | collective-permute-done | bytes 368672 | tf_op jit(solution)/shard_map/ppermute | solution.py:26
  108.6 3.9 %collective-permute-start.14 = (bf16[2,48,768]{2,1,0:T(8,128)(2,1)S(1)}, bf16[2,48,768]{2,1,0:T(8,128)(2,1)S(1)}, u32[]{:S(2)}, u32[]{:S(2)}) collective-permute-start(bf16[2,48,768]{2,1,0:T(8,128)(2,1)S(1)} %bitcast.53), channel_id=1, source_target_pairs={{0,48},{16,0},{32,16},{48,32},{1,49},{17,1},{33,17},{49,33},{2,50}... | collective-permute-start | bytes 442376 | tf_op jit(solution)/shard_map/ppermute | solution.py:22
  112.5 25.7 %collective-permute-done.26 = bf16[192,768]{1,0:T(8,128)(2,1)S(1)} collective-permute-done((bf16[192,768]{1,0:T(8,128)(2,1)S(1)}, bf16[192,768]{1,0:T(8,128)(2,1)S(1)}, u32[]{:S(2)}, u32[]{:S(2)}) %collective-permute-start.26) | collective-permute-done | bytes 294944 | tf_op jit(solution)/shard_map/ppermute | solution.py:22
  138.3 2.9 %collective-permute-start.27 = (bf16[144,768]{1,0:T(8,128)(2,1)S(1)}, bf16[144,768]{1,0:T(8,128)(2,1)S(1)}, u32[]{:S(2)}, u32[]{:S(2)}) collective-permute-start(bf16[144,768]{1,0:T(8,128)(2,1)S(1)} %slice.174), channel_id=1, source_target_pairs={{0,2},{2,0},{1,3},{3,1},{4,6},{6,4},{5,7},{7,5},{8,10},{10,8},{9,1... | collective-permute-start | bytes 663560 | tf_op jit(solution)/shard_map/ppermute | solution.py:26
  143.2 2.0 collective-permute-done.27
  145.2 2.4 %collective-permute-start.18 = (bf16[2,48,768]{2,1,0:T(8,128)(2,1)S(1)}, bf16[2,48,768]{2,1,0:T(8,128)(2,1)S(1)}, u32[]{:S(2)}, u32[]{:S(2)}) collective-permute-start(bf16[2,48,768]{2,1,0:T(8,128)(2,1)S(1)} %collective-permute-done.14.refs_11_), channel_id=1, source_target_pairs={{0,1},{1,0},{2,3},{3,2},{4,5},{5,4},{6,7},{7,6},{8,9},{9,8},{10,11... | collective-permute-start | bytes 442376 | tf_op jit(solution)/shard_map/ppermute | solution.py:26
  148.6 3.0 %collective-permute-start.43 = (bf16[4,48,768]{2,1,0:T(8,128)(2,1)S(1)}, bf16[4,48,768]{2,1,0:T(8,128)(2,1)S(1)}, u32[]{:S(2)}, u32[]{:S(2)}) collective-permute-start(bf16[4,48,768]{2,1,0:T(8,128)(2,1)S(1)} %bitcast.47), channel_id=1, source_target_pairs={{0,32},{16,48},{32,0},{48,16},{1,33},{17,49},{33,1},{49,17},{2,34}... | collective-permute-start | bytes 884744 | tf_op jit(solution)/shard_map/ppermute | solution.py:22
  153.1 4.2 %collective-permute-done.44.refs_29_ = bf16[4,48,768]{2,1,0:T(8,128)(2,1)S(1)} collective-permute-done((bf16[4,48,768]{2,1,0:T(8,128)(2,1)S(1)}, bf16[4,48,768]{2,1,0:T(8,128)(2,1)S(1)}, u32[]{:S(2)}, u32[]{:S(2)}) %collective-permute-start.44) | collective-permute-done | bytes 294944 | tf_op jit(solution)/shard_map/ppermute | solution.py:22
  158.7 5.4 %collective-permute-start.30 = (bf16[10,48,768]{2,1,0:T(8,128)(2,1)S(1)}, bf16[10,48,768]{2,1,0:T(8,128)(2,1)S(1)}, u32[]{:S(2)}, u32[]{:S(2)}) collective-permute-start(bf16[10,48,768]{2,1,0:T(8,128)(2,1)S(1)} %bitcast.55), channel_id=1, source_target_pairs={{0,16},{16,32},{32,48},{48,0},{1,17},{17,33},{33,49},{49,1},{2,18}... | collective-permute-start | bytes 2211848 | tf_op jit(solution)/shard_map/ppermute | solution.py:22
  164.1 2.6 %collective-permute-start.29 = (bf16[10,48,768]{2,1,0:T(8,128)(2,1)S(1)}, bf16[10,48,768]{2,1,0:T(8,128)(2,1)S(1)}, u32[]{:S(2)}, u32[]{:S(2)}) collective-permute-start(bf16[10,48,768]{2,1,0:T(8,128)(2,1)S(1)} %bitcast.56), channel_id=1, source_target_pairs={{0,32},{16,48},{32,0},{48,16},{1,33},{17,49},{33,1},{49,17},{2,34}... | collective-permute-start | bytes 2211848 | tf_op jit(solution)/shard_map/ppermute | solution.py:22
  172.8 8.1 %collective-permute-done.30.refs_21_ = bf16[10,48,768]{2,1,0:T(8,128)(2,1)S(1)} collective-permute-done((bf16[10,48,768]{2,1,0:T(8,128)(2,1)S(1)}, bf16[10,48,768]{2,1,0:T(8,128)(2,1)S(1)}, u32[]{:S(2)}, u32[]{:S(2)}) %collective-permute-start.30) | collective-permute-done | bytes 737312 | tf_op jit(solution)/shard_map/ppermute | solution.py:22
  181.3 17.9 %collective-permute-done.29.refs_20_ = bf16[10,48,768]{2,1,0:T(8,128)(2,1)S(1)} collective-permute-done((bf16[10,48,768]{2,1,0:T(8,128)(2,1)S(1)}, bf16[10,48,768]{2,1,0:T(8,128)(2,1)S(1)}, u32[]{:S(2)}, u32[]{:S(2)}) %collective-permute-start.29) | collective-permute-done | bytes 737312 | tf_op jit(solution)/shard_map/ppermute | solution.py:22
  200.0 15.6 %collective-permute-done.8.refs_9_ = bf16[384,768]{1,0:T(8,128)(2,1)S(1)} collective-permute-done((bf16[384,768]{1,0:T(8,128)(2,1)S(1)}, bf16[384,768]{1,0:T(8,128)(2,1)S(1)}, u32[]{:S(2)}, u32[]{:S(2)}) %collective-permute-start.8) | collective-permute-done | bytes 589856 | tf_op jit(solution)/shard_map/ppermute | solution.py:22
  215.6 15.1 %shard_map.45 = (bf16[768,768]{1,0:T(8,128)(2,1)}, bf16[384,768]{1,0:T(8,128)(2,1)}) custom-call(bf16[768,768]{1,0:T(8,128)(2,1)S(1)} %shard_map.41.own.refs_0_, bf16[768,768]{1,0:T(8,128)(2,1)S(1)} %copy-done.9, bf16[768,768]{1,0:T(8,128)(2,1)} %copy-done.11, bf16[768,768]{1,0:T(8,128)(2,1)} %copy-done.13, bf16[768,768]{1,0:T(8,128)(2,1)} %copy-done.12, ...), custom_call_target="tpu_custom_call" | custom-call | flops 7247757312 | bytes 21233664 | tf_op jit(solution)/shard_map/pallas_call | solution.py:228
  (123 shorter events, 44.2 us)
Async XLA Ops:
  4.5 28.6 %collective-permute-start.1 = (bf16[768,768]{1,0:T(8,128)(2,1)S(1)}, bf16[768,768]{1,0:T(8,128)(2,1)S(1)}, u32[]{:S(2)}, u32[]{:S(2)}) collective-permute-start(bf16[768,768]{1,0:T(8,128)(2,1)S(1)} %shard_map.41.own.refs_0_), channel_id=1, source_target_pairs={{0,4},{4,8},{8,12},{12,0},{1,5},{5,9},{9,13},{13,1},{2,6},{6,10},{... | collective-permute-start | bytes 3538952 | tf_op jit(solution)/shard_map/ppermute | solution.py:22
  6.7 27.0 %collective-permute-start = (bf16[768,768]{1,0:T(8,128)(2,1)S(1)}, bf16[768,768]{1,0:T(8,128)(2,1)S(1)}, u32[]{:S(2)}, u32[]{:S(2)}) collective-permute-start(bf16[768,768]{1,0:T(8,128)(2,1)S(1)} %shard_map.41.own.refs_0_), channel_id=1, source_target_pairs={{0,12},{4,0},{8,4},{12,8},{1,13},{5,1},{9,5},{13,9},{2,14},{6,2},{... | collective-permute-start | bytes 3538952 | tf_op jit(solution)/shard_map/ppermute | solution.py:22
  8.0 33.2 %collective-permute-start.2 = (bf16[768,768]{1,0:T(8,128)(2,1)S(1)}, bf16[768,768]{1,0:T(8,128)(2,1)S(1)}, u32[]{:S(2)}, u32[]{:S(2)}) collective-permute-start(bf16[768,768]{1,0:T(8,128)(2,1)S(1)} %shard_map.41.own.refs_0_), channel_id=1, source_target_pairs={{0,2},{2,0},{1,3},{3,1},{4,6},{6,4},{5,7},{7,5},{8,10},{10,8},{9,1... | collective-permute-start | bytes 3538952 | tf_op jit(solution)/shard_map/ppermute | solution.py:26
  33.2 14.4 %collective-permute-start.4 = (bf16[384,768]{1,0:T(8,128)(2,1)S(1)}, bf16[384,768]{1,0:T(8,128)(2,1)S(1)}, u32[]{:S(2)}, u32[]{:S(2)}) collective-permute-start(bf16[384,768]{1,0:T(8,128)(2,1)S(1)} %slice.161), channel_id=1, source_target_pairs={{0,4},{4,8},{8,12},{12,0},{1,5},{5,9},{9,13},{13,1},{2,6},{6,10},{... | collective-permute-start | bytes 1769480 | tf_op jit(solution)/shard_map/ppermute | solution.py:22
  34.2 13.4 %collective-permute-start.3 = (bf16[384,768]{1,0:T(8,128)(2,1)S(1)}, bf16[384,768]{1,0:T(8,128)(2,1)S(1)}, u32[]{:S(2)}, u32[]{:S(2)}) collective-permute-start(bf16[384,768]{1,0:T(8,128)(2,1)S(1)} %slice.160), channel_id=1, source_target_pairs={{0,12},{4,0},{8,4},{12,8},{1,13},{5,1},{9,5},{13,9},{2,14},{6,2},{... | collective-permute-start | bytes 1769480 | tf_op jit(solution)/shard_map/ppermute | solution.py:22
  38.9 14.8 %collective-permute-start.9 = (bf16[4,96,768]{2,1,0:T(8,128)(2,1)}, bf16[4,96,768]{2,1,0:T(8,128)(2,1)}, u32[]{:S(2)}, u32[]{:S(2)}) collective-permute-start(bf16[4,96,768]{2,1,0:T(8,128)(2,1)} %get-tuple-element.11), channel_id=1, source_target_pairs={{0,1},{1,0},{2,3},{3,2},{4,5},{5,4},{6,7},{7,6},{8,9},{9,8},{10,11... | collective-permute-start | bytes 1769480 | tf_op jit(solution)/shard_map/ppermute | solution.py:26
  45.3 31.0 %collective-permute-start.21 = (bf16[4,240,768]{2,1,0:T(8,128)(2,1)}, bf16[4,240,768]{2,1,0:T(8,128)(2,1)}, u32[]{:S(2)}, u32[]{:S(2)}) collective-permute-start(bf16[4,240,768]{2,1,0:T(8,128)(2,1)} %get-tuple-element.13), channel_id=1, source_target_pairs={{0,1},{1,0},{2,3},{3,2},{4,5},{5,4},{6,7},{7,6},{8,9},{9,8},{10,11... | collective-permute-start | bytes 4423688 | tf_op jit(solution)/shard_map/ppermute | solution.py:26
  57.1 10.5 %collective-permute-start.12 = (bf16[96,768]{1,0:T(8,128)(2,1)S(1)}, bf16[96,768]{1,0:T(8,128)(2,1)S(1)}, u32[]{:S(2)}, u32[]{:S(2)}) collective-permute-start(bf16[96,768]{1,0:T(8,128)(2,1)S(1)} %get-tuple-element.23), channel_id=1, source_target_pairs={{0,32},{16,48},{32,0},{48,16},{1,33},{17,49},{33,1},{49,17},{2,34}... | collective-permute-start | bytes 442376 | tf_op jit(solution)/shard_map/ppermute | solution.py:22
  63.5 10.5 %collective-permute-start.38 = (bf16[96,768]{1,0:T(8,128)(2,1)S(1)}, bf16[96,768]{1,0:T(8,128)(2,1)S(1)}, u32[]{:S(2)}, u32[]{:S(2)}) collective-permute-start(bf16[96,768]{1,0:T(8,128)(2,1)S(1)} %get-tuple-element.20), channel_id=1, source_target_pairs={{0,32},{16,48},{32,0},{48,16},{1,33},{17,49},{33,1},{49,17},{2,34}... | collective-permute-start | bytes 442376 | tf_op jit(solution)/shard_map/ppermute | solution.py:22
  68.7 29.9 %collective-permute-start.13 = (bf16[96,768]{1,0:T(8,128)(2,1)S(1)}, bf16[96,768]{1,0:T(8,128)(2,1)S(1)}, u32[]{:S(2)}, u32[]{:S(2)}) collective-permute-start(bf16[96,768]{1,0:T(8,128)(2,1)S(1)} %fusion.11), channel_id=1, source_target_pairs={{0,64},{64,0},{1,65},{65,1},{2,66},{66,2},{3,67},{67,3},{4,68},{68... | collective-permute-start | bytes 442376 | tf_op jit(solution)/shard_map/ppermute | solution.py:26
  78.7 18.3 %collective-permute-start.24 = (bf16[240,768]{1,0:T(8,128)(2,1)S(1)}, bf16[240,768]{1,0:T(8,128)(2,1)S(1)}, u32[]{:S(2)}, u32[]{:S(2)}) collective-permute-start(bf16[240,768]{1,0:T(8,128)(2,1)S(1)} %get-tuple-element.17), channel_id=1, source_target_pairs={{0,32},{16,48},{32,0},{48,16},{1,33},{17,49},{33,1},{49,17},{2,34}... | collective-permute-start | bytes 1105928 | tf_op jit(solution)/shard_map/ppermute | solution.py:22
  81.2 15.9 %collective-permute-start.23 = (bf16[240,768]{1,0:T(8,128)(2,1)S(1)}, bf16[240,768]{1,0:T(8,128)(2,1)S(1)}, u32[]{:S(2)}, u32[]{:S(2)}) collective-permute-start(bf16[240,768]{1,0:T(8,128)(2,1)S(1)} %get-tuple-element.18), channel_id=1, source_target_pairs={{0,48},{16,0},{32,16},{48,32},{1,49},{17,1},{33,17},{49,33},{2,50}... | collective-permute-start | bytes 1105928 | tf_op jit(solution)/shard_map/ppermute | solution.py:22
  81.3 22.6 %collective-permute-start.41 = (bf16[96,768]{1,0:T(8,128)(2,1)S(1)}, bf16[96,768]{1,0:T(8,128)(2,1)S(1)}, u32[]{:S(2)}, u32[]{:S(2)}) collective-permute-start(bf16[96,768]{1,0:T(8,128)(2,1)S(1)} %multiply_convert_fusion.1), channel_id=1, source_target_pairs={{0,8},{4,12},{8,0},{12,4},{1,9},{5,13},{9,1},{13,5},{2,10},{6,14},... | collective-permute-start | bytes 442376 | tf_op jit(solution)/shard_map/ppermute | solution.py:22
  88.1 13.0 %collective-permute-start.40 = (bf16[48,768]{1,0:T(8,128)(2,1)S(1)}, bf16[48,768]{1,0:T(8,128)(2,1)S(1)}, u32[]{:S(2)}, u32[]{:S(2)}) collective-permute-start(bf16[48,768]{1,0:T(8,128)(2,1)S(1)} %get-tuple-element.32), channel_id=1, source_target_pairs={{0,2},{2,0},{1,3},{3,1},{4,6},{6,4},{5,7},{7,5},{8,10},{10,8},{9,1... | collective-permute-start | bytes 221192 | tf_op jit(solution)/shard_map/ppermute | solution.py:26
  101.1 50.6 %collective-permute-start.6 = (bf16[768,768]{1,0:T(8,128)(2,1)S(1)}, bf16[768,768]{1,0:T(8,128)(2,1)S(1)}, u32[]{:S(2)}, u32[]{:S(2)}) collective-permute-start(bf16[768,768]{1,0:T(8,128)(2,1)S(1)} %copy-done.2), channel_id=1, source_target_pairs={{0,12},{4,0},{8,4},{12,8},{1,13},{5,1},{9,5},{13,9},{2,14},{6,2},{... | collective-permute-start | bytes 3538952 | tf_op jit(solution)/shard_map/ppermute | solution.py:22
  103.9 54.8 %collective-permute-start.5 = (bf16[768,768]{1,0:T(8,128)(2,1)S(1)}, bf16[768,768]{1,0:T(8,128)(2,1)S(1)}, u32[]{:S(2)}, u32[]{:S(2)}) collective-permute-start(bf16[768,768]{1,0:T(8,128)(2,1)S(1)} %copy-done.2), channel_id=1, source_target_pairs={{0,4},{4,8},{8,12},{12,0},{1,5},{5,9},{9,13},{13,1},{2,6},{6,10},{... | collective-permute-start | bytes 3538952 | tf_op jit(solution)/shard_map/ppermute | solution.py:22
  107.0 31.2 %collective-permute-start.26 = (bf16[192,768]{1,0:T(8,128)(2,1)S(1)}, bf16[192,768]{1,0:T(8,128)(2,1)S(1)}, u32[]{:S(2)}, u32[]{:S(2)}) collective-permute-start(bf16[192,768]{1,0:T(8,128)(2,1)S(1)} %slice.173), channel_id=1, source_target_pairs={{0,4},{4,8},{8,12},{12,0},{1,5},{5,9},{9,13},{13,1},{2,6},{6,10},{... | collective-permute-start | bytes 884744 | tf_op jit(solution)/shard_map/ppermute | solution.py:22
  107.3 33.9 %collective-permute-start.15 = (bf16[2,48,768]{2,1,0:T(8,128)(2,1)S(1)}, bf16[2,48,768]{2,1,0:T(8,128)(2,1)S(1)}, u32[]{:S(2)}, u32[]{:S(2)}) collective-permute-start(bf16[2,48,768]{2,1,0:T(8,128)(2,1)S(1)} %bitcast.52), channel_id=1, source_target_pairs={{0,32},{16,48},{32,0},{48,16},{1,33},{17,49},{33,1},{49,17},{2,34}... | collective-permute-start | bytes 442376 | tf_op jit(solution)/shard_map/ppermute | solution.py:22
  108.6 34.5 %collective-permute-start.14 = (bf16[2,48,768]{2,1,0:T(8,128)(2,1)S(1)}, bf16[2,48,768]{2,1,0:T(8,128)(2,1)S(1)}, u32[]{:S(2)}, u32[]{:S(2)}) collective-permute-start(bf16[2,48,768]{2,1,0:T(8,128)(2,1)S(1)} %bitcast.53), channel_id=1, source_target_pairs={{0,48},{16,0},{32,16},{48,32},{1,49},{17,1},{33,17},{49,33},{2,50}... | collective-permute-start | bytes 442376 | tf_op jit(solution)/shard_map/ppermute | solution.py:22
  147.7 16.4 %collective-permute-start.45 = (bf16[4,48,768]{2,1,0:T(8,128)(2,1)S(1)}, bf16[4,48,768]{2,1,0:T(8,128)(2,1)S(1)}, u32[]{:S(2)}, u32[]{:S(2)}) collective-permute-start(bf16[4,48,768]{2,1,0:T(8,128)(2,1)S(1)} %bitcast.45), channel_id=1, source_target_pairs={{0,1},{1,0},{2,3},{3,2},{4,5},{5,4},{6,7},{7,6},{8,9},{9,8},{10,11... | collective-permute-start | bytes 884744 | tf_op jit(solution)/shard_map/ppermute | solution.py:26
  148.6 18.1 %collective-permute-start.43 = (bf16[4,48,768]{2,1,0:T(8,128)(2,1)S(1)}, bf16[4,48,768]{2,1,0:T(8,128)(2,1)S(1)}, u32[]{:S(2)}, u32[]{:S(2)}) collective-permute-start(bf16[4,48,768]{2,1,0:T(8,128)(2,1)S(1)} %bitcast.47), channel_id=1, source_target_pairs={{0,32},{16,48},{32,0},{48,16},{1,33},{17,49},{33,1},{49,17},{2,34}... | collective-permute-start | bytes 884744 | tf_op jit(solution)/shard_map/ppermute | solution.py:22
  151.7 17.0 %collective-permute-start.42 = (bf16[4,48,768]{2,1,0:T(8,128)(2,1)S(1)}, bf16[4,48,768]{2,1,0:T(8,128)(2,1)S(1)}, u32[]{:S(2)}, u32[]{:S(2)}) collective-permute-start(bf16[4,48,768]{2,1,0:T(8,128)(2,1)S(1)} %bitcast.48), channel_id=1, source_target_pairs={{0,48},{16,0},{32,16},{48,32},{1,49},{17,1},{33,17},{49,33},{2,50}... | collective-permute-start | bytes 884744 | tf_op jit(solution)/shard_map/ppermute | solution.py:22
  157.2 12.4 %collective-permute-start.48 = (bf16[4,48,768]{2,1,0:T(8,128)(2,1)S(1)}, bf16[4,48,768]{2,1,0:T(8,128)(2,1)S(1)}, u32[]{:S(2)}, u32[]{:S(2)}) collective-permute-start(bf16[4,48,768]{2,1,0:T(8,128)(2,1)S(1)} %collective-permute-done.44.refs_29_), channel_id=1, source_target_pairs={{0,1},{1,0},{2,3},{3,2},{4,5},{5,4},{6,7},{7,6},{8,9},{9,8},{10,11... | collective-permute-start | bytes 884744 | tf_op jit(solution)/shard_map/ppermute | solution.py:26
  158.7 22.1 %collective-permute-start.30 = (bf16[10,48,768]{2,1,0:T(8,128)(2,1)S(1)}, bf16[10,48,768]{2,1,0:T(8,128)(2,1)S(1)}, u32[]{:S(2)}, u32[]{:S(2)}) collective-permute-start(bf16[10,48,768]{2,1,0:T(8,128)(2,1)S(1)} %bitcast.55), channel_id=1, source_target_pairs={{0,16},{16,32},{32,48},{48,0},{1,17},{17,33},{33,49},{49,1},{2,18}... | collective-permute-start | bytes 2211848 | tf_op jit(solution)/shard_map/ppermute | solution.py:22
  164.1 35.1 %collective-permute-start.29 = (bf16[10,48,768]{2,1,0:T(8,128)(2,1)S(1)}, bf16[10,48,768]{2,1,0:T(8,128)(2,1)S(1)}, u32[]{:S(2)}, u32[]{:S(2)}) collective-permute-start(bf16[10,48,768]{2,1,0:T(8,128)(2,1)S(1)} %bitcast.56), channel_id=1, source_target_pairs={{0,32},{16,48},{32,0},{48,16},{1,33},{17,49},{33,1},{49,17},{2,34}... | collective-permute-start | bytes 2211848 | tf_op jit(solution)/shard_map/ppermute | solution.py:22
  166.7 33.1 %collective-permute-start.28 = (bf16[10,48,768]{2,1,0:T(8,128)(2,1)S(1)}, bf16[10,48,768]{2,1,0:T(8,128)(2,1)S(1)}, u32[]{:S(2)}, u32[]{:S(2)}) collective-permute-start(bf16[10,48,768]{2,1,0:T(8,128)(2,1)S(1)} %bitcast.57), channel_id=1, source_target_pairs={{0,48},{16,0},{32,16},{48,32},{1,49},{17,1},{33,17},{49,33},{2,50}... | collective-permute-start | bytes 2211848 | tf_op jit(solution)/shard_map/ppermute | solution.py:22
  169.6 30.2 %collective-permute-start.7 = (bf16[384,768]{1,0:T(8,128)(2,1)S(1)}, bf16[384,768]{1,0:T(8,128)(2,1)S(1)}, u32[]{:S(2)}, u32[]{:S(2)}) collective-permute-start(bf16[384,768]{1,0:T(8,128)(2,1)S(1)} %slice.162), channel_id=1, source_target_pairs={{0,12},{4,0},{8,4},{12,8},{1,13},{5,1},{9,5},{13,9},{2,14},{6,2},{... | collective-permute-start | bytes 1769480 | tf_op jit(solution)/shard_map/ppermute | solution.py:22
  172.4 43.2 %collective-permute-start.31 = (bf16[10,48,768]{2,1,0:T(8,128)(2,1)S(1)}, bf16[10,48,768]{2,1,0:T(8,128)(2,1)S(1)}, u32[]{:S(2)}, u32[]{:S(2)}) collective-permute-start(bf16[10,48,768]{2,1,0:T(8,128)(2,1)S(1)} %bitcast.58), channel_id=1, source_target_pairs={{0,1},{1,0},{2,3},{3,2},{4,5},{5,4},{6,7},{7,6},{8,9},{9,8},{10,11... | collective-permute-start | bytes 2211848 | tf_op jit(solution)/shard_map/ppermute | solution.py:26
  180.8 34.7 %collective-permute-start.34 = (bf16[10,48,768]{2,1,0:T(8,128)(2,1)S(1)}, bf16[10,48,768]{2,1,0:T(8,128)(2,1)S(1)}, u32[]{:S(2)}, u32[]{:S(2)}) collective-permute-start(bf16[10,48,768]{2,1,0:T(8,128)(2,1)S(1)} %collective-permute-done.30.refs_21_), channel_id=1, source_target_pairs={{0,1},{1,0},{2,3},{3,2},{4,5},{5,4},{6,7},{7,6},{8,9},{9,8},{10,11... | collective-permute-start | bytes 2211848 | tf_op jit(solution)/shard_map/ppermute | solution.py:26
  199.2 16.4 %collective-permute-start.33 = (bf16[10,48,768]{2,1,0:T(8,128)(2,1)S(1)}, bf16[10,48,768]{2,1,0:T(8,128)(2,1)S(1)}, u32[]{:S(2)}, u32[]{:S(2)}) collective-permute-start(bf16[10,48,768]{2,1,0:T(8,128)(2,1)S(1)} %collective-permute-done.29.refs_20_), channel_id=1, source_target_pairs={{0,1},{1,0},{2,3},{3,2},{4,5},{5,4},{6,7},{7,6},{8,9},{9,8},{10,11... | collective-permute-start | bytes 2211848 | tf_op jit(solution)/shard_map/ppermute | solution.py:26
  199.8 15.7 %collective-permute-start.32 = (bf16[10,48,768]{2,1,0:T(8,128)(2,1)S(1)}, bf16[10,48,768]{2,1,0:T(8,128)(2,1)S(1)}, u32[]{:S(2)}, u32[]{:S(2)}) collective-permute-start(bf16[10,48,768]{2,1,0:T(8,128)(2,1)S(1)} %collective-permute-done.28.refs_19_), channel_id=1, source_target_pairs={{0,1},{1,0},{2,3},{3,2},{4,5},{5,4},{6,7},{7,6},{8,9},{9,8},{10,11... | collective-permute-start | bytes 2211848 | tf_op jit(solution)/shard_map/ppermute | solution.py:26
  199.9 15.7 %collective-permute-start.8 = (bf16[384,768]{1,0:T(8,128)(2,1)S(1)}, bf16[384,768]{1,0:T(8,128)(2,1)S(1)}, u32[]{:S(2)}, u32[]{:S(2)}) collective-permute-start(bf16[384,768]{1,0:T(8,128)(2,1)S(1)} %slice.163), channel_id=1, source_target_pairs={{0,4},{4,8},{8,12},{12,0},{1,5},{5,9},{9,13},{13,1},{2,6},{6,10},{... | collective-permute-start | bytes 1769480 | tf_op jit(solution)/shard_map/ppermute | solution.py:22
  (31 other events, 422.6 us)

commit v2 on v0

v2 whole, which is shorter than its diff:
```python
import functools

import jax
import jax.numpy as jnp
from jax import lax
from jax.experimental import pallas as pl
from jax.experimental.pallas import tpu as pltpu
from jax.sharding import Mesh, PartitionSpec as P

N = 12288
BLOCK = 64
AXES = ("yl", "z", "x", "yh", "core")
F32, BF16 = jnp.float32, jnp.bfloat16
T = 768
H = T // 2
S = 48
VMEM = pl.BlockSpec(memory_space=pltpu.VMEM)


def ring(axis, step):
    return lambda a: lax.ppermute(a, axis, [(i, (i + step) % 4) for i in range(4)])


def swap(axis):
    return lambda a: lax.ppermute(a, axis, [(0, 1), (1, 0)])


def tdot(a, b):
    return lax.dot_general(a, b, (((0,), (0,)), ((), ())), preferred_element_type=F32)


def dot(a, b):
    return jnp.dot(a, b, preferred_element_type=F32)


def dot_t(a, b):
    return lax.dot_general(a, b, (((1,), (1,)), ((), ())), preferred_element_type=F32)


def params(mib):
    return pltpu.CompilerParams(vmem_limit_bytes=mib << 20)


def cost(flops, size):
    return pl.CostEstimate(flops=flops, bytes_accessed=size, transcendentals=0)


def dequant_kernel(codes, scales, out):
    factor = scales[...].T
    lane = lax.broadcasted_iota(jnp.int32, (T, 128), 1)
    for g in range(T // 128):
        both = jnp.where(lane < BLOCK, factor[:, 2 * g : 2 * g + 1], factor[:, 2 * g + 1 : 2 * g + 2])
        levels = codes[:, 128 * g : 128 * (g + 1)].astype(F32) - 7.5
        out[:, 128 * g : 128 * (g + 1)] = (levels * both).astype(BF16)


def dequant(codes, scales):
    return pl.pallas_call(
        dequant_kernel,
        out_shape=jax.ShapeDtypeStruct((T, T), BF16),
        in_specs=[VMEM, VMEM],
        out_specs=VMEM,
        compiler_params=params(12),
        cost_estimate=cost(2 * T * T, 6 * T * T),
    )(codes, scales)


def cut(full, first, count, keep, send):
    z, k = lax.axis_index("z"), lax.axis_index("core")
    for half in range(count):
        for j in range(4):
            at = half * H + lax.rem(z + j, 4) * S
            to = pl.ds((first + half) * S, S)
            keep[j, to, :] = full[pl.ds(pl.multiple_of(at + k * (4 * S), 16), S), :].astype(BF16)
            send[j, to, :] = full[pl.ds(pl.multiple_of(at + (1 - k) * (4 * S), 16), S), :].astype(BF16)


def gram_kernel0(own, keep, send, full):
    full[...] = tdot(own[...], own[...])
    cut(full, 0, 2, keep, send)


def gram_kernel1(own, near1, far, _, keep, send, full):
    turned = near1[...].T
    full[...] = dot(turned, own[...])
    cut(full, 0, 2, keep, send)
    full[...] = dot(turned, far[...])
    cut(full, 2, 2, keep, send)
    h = lax.axis_index("yh")

    @pl.when(h == 0)
    def _():
        full[0:H, :] = tdot(far[:, 0:H], own[...])

    @pl.when(h != 0)
    def _():
        full[0:H, :] = tdot(own[:, H:T], far[...])

    cut(full, 4, 1, keep, send)


def gram_kernel2(own, far, near2a, near2b, _, keep, send, full):
    low = lax.axis_index("x") < 2
    for i, other in enumerate((own, far)):

        @pl.when(low)
        def _():
            full[0:H, :] = tdot(near2a[:, 0:H], other[0:H, :]) + tdot(near2b[:, 0:H], other[H:T, :])

        @pl.when(jnp.logical_not(low))
        def _():
            full[0:H, :] = tdot(other[0:H, H:T], near2a[...]) + tdot(other[H:T, H:T], near2b[...])

        cut(full, i, 1, keep, send)


def gram(kernel, halves, tiles, later=()):
    out = jax.ShapeDtypeStruct((4, halves * S, T), BF16)
    return pl.pallas_call(
        kernel,
        out_shape=(out, out),
        in_specs=[VMEM] * (len(tiles) + len(later)),
        out_specs=(VMEM, VMEM),
        scratch_shapes=[pltpu.VMEM((T, T), F32)],
        compiler_params=params(14),
        cost_estimate=cost(halves * T * T * T, 6 * T * T),
    )(*tiles, *later)


def halves_kernel(near1, near3, _, top, bottom):
    top[...] = near1[0:H, :]
    bottom[...] = near3[H:T, :]


def halves(near1, near3, later):
    out = jax.ShapeDtypeStruct((H, T), BF16)
    return pl.pallas_call(
        halves_kernel,
        out_shape=(out, out),
        in_specs=[VMEM, VMEM, VMEM],
        out_specs=(VMEM, VMEM),
        compiler_params=params(8),
        cost_estimate=cost(0, 4 * T * T),
    )(near1, near3, later)


def gate_kernel(*refs):
    pass


def gate(value, *later):
    return pl.pallas_call(
        gate_kernel,
        out_shape=jax.ShapeDtypeStruct(value.shape, value.dtype),
        in_specs=[VMEM] * (1 + len(later)),
        out_specs=VMEM,
        input_output_aliases={0: 0},
        compiler_params=params(8),
        cost_estimate=cost(0, 0),
    )(value, *later)


def line_kernel1(shard, from_x, from_y, _, __, out):
    out[0 : 2 * S] = shard[0 : 2 * S]
    out[2 * S : 6 * S] = from_x[...]
    out[6 * S : 8 * S] = from_y[0 : 2 * S]
    h = lax.axis_index("yh")
    out[pl.ds(pl.multiple_of((8 + h) * S, S), S)] = shard[4 * S : 5 * S]
    out[pl.ds(pl.multiple_of((9 - h) * S, S), S)] = from_y[2 * S : 3 * S]


def line_kernel2(shard, from_x, from_y, _, __, ___, ____, out):
    out[0 : 2 * S] = shard[0 : 2 * S]
    high = (lax.axis_index("x") >= 2).astype(jnp.int32)
    for at, mine, theirs in (
        (2, shard[2 * S : 3 * S], from_x[0:S]),
        (4, from_y[...], from_x[S : 2 * S]),
    ):
        out[pl.ds(pl.multiple_of((at + high) * S, S), S)] = mine
        out[pl.ds(pl.multiple_of((at + 1 - high) * S, S), S)] = theirs


def line_up(kernel, count, parts, later=()):
    return pl.pallas_call(
        kernel,
        out_shape=jax.ShapeDtypeStruct((count * S, T), BF16),
        in_specs=[VMEM] * (len(parts) + len(later)),
        out_specs=VMEM,
        compiler_params=params(8),
        cost_estimate=cost(0, 4 * count * S * T),
    )(*parts, *later).reshape(count, S, T)


def product_kernel(plan, final, *refs):
    count = len(plan)
    x, h, z, k = (lax.axis_index(axis) for axis in ("x", "yh", "z", "core"))
    refs = list(refs)
    tiles = [[refs.pop(0) for _ in source] for _, source, _ in plan]
    slices = [refs.pop(0) for _ in range(10)]
    before = [refs.pop(0) for _ in range(2 if final else 0)]
    out, gram_out, g, g_sem = refs[:4]
    acc = refs[4] if final else out

    g_copies = []
    ranges = ((0, 0, 2 * count), (1, 0, 2 * count), (3, 0, 2 * count), (2, 0, count), (2, count, count))
    for c in range(2):
        for i, (j, first, size) in enumerate(ranges):
            core = k if c == 0 else 1 - k
            at = pl.multiple_of(core * (4 * S) + lax.rem(z + j, 4) * S, 16)
            n = c * 5 + i
            g_copies.append(pltpu.make_async_copy(slices[n], g.at[pl.ds(first, size), pl.ds(at, S)], g_sem.at[n]))
    for copy in g_copies:
        copy.start()
    for copy in g_copies:
        copy.wait()

    def tile(t):
        return g[2 * t : 2 * t + 2].reshape(T, T)

    def is_turned(turn):
        return {"no": z < 0, "yes": z >= 0, "h": h != 0, "x": x >= 2}[turn]

    for t, (_, _, turn) in enumerate(plan):
        turned = is_turned(turn)

        def add(multiply):
            at = 0
            for part in tiles[t]:
                rows = slice(at, at + part.shape[0])
                value = multiply(part[...], tile(t))
                if t > 0:
                    acc[rows, :] += value
                elif final:
                    acc[rows, :] = before[0][rows, :] + value
                else:
                    acc[rows, :] = value
                at += part.shape[0]

        if turn != "yes":

            @pl.when(jnp.logical_not(turned))
            def _():
                add(dot)

        if turn != "no":

            @pl.when(turned)
            def _():
                add(dot_t)

    if final:
        out[...] = (1.5 * tiles[0][0][...].astype(F32) - 0.5 * acc[...]).astype(BF16)
        gram_out[...] = before[1][...]
    line = lax.axis_index("yl") * 4 + z
    dx, dh = lax.rem(line // 2 - x + 4, 4), lax.rem(line + h, 2)
    for t, ((ax, ah), _, turn) in enumerate(plan):
        mine, turned = (dx == ax) & (dh == ah), is_turned(turn)
        if turn != "yes":

            @pl.when(mine & jnp.logical_not(turned))
            def _():
                gram_out[...] = g[2 * t + k]

        if turn != "no":
            for side in range(2):

                @pl.when(mine & turned & (k == side))
                def _():
                    gram_out[...] = g[2 * t : 2 * t + 2, :, side * H : (side + 1) * H].reshape(T, H).T


def product(plan, slices, before=()):
    final, count = bool(before), len(plan)
    tiles = [part for _, source, _ in plan for part in source]
    shape = tuple((d, tuple(range(len(source))), turn) for d, source, turn in plan)
    return pl.pallas_call(
        functools.partial(product_kernel, shape, final),
        out_shape=(jax.ShapeDtypeStruct((T, T), BF16 if final else F32), jax.ShapeDtypeStruct((H, T), BF16)),
        in_specs=[VMEM] * (len(tiles) + len(slices) + len(before)),
        out_specs=(VMEM, VMEM),
        scratch_shapes=[pltpu.VMEM((2 * count, H, T), BF16), pltpu.SemaphoreType.DMA((10,))]
        + [pltpu.VMEM((T, T), F32)] * final,
        compiler_params=params(24),
        cost_estimate=cost(2 * count * T * T * T, 4 * count * T * T),
    )(*tiles, *slices, *before)


def sum_core(keep, send):
    other = swap("core")(send)
    return [keep[j].astype(F32) + other[j].astype(F32) for j in range(4)]


def sum_z(sums):
    total = sums[0]
    for j in (1, 3, 2):
        total = total + ring("z", j)(sums[j].astype(BF16)).astype(F32)
    return total.astype(BF16)


def sum_yl(total):
    total = total.astype(F32) + swap("yl")(total).astype(F32)
    return (total * (1.0 / N)).astype(BF16)


def spread(shard):
    n = shard.shape[0] // 2
    one, three = ring("z", -1)(shard), ring("z", 1)(shard)
    mine = [shard, one, three, ring("z", -1)(one[:n]), ring("z", 1)(three[n:])]
    return mine + [swap("core")(a) for a in mine]


def body(quant_codes, block_scales):
    own = dequant(quant_codes, block_scales)

    near1 = ring("x", -1)(own)
    near3 = ring("x", 1)(own)
    far = swap("yh")(own)
    total0 = sum_z(sum_core(*gram(gram_kernel0, 2, [own])))
    top, bottom = halves(near1, near3, total0)
    near2 = (ring("x", -1)(top), ring("x", 1)(bottom))

    total1 = sum_z(sum_core(*gram(gram_kernel1, 5, [own, near1, far], [top])))
    far = gate(far, *near2)
    far1 = ring("x", -1)(far)
    far3 = ring("x", 1)(far)
    sums2 = sum_core(*gram(gram_kernel2, 2, [own, far, *near2], [total1]))

    shard = sum_yl(total1)
    from_x = ring("x", 1)(shard[: 4 * S])
    from_y = swap("yh")(shard[2 * S :])
    line1 = line_up(line_kernel1, 10, [shard, from_x, from_y], [far1, far3])
    slices1 = spread(line1)
    top, bottom = halves(far1, far3, line1)
    far2 = (ring("x", -1)(top), ring("x", 1)(bottom))

    shard = sum_yl(jnp.concatenate([total0, sum_z(sums2)]))
    from_x = ring("x", 2)(shard[2 * S :])
    from_y = swap("yh")(shard[3 * S :])
    slices2 = spread(line_up(line_kernel2, 6, [shard, from_x, from_y], [*slices1[1:3], *far2]))

    plan1 = (
        ((1, 0), (near1,), "no"),
        ((3, 0), (near3,), "yes"),
        ((3, 1), (far3,), "yes"),
        ((1, 1), (far1,), "no"),
        ((0, 1), (far,), "h"),
    )
    plan2 = (((0, 0), (own,), "no"), ((2, 0), near2, "x"), ((2, 1), far2, "x"))
    return product(plan2, slices2, product(plan1, slices1))


def solution(mesh):
    split = Mesh(mesh.devices.reshape(2, 4, 4, 2, 2), AXES)
    line, side = ("yl", "z", "core"), ("x", "yh")
    return jax.shard_map(
        body,
        mesh=split,
        in_specs=(P(line, side), P(side, line)),
        out_specs=(P(line, side), P(line, side)),
        check_vma=False,
    )
```

time: 335 us -> 177 us (0.53)
  waiting for transfers between devices: 284 us -> 89.7 us
  starting transfers between devices: 0.12 us -> 63.2 us
  matrix products: 27.7 us -> 0 us
  Pallas kernels: 0 us -> 19.2 us
  between operations: 13.8 us -> 1.07 us
  other arithmetic: 5.88 us -> 1.2 us
    all_gather x2 -> x0, waiting for transfers between devices: 178 us -> none  [the longest x1 120 us: body(): row_panel = lax.all_gather(basis_tile, 'col', axis=1, tiled=True)]
    reduce_scatter x1 -> x0, waiting for transfers between devices: 106 us -> none  [body(): lax.psum_scatter(lax.dot_general(columns, basis_tile, (((0,), (0,)), ((),...]
    ppermute x0 -> x45, waiting for transfers between devices: none -> 89.7 us  [the longest x27 80.9 us: ring(): lax.ppermute(a, axis, [(i, (i + step) % 4) for i in range(4)])]
    ppermute x0 -> x45, starting transfers between devices: none -> 63.2 us  [the longest x27 32.8 us: ring(): lax.ppermute(a, axis, [(i, (i + step) % 4) for i in range(4)])]
    dot_general x2 -> x0, matrix products: 27.7 us -> none  [the longest x1 14.2 us: body(): lax.dot_general(columns, basis_tile, (((0,), (0,)), ((), ())), preferred_...]
    pallas_call x0 -> x11, Pallas kernels: none -> 19.2 us  [the longest x2 11.3 us: product(): pl.pallas_call(functools.partial(product_kernel, shape, final), out_shape...]
    convert_element_type x2 -> x8, other arithmetic: 5.88 us -> 1.18 us  [the longest x3 0.5 us: sum_z(): total = total + ring('z', j)(sums[j].astype(BF16)).astype(F32)]
  transfers between devices with their start and end apart: 3 -> 45, of which waited for: 3 -> 19; matrix products, arithmetic and copies ran while one was open for 0% -> 1% of each run, Pallas kernels for 0% -> 3%
where the time goes in v2:
time: 177 us
  waiting for transfers between devices  89.7 us (51%)
  starting transfers between devices  63.2 us (36%)
  Pallas kernels  19.2 us (11%)
  local copies, waits for them, and re-layouts  2.59 us (1%)
    ppermute x27, waiting for transfers between devices, ring(): lax.ppermute(a, axis, [(i, (i + step) % 4) for i in range(4)])  80.9 us
    ppermute x27, starting transfers between devices, ring(): lax.ppermute(a, axis, [(i, (i + step) % 4) for i in range(4)])  32.8 us
    ppermute x18, starting transfers between devices, swap(): return lambda a: lax.ppermute(a, axis, [(0, 1), (1, 0)])  30.4 us
    pallas_call x2, Pallas kernels, product(): pl.pallas_call(functools.partial(product_kernel, shape, final), out_shape...  11.3 us
    ppermute x18, waiting for transfers between devices, swap(): return lambda a: lax.ppermute(a, axis, [(0, 1), (1, 0)])  8.74 us
    pallas_call x3, Pallas kernels, gram(): pl.pallas_call(kernel, out_shape=(out, out), in_specs=[VMEM] * (len(tiles...  6.14 us
  transfers between devices with their start and end apart: 45, of which 19 were waited for; matrix products, arithmetic and copies ran while one was open for 1% of the time, Pallas kernels for 3%

profile of v2, /device:TPU:1, one launch (start us, length us, event | category | flops | bytes accessed | tf_op | source)
XLA Modules:
  0.0 176.9 jit_solution(12730081372370615695)
XLA Ops:
  10.0 3.0 %collective-permute-start.8 = (bf16[768,768]{1,0:T(8,128)(2,1)S(1)}, bf16[768,768]{1,0:T(8,128)(2,1)S(1)}, u32[]{:S(2)}, u32[]{:S(2)}) collective-permute-start(bf16[768,768]{1,0:T(8,128)(2,1)S(1)} %shard_map.41.own.refs_0_), channel_id=1, source_target_pairs={{0,2},{2,0},{1,3},{3,1},{4,6},{6,4},{5,7},{7,5},{8,10},{10,8},{9,1... | collective-permute-start | bytes 3538952 | tf_op jit(solution)/shard_map/ppermute | solution.py:25
  14.8 3.3 %collective-permute-start.5 = (bf16[96,768]{1,0:T(8,128)(2,1)S(1)}, bf16[96,768]{1,0:T(8,128)(2,1)S(1)}, u32[]{:S(2)}, u32[]{:S(2)}) collective-permute-start(bf16[96,768]{1,0:T(8,128)(2,1)S(1)} %get-tuple-element.33), channel_id=1, source_target_pairs={{0,32},{16,48},{32,0},{48,16},{1,33},{17,49},{33,1},{49,17},{2,34}... | collective-permute-start | bytes 442376 | tf_op jit(solution)/shard_map/ppermute | solution.py:21
  18.1 2.1 %collective-permute-done.3 = bf16[96,768]{1,0:T(8,128)(2,1)S(1)} collective-permute-done((bf16[96,768]{1,0:T(8,128)(2,1)S(1)}, bf16[96,768]{1,0:T(8,128)(2,1)S(1)}, u32[]{:S(2)}, u32[]{:S(2)}) %collective-permute-start.3) | collective-permute-done | bytes 147488 | tf_op jit(solution)/shard_map/ppermute | solution.py:21
  21.4 2.9 %collective-permute-done.5 = bf16[96,768]{1,0:T(8,128)(2,1)S(1)} collective-permute-done((bf16[96,768]{1,0:T(8,128)(2,1)S(1)}, bf16[96,768]{1,0:T(8,128)(2,1)S(1)}, u32[]{:S(2)}, u32[]{:S(2)}) %collective-permute-start.5) | collective-permute-done | bytes 147488 | tf_op jit(solution)/shard_map/ppermute | solution.py:21
  24.6 11.4 %collective-permute-done.1.near3.refs_1_ = bf16[768,768]{1,0:T(8,128)(2,1)S(1)} collective-permute-done((bf16[768,768]{1,0:T(8,128)(2,1)S(1)}, bf16[768,768]{1,0:T(8,128)(2,1)S(1)}, u32[]{:S(2)}, u32[]{:S(2)}) %collective-permute-start.1) | collective-permute-done | bytes 1179680 | tf_op jit(solution)/shard_map/ppermute | solution.py:21
  36.1 2.3 %collective-permute-done.8.refs_0_.far = bf16[768,768]{1,0:T(8,128)(2,1)S(1)} collective-permute-done((bf16[768,768]{1,0:T(8,128)(2,1)S(1)}, bf16[768,768]{1,0:T(8,128)(2,1)S(1)}, u32[]{:S(2)}, u32[]{:S(2)}) %collective-permute-start.8) | collective-permute-done | bytes 1179680 | tf_op jit(solution)/shard_map/ppermute | solution.py:25
  38.4 3.0 %shard_map.45 = (bf16[4,240,768]{2,1,0:T(8,128)(2,1)S(1)}, bf16[4,240,768]{2,1,0:T(8,128)(2,1)S(1)}) custom-call(bf16[768,768]{1,0:T(8,128)(2,1)S(1)} %shard_map.41.own.refs_0_, bf16[768,768]{1,0:T(8,128)(2,1)S(1)} %collective-permute-done.near1.refs_0_, bf16[768,768]{1,0:T(8,128)(2,1)S(1)} %collective-permute-done.8.refs_0_.far, ...), custom_call_target="tpu_custom_call" | custom-call | flops 2264924160 | bytes 3538944 | tf_op jit(solution)/shard_map/pallas_call | solution.py:119
  47.9 3.3 %collective-permute-start.14 = (bf16[240,768]{1,0:T(8,128)(2,1)S(1)}, bf16[240,768]{1,0:T(8,128)(2,1)S(1)}, u32[]{:S(2)}, u32[]{:S(2)}) collective-permute-start(bf16[240,768]{1,0:T(8,128)(2,1)S(1)} %get-tuple-element.27), channel_id=1, source_target_pairs={{0,32},{16,48},{32,0},{48,16},{1,33},{17,49},{33,1},{49,17},{2,34}... | collective-permute-start | bytes 1105928 | tf_op jit(solution)/shard_map/ppermute | solution.py:21
  51.9 8.1 %collective-permute-done.7.refs_2_.near2b = bf16[384,768]{1,0:T(8,128)(2,1)S(1)} collective-permute-done((bf16[384,768]{1,0:T(8,128)(2,1)S(1)}, bf16[384,768]{1,0:T(8,128)(2,1)S(1)}, u32[]{:S(2)}, u32[]{:S(2)}) %collective-permute-start.7) | collective-permute-done | bytes 589856 | tf_op jit(solution)/shard_map/ppermute | solution.py:21
  60.1 7.4 %collective-permute-done.14 = bf16[240,768]{1,0:T(8,128)(2,1)S(1)} collective-permute-done((bf16[240,768]{1,0:T(8,128)(2,1)S(1)}, bf16[240,768]{1,0:T(8,128)(2,1)S(1)}, u32[]{:S(2)}, u32[]{:S(2)}) %collective-permute-start.14) | collective-permute-done | bytes 368672 | tf_op jit(solution)/shard_map/ppermute | solution.py:21
  67.7 1.9 %shard_map.48 = (bf16[4,96,768]{2,1,0:T(8,128)(2,1)S(1)}, bf16[4,96,768]{2,1,0:T(8,128)(2,1)S(1)}) custom-call(bf16[768,768]{1,0:T(8,128)(2,1)S(1)} %shard_map.41.own.refs_0_, bf16[768,768]{1,0:T(8,128)(2,1)S(1)} %shard_map.44.far.refs_4_, bf16[384,768]{1,0:T(8,128)(2,1)S(1)} %collective-permute-done.6.refs_1_.near2a, ...), custom_call_target="tpu_custom_call" | custom-call | flops 905969664 | bytes 3538944 | tf_op jit(solution)/shard_map/pallas_call | solution.py:119
  72.2 2.7 %collective-permute-start.9 = (bf16[768,768]{1,0:T(8,128)(2,1)S(1)}, bf16[768,768]{1,0:T(8,128)(2,1)S(1)}, u32[]{:S(2)}, u32[]{:S(2)}) collective-permute-start(bf16[768,768]{1,0:T(8,128)(2,1)S(1)} %shard_map.44.far.refs_4_), channel_id=1, source_target_pairs={{0,12},{4,0},{8,4},{12,8},{1,13},{5,1},{9,5},{13,9},{2,14},{6,2},{... | collective-permute-start | bytes 3538952 | tf_op jit(solution)/shard_map/ppermute | solution.py:21
  76.1 2.1 %collective-permute-start.23 = (bf16[96,768]{1,0:T(8,128)(2,1)S(1)}, bf16[96,768]{1,0:T(8,128)(2,1)S(1)}, u32[]{:S(2)}, u32[]{:S(2)}) collective-permute-start(bf16[96,768]{1,0:T(8,128)(2,1)S(1)} %get-tuple-element.30), channel_id=1, source_target_pairs={{0,32},{16,48},{32,0},{48,16},{1,33},{17,49},{33,1},{49,17},{2,34}... | collective-permute-start | bytes 442376 | tf_op jit(solution)/shard_map/ppermute | solution.py:21
  78.2 2.9 %collective-permute-done.15 = bf16[240,768]{1,0:T(8,128)(2,1)S(1)} collective-permute-done((bf16[240,768]{1,0:T(8,128)(2,1)S(1)}, bf16[240,768]{1,0:T(8,128)(2,1)S(1)}, u32[]{:S(2)}, u32[]{:S(2)}) %collective-permute-start.15) | collective-permute-done | bytes 368672 | tf_op jit(solution)/shard_map/ppermute | solution.py:25
  81.1 1.9 %collective-permute-start.22 = (bf16[96,768]{1,0:T(8,128)(2,1)S(1)}, bf16[96,768]{1,0:T(8,128)(2,1)S(1)}, u32[]{:S(2)}, u32[]{:S(2)}) collective-permute-start(bf16[96,768]{1,0:T(8,128)(2,1)S(1)} %get-tuple-element.31), channel_id=1, source_target_pairs={{0,48},{16,0},{32,16},{48,32},{1,49},{17,1},{33,17},{49,33},{2,50}... | collective-permute-start | bytes 442376 | tf_op jit(solution)/shard_map/ppermute | solution.py:21
  87.1 2.7 %collective-permute-start.17 = (bf16[144,768]{1,0:T(8,128)(2,1)S(1)}, bf16[144,768]{1,0:T(8,128)(2,1)S(1)}, u32[]{:S(2)}, u32[]{:S(2)}) collective-permute-start(bf16[144,768]{1,0:T(8,128)(2,1)S(1)} %slice.137), channel_id=1, source_target_pairs={{0,2},{2,0},{1,3},{3,1},{4,6},{6,4},{5,7},{7,5},{8,10},{10,8},{9,1... | collective-permute-start | bytes 663560 | tf_op jit(solution)/shard_map/ppermute | solution.py:25
  89.8 10.8 %collective-permute-done.10.__.near3.refs_2_ = bf16[768,768]{1,0:T(8,128)(2,1)S(1)} collective-permute-done((bf16[768,768]{1,0:T(8,128)(2,1)S(1)}, bf16[768,768]{1,0:T(8,128)(2,1)S(1)}, u32[]{:S(2)}, u32[]{:S(2)}) %collective-permute-start.10) | collective-permute-done | bytes 1179680 | tf_op jit(solution)/shard_map/ppermute | solution.py:21
  100.6 6.3 %collective-permute-done.16.from_x = bf16[192,768]{1,0:T(8,128)(2,1)S(1)} collective-permute-done((bf16[192,768]{1,0:T(8,128)(2,1)S(1)}, bf16[192,768]{1,0:T(8,128)(2,1)S(1)}, u32[]{:S(2)}, u32[]{:S(2)}) %collective-permute-start.16) | collective-permute-done | bytes 294944 | tf_op jit(solution)/shard_map/ppermute | solution.py:21
  111.5 2.7 %collective-permute-start.26 = (bf16[48,768]{1,0:T(8,128)(2,1)S(1)}, bf16[48,768]{1,0:T(8,128)(2,1)S(1)}, u32[]{:S(2)}, u32[]{:S(2)}) collective-permute-start(bf16[48,768]{1,0:T(8,128)(2,1)S(1)} %slice.143), channel_id=1, source_target_pairs={{0,2},{2,0},{1,3},{3,1},{4,6},{6,4},{5,7},{7,5},{8,10},{10,8},{9,1... | collective-permute-start | bytes 221192 | tf_op jit(solution)/shard_map/ppermute | solution.py:25
  114.2 2.1 %collective-permute-done.26.from_y = bf16[48,768]{1,0:T(8,128)(2,1)S(1)} collective-permute-done((bf16[48,768]{1,0:T(8,128)(2,1)S(1)}, bf16[48,768]{1,0:T(8,128)(2,1)S(1)}, u32[]{:S(2)}, u32[]{:S(2)}) %collective-permute-start.26) | collective-permute-done | bytes 73760 | tf_op jit(solution)/shard_map/ppermute | solution.py:25
  116.6 9.3 %collective-permute-done.25.from_x = bf16[96,768]{1,0:T(8,128)(2,1)S(1)} collective-permute-done((bf16[96,768]{1,0:T(8,128)(2,1)S(1)}, bf16[96,768]{1,0:T(8,128)(2,1)S(1)}, u32[]{:S(2)}, u32[]{:S(2)}) %collective-permute-start.25) | collective-permute-done | bytes 147488 | tf_op jit(solution)/shard_map/ppermute | solution.py:21
  125.9 3.4 %collective-permute-start.40 = (bf16[10,48,768]{2,1,0:T(8,128)(2,1)S(1)}, bf16[10,48,768]{2,1,0:T(8,128)(2,1)S(1)}, u32[]{:S(2)}, u32[]{:S(2)}) collective-permute-start(bf16[10,48,768]{2,1,0:T(8,128)(2,1)S(1)} %bitcast.47), channel_id=1, source_target_pairs={{0,1},{1,0},{2,3},{3,2},{4,5},{5,4},{6,7},{7,6},{8,9},{9,8},{10,11... | collective-permute-start | bytes 2211848 | tf_op jit(solution)/shard_map/ppermute | solution.py:25
  129.9 2.3 %collective-permute-start.29 = (bf16[6,48,768]{2,1,0:T(8,128)(2,1)S(1)}, bf16[6,48,768]{2,1,0:T(8,128)(2,1)S(1)}, u32[]{:S(2)}, u32[]{:S(2)}) collective-permute-start(bf16[6,48,768]{2,1,0:T(8,128)(2,1)S(1)} %bitcast.50), channel_id=1, source_target_pairs={{0,48},{16,0},{32,16},{48,32},{1,49},{17,1},{33,17},{49,33},{2,50}... | collective-permute-start | bytes 1327112 | tf_op jit(solution)/shard_map/ppermute | solution.py:21
  133.7 2.0 %collective-permute-start.42 = (bf16[10,48,768]{2,1,0:T(8,128)(2,1)S(1)}, bf16[10,48,768]{2,1,0:T(8,128)(2,1)S(1)}, u32[]{:S(2)}, u32[]{:S(2)}) collective-permute-start(bf16[10,48,768]{2,1,0:T(8,128)(2,1)S(1)} %collective-permute-done.28.__.refs_7_), channel_id=1, source_target_pairs={{0,1},{1,0},{2,3},{3,2},{4,5},{5,4},{6,7},{7,6},{8,9},{9,8},{10,11... | collective-permute-start | bytes 2211848 | tf_op jit(solution)/shard_map/ppermute | solution.py:25
  135.7 5.8 %collective-permute-done.30.refs_7_ = bf16[6,48,768]{2,1,0:T(8,128)(2,1)S(1)} collective-permute-done((bf16[6,48,768]{2,1,0:T(8,128)(2,1)S(1)}, bf16[6,48,768]{2,1,0:T(8,128)(2,1)S(1)}, u32[]{:S(2)}, u32[]{:S(2)}) %collective-permute-start.30) | collective-permute-done | bytes 442400 | tf_op jit(solution)/shard_map/ppermute | solution.py:21
  141.4 3.1 %collective-permute-start.41 = (bf16[10,48,768]{2,1,0:T(8,128)(2,1)S(1)}, bf16[10,48,768]{2,1,0:T(8,128)(2,1)S(1)}, u32[]{:S(2)}, u32[]{:S(2)}) collective-permute-start(bf16[10,48,768]{2,1,0:T(8,128)(2,1)S(1)} %collective-permute-done.27._.refs_6_), channel_id=1, source_target_pairs={{0,1},{1,0},{2,3},{3,2},{4,5},{5,4},{6,7},{7,6},{8,9},{9,8},{10,11... | collective-permute-start | bytes 2211848 | tf_op jit(solution)/shard_map/ppermute | solution.py:25
  144.5 4.8 %collective-permute-done.39.refs_9_ = bf16[5,48,768]{2,1,0:T(8,128)(2,1)S(1)} collective-permute-done((bf16[5,48,768]{2,1,0:T(8,128)(2,1)S(1)}, bf16[5,48,768]{2,1,0:T(8,128)(2,1)S(1)}, u32[]{:S(2)}, u32[]{:S(2)}) %collective-permute-start.39) | collective-permute-done | bytes 368672 | tf_op jit(solution)/shard_map/ppermute | solution.py:21
  151.2 4.5 %collective-permute-done.32.refs_9_ = bf16[3,48,768]{2,1,0:T(8,128)(2,1)S(1)} collective-permute-done((bf16[3,48,768]{2,1,0:T(8,128)(2,1)S(1)}, bf16[3,48,768]{2,1,0:T(8,128)(2,1)S(1)}, u32[]{:S(2)}, u32[]{:S(2)}) %collective-permute-start.32) | collective-permute-done | bytes 221216 | tf_op jit(solution)/shard_map/ppermute | solution.py:21
  155.7 4.8 %collective-permute-done.31.refs_8_ = bf16[3,48,768]{2,1,0:T(8,128)(2,1)S(1)} collective-permute-done((bf16[3,48,768]{2,1,0:T(8,128)(2,1)S(1)}, bf16[3,48,768]{2,1,0:T(8,128)(2,1)S(1)}, u32[]{:S(2)}, u32[]{:S(2)}) %collective-permute-start.31) | collective-permute-done | bytes 221216 | tf_op jit(solution)/shard_map/ppermute | solution.py:21
  160.5 3.8 %collective-permute-start.33 = (bf16[6,48,768]{2,1,0:T(8,128)(2,1)S(1)}, bf16[6,48,768]{2,1,0:T(8,128)(2,1)S(1)}, u32[]{:S(2)}, u32[]{:S(2)}) collective-permute-start(bf16[6,48,768]{2,1,0:T(8,128)(2,1)S(1)} %bitcast.51), channel_id=1, source_target_pairs={{0,1},{1,0},{2,3},{3,2},{4,5},{5,4},{6,7},{7,6},{8,9},{9,8},{10,11... | collective-permute-start | bytes 1327112 | tf_op jit(solution)/shard_map/ppermute | solution.py:25
  165.4 5.6 %shard_map.50 = (f32[768,768]{1,0:T(8,128)S(1)}, bf16[384,768]{1,0:T(8,128)(2,1)S(1)}) custom-call(bf16[768,768]{1,0:T(8,128)(2,1)S(1)} %collective-permute-done.near1.refs_0_, bf16[768,768]{1,0:T(8,128)(2,1)S(1)} %collective-permute-done.1.near3.refs_1_, bf16[768,768]{1,0:T(8,128)(2,1)S(1)} %collective-permute-done.10.__.near3.refs_2_, ...), custom_call_target="tpu_custom_call" | custom-call | flops 4529848320 | bytes 11796480 | tf_op jit(solution)/shard_map/pallas_call | solution.py:276
  171.0 5.8 %shard_map.51 = (bf16[768,768]{1,0:T(8,128)(2,1)}, bf16[384,768]{1,0:T(8,128)(2,1)}) custom-call(bf16[768,768]{1,0:T(8,128)(2,1)S(1)} %shard_map.41.own.refs_0_, bf16[384,768]{1,0:T(8,128)(2,1)S(1)} %collective-permute-done.6.refs_1_.near2a, bf16[384,768]{1,0:T(8,128)(2,1)S(1)} %collective-permute-done.7.refs_2_.near2b, ...), custom_call_target="tpu_custom_call" | custom-call | flops 2717908992 | bytes 7077888 | tf_op jit(solution)/shard_map/pallas_call | solution.py:276
  (90 shorter events, 37.9 us)
Async XLA Ops:
  7.3 28.7 %collective-permute-start.1 = (bf16[768,768]{1,0:T(8,128)(2,1)S(1)}, bf16[768,768]{1,0:T(8,128)(2,1)S(1)}, u32[]{:S(2)}, u32[]{:S(2)}) collective-permute-start(bf16[768,768]{1,0:T(8,128)(2,1)S(1)} %shard_map.41.own.refs_0_), channel_id=1, source_target_pairs={{0,4},{4,8},{8,12},{12,0},{1,5},{5,9},{9,13},{13,1},{2,6},{6,10},{... | collective-permute-start | bytes 3538952 | tf_op jit(solution)/shard_map/ppermute | solution.py:21
  8.6 27.4 %collective-permute-start = (bf16[768,768]{1,0:T(8,128)(2,1)S(1)}, bf16[768,768]{1,0:T(8,128)(2,1)S(1)}, u32[]{:S(2)}, u32[]{:S(2)}) collective-permute-start(bf16[768,768]{1,0:T(8,128)(2,1)S(1)} %shard_map.41.own.refs_0_), channel_id=1, source_target_pairs={{0,12},{4,0},{8,4},{12,8},{1,13},{5,1},{9,5},{13,9},{2,14},{6,2},{... | collective-permute-start | bytes 3538952 | tf_op jit(solution)/shard_map/ppermute | solution.py:21
  10.0 28.5 %collective-permute-start.8 = (bf16[768,768]{1,0:T(8,128)(2,1)S(1)}, bf16[768,768]{1,0:T(8,128)(2,1)S(1)}, u32[]{:S(2)}, u32[]{:S(2)}) collective-permute-start(bf16[768,768]{1,0:T(8,128)(2,1)S(1)} %shard_map.41.own.refs_0_), channel_id=1, source_target_pairs={{0,2},{2,0},{1,3},{3,1},{4,6},{6,4},{5,7},{7,5},{8,10},{10,8},{9,1... | collective-permute-start | bytes 3538952 | tf_op jit(solution)/shard_map/ppermute | solution.py:25
  14.8 9.4 %collective-permute-start.5 = (bf16[96,768]{1,0:T(8,128)(2,1)S(1)}, bf16[96,768]{1,0:T(8,128)(2,1)S(1)}, u32[]{:S(2)}, u32[]{:S(2)}) collective-permute-start(bf16[96,768]{1,0:T(8,128)(2,1)S(1)} %get-tuple-element.33), channel_id=1, source_target_pairs={{0,32},{16,48},{32,0},{48,16},{1,33},{17,49},{33,1},{49,17},{2,34}... | collective-permute-start | bytes 442376 | tf_op jit(solution)/shard_map/ppermute | solution.py:21
  43.0 17.1 %collective-permute-start.6 = (bf16[384,768]{1,0:T(8,128)(2,1)S(1)}, bf16[384,768]{1,0:T(8,128)(2,1)S(1)}, u32[]{:S(2)}, u32[]{:S(2)}) collective-permute-start(bf16[384,768]{1,0:T(8,128)(2,1)S(1)} %get-tuple-element.16._), channel_id=1, source_target_pairs={{0,12},{4,0},{8,4},{12,8},{1,13},{5,1},{9,5},{13,9},{2,14},{6,2},{... | collective-permute-start | bytes 1769480 | tf_op jit(solution)/shard_map/ppermute | solution.py:21
  44.3 15.8 %collective-permute-start.7 = (bf16[384,768]{1,0:T(8,128)(2,1)S(1)}, bf16[384,768]{1,0:T(8,128)(2,1)S(1)}, u32[]{:S(2)}, u32[]{:S(2)}) collective-permute-start(bf16[384,768]{1,0:T(8,128)(2,1)S(1)} %get-tuple-element.17), channel_id=1, source_target_pairs={{0,4},{4,8},{8,12},{12,0},{1,5},{5,9},{9,13},{13,1},{2,6},{6,10},{... | collective-permute-start | bytes 1769480 | tf_op jit(solution)/shard_map/ppermute | solution.py:21
  46.1 13.9 %collective-permute-start.12 = (bf16[240,768]{1,0:T(8,128)(2,1)S(1)}, bf16[240,768]{1,0:T(8,128)(2,1)S(1)}, u32[]{:S(2)}, u32[]{:S(2)}) collective-permute-start(bf16[240,768]{1,0:T(8,128)(2,1)S(1)} %get-tuple-element.26), channel_id=1, source_target_pairs={{0,16},{16,32},{32,48},{48,0},{1,17},{17,33},{33,49},{49,1},{2,18}... | collective-permute-start | bytes 1105928 | tf_op jit(solution)/shard_map/ppermute | solution.py:21
  47.9 19.5 %collective-permute-start.14 = (bf16[240,768]{1,0:T(8,128)(2,1)S(1)}, bf16[240,768]{1,0:T(8,128)(2,1)S(1)}, u32[]{:S(2)}, u32[]{:S(2)}) collective-permute-start(bf16[240,768]{1,0:T(8,128)(2,1)S(1)} %get-tuple-element.27), channel_id=1, source_target_pairs={{0,32},{16,48},{32,0},{48,16},{1,33},{17,49},{33,1},{49,17},{2,34}... | collective-permute-start | bytes 1105928 | tf_op jit(solution)/shard_map/ppermute | solution.py:21
  51.2 16.2 %collective-permute-start.13 = (bf16[240,768]{1,0:T(8,128)(2,1)S(1)}, bf16[240,768]{1,0:T(8,128)(2,1)S(1)}, u32[]{:S(2)}, u32[]{:S(2)}) collective-permute-start(bf16[240,768]{1,0:T(8,128)(2,1)S(1)} %get-tuple-element.28), channel_id=1, source_target_pairs={{0,48},{16,0},{32,16},{48,32},{1,49},{17,1},{33,17},{49,33},{2,50}... | collective-permute-start | bytes 1105928 | tf_op jit(solution)/shard_map/ppermute | solution.py:21
  70.9 10.1 %collective-permute-start.15 = (bf16[240,768]{1,0:T(8,128)(2,1)S(1)}, bf16[240,768]{1,0:T(8,128)(2,1)S(1)}, u32[]{:S(2)}, u32[]{:S(2)}) collective-permute-start(bf16[240,768]{1,0:T(8,128)(2,1)S(1)} %fusion.2._), channel_id=1, source_target_pairs={{0,64},{64,0},{1,65},{65,1},{2,66},{66,2},{3,67},{67,3},{4,68},{68... | collective-permute-start | bytes 1105928 | tf_op jit(solution)/shard_map/ppermute | solution.py:25
  72.2 28.4 %collective-permute-start.10 = (bf16[768,768]{1,0:T(8,128)(2,1)S(1)}, bf16[768,768]{1,0:T(8,128)(2,1)S(1)}, u32[]{:S(2)}, u32[]{:S(2)}) collective-permute-start(bf16[768,768]{1,0:T(8,128)(2,1)S(1)} %shard_map.44.far.refs_4_), channel_id=1, source_target_pairs={{0,4},{4,8},{8,12},{12,0},{1,5},{5,9},{9,13},{13,1},{2,6},{6,10},{... | collective-permute-start | bytes 3538952 | tf_op jit(solution)/shard_map/ppermute | solution.py:21
  72.2 28.4 %collective-permute-start.9 = (bf16[768,768]{1,0:T(8,128)(2,1)S(1)}, bf16[768,768]{1,0:T(8,128)(2,1)S(1)}, u32[]{:S(2)}, u32[]{:S(2)}) collective-permute-start(bf16[768,768]{1,0:T(8,128)(2,1)S(1)} %shard_map.44.far.refs_4_), channel_id=1, source_target_pairs={{0,12},{4,0},{8,4},{12,8},{1,13},{5,1},{9,5},{13,9},{2,14},{6,2},{... | collective-permute-start | bytes 3538952 | tf_op jit(solution)/shard_map/ppermute | solution.py:21
  75.0 8.1 %collective-permute-start.21 = (bf16[96,768]{1,0:T(8,128)(2,1)S(1)}, bf16[96,768]{1,0:T(8,128)(2,1)S(1)}, u32[]{:S(2)}, u32[]{:S(2)}) collective-permute-start(bf16[96,768]{1,0:T(8,128)(2,1)S(1)} %get-tuple-element.29), channel_id=1, source_target_pairs={{0,16},{16,32},{32,48},{48,0},{1,17},{17,33},{33,49},{49,1},{2,18}... | collective-permute-start | bytes 442376 | tf_op jit(solution)/shard_map/ppermute | solution.py:21
  76.1 8.2 %collective-permute-start.23 = (bf16[96,768]{1,0:T(8,128)(2,1)S(1)}, bf16[96,768]{1,0:T(8,128)(2,1)S(1)}, u32[]{:S(2)}, u32[]{:S(2)}) collective-permute-start(bf16[96,768]{1,0:T(8,128)(2,1)S(1)} %get-tuple-element.30), channel_id=1, source_target_pairs={{0,32},{16,48},{32,0},{48,16},{1,33},{17,49},{33,1},{49,17},{2,34}... | collective-permute-start | bytes 442376 | tf_op jit(solution)/shard_map/ppermute | solution.py:21
  83.1 23.8 %collective-permute-start.16 = (bf16[192,768]{1,0:T(8,128)(2,1)S(1)}, bf16[192,768]{1,0:T(8,128)(2,1)S(1)}, u32[]{:S(2)}, u32[]{:S(2)}) collective-permute-start(bf16[192,768]{1,0:T(8,128)(2,1)S(1)} %slice.136), channel_id=1, source_target_pairs={{0,4},{4,8},{8,12},{12,0},{1,5},{5,9},{9,13},{13,1},{2,6},{6,10},{... | collective-permute-start | bytes 884744 | tf_op jit(solution)/shard_map/ppermute | solution.py:21
  85.7 25.7 %collective-permute-start.24 = (bf16[192,768]{1,0:T(8,128)(2,1)S(1)}, bf16[192,768]{1,0:T(8,128)(2,1)S(1)}, u32[]{:S(2)}, u32[]{:S(2)}) collective-permute-start(bf16[192,768]{1,0:T(8,128)(2,1)S(1)} %pad_maximum_fusion), channel_id=1, source_target_pairs={{0,64},{64,0},{1,65},{65,1},{2,66},{66,2},{3,67},{67,3},{4,68},{68... | collective-permute-start | bytes 884744 | tf_op jit(solution)/shard_map/ppermute | solution.py:25
  87.1 13.5 %collective-permute-start.17 = (bf16[144,768]{1,0:T(8,128)(2,1)S(1)}, bf16[144,768]{1,0:T(8,128)(2,1)S(1)}, u32[]{:S(2)}, u32[]{:S(2)}) collective-permute-start(bf16[144,768]{1,0:T(8,128)(2,1)S(1)} %slice.137), channel_id=1, source_target_pairs={{0,2},{2,0},{1,3},{3,1},{4,6},{6,4},{5,7},{7,5},{8,10},{10,8},{9,1... | collective-permute-start | bytes 663560 | tf_op jit(solution)/shard_map/ppermute | solution.py:25
  107.0 22.2 %collective-permute-start.28 = (bf16[10,48,768]{2,1,0:T(8,128)(2,1)S(1)}, bf16[10,48,768]{2,1,0:T(8,128)(2,1)S(1)}, u32[]{:S(2)}, u32[]{:S(2)}) collective-permute-start(bf16[10,48,768]{2,1,0:T(8,128)(2,1)S(1)} %bitcast.44), channel_id=1, source_target_pairs={{0,16},{16,32},{32,48},{48,0},{1,17},{17,33},{33,49},{49,1},{2,18}... | collective-permute-start | bytes 2211848 | tf_op jit(solution)/shard_map/ppermute | solution.py:21
  108.0 21.2 %collective-permute-start.27 = (bf16[10,48,768]{2,1,0:T(8,128)(2,1)S(1)}, bf16[10,48,768]{2,1,0:T(8,128)(2,1)S(1)}, u32[]{:S(2)}, u32[]{:S(2)}) collective-permute-start(bf16[10,48,768]{2,1,0:T(8,128)(2,1)S(1)} %bitcast.45), channel_id=1, source_target_pairs={{0,48},{16,0},{32,16},{48,32},{1,49},{17,1},{33,17},{49,33},{2,50}... | collective-permute-start | bytes 2211848 | tf_op jit(solution)/shard_map/ppermute | solution.py:21
  109.8 19.4 %collective-permute-start.18 = (bf16[384,768]{1,0:T(8,128)(2,1)S(1)}, bf16[384,768]{1,0:T(8,128)(2,1)S(1)}, u32[]{:S(2)}, u32[]{:S(2)}) collective-permute-start(bf16[384,768]{1,0:T(8,128)(2,1)S(1)} %get-tuple-element.20), channel_id=1, source_target_pairs={{0,12},{4,0},{8,4},{12,8},{1,13},{5,1},{9,5},{13,9},{2,14},{6,2},{... | collective-permute-start | bytes 1769480 | tf_op jit(solution)/shard_map/ppermute | solution.py:21
  110.0 19.3 %collective-permute-start.19 = (bf16[384,768]{1,0:T(8,128)(2,1)S(1)}, bf16[384,768]{1,0:T(8,128)(2,1)S(1)}, u32[]{:S(2)}, u32[]{:S(2)}) collective-permute-start(bf16[384,768]{1,0:T(8,128)(2,1)S(1)} %get-tuple-element.21), channel_id=1, source_target_pairs={{0,4},{4,8},{8,12},{12,0},{1,5},{5,9},{9,13},{13,1},{2,6},{6,10},{... | collective-permute-start | bytes 1769480 | tf_op jit(solution)/shard_map/ppermute | solution.py:21
  116.3 9.6 %collective-permute-start.25 = (bf16[96,768]{1,0:T(8,128)(2,1)S(1)}, bf16[96,768]{1,0:T(8,128)(2,1)S(1)}, u32[]{:S(2)}, u32[]{:S(2)}) collective-permute-start(bf16[96,768]{1,0:T(8,128)(2,1)S(1)} %slice.142), channel_id=1, source_target_pairs={{0,8},{4,12},{8,0},{12,4},{1,9},{5,13},{9,1},{13,5},{2,10},{6,14},... | collective-permute-start | bytes 442376 | tf_op jit(solution)/shard_map/ppermute | solution.py:21
  125.9 7.8 %collective-permute-start.40 = (bf16[10,48,768]{2,1,0:T(8,128)(2,1)S(1)}, bf16[10,48,768]{2,1,0:T(8,128)(2,1)S(1)}, u32[]{:S(2)}, u32[]{:S(2)}) collective-permute-start(bf16[10,48,768]{2,1,0:T(8,128)(2,1)S(1)} %bitcast.47), channel_id=1, source_target_pairs={{0,1},{1,0},{2,3},{3,2},{4,5},{5,4},{6,7},{7,6},{8,9},{9,8},{10,11... | collective-permute-start | bytes 2211848 | tf_op jit(solution)/shard_map/ppermute | solution.py:25
  129.3 12.1 %collective-permute-start.30 = (bf16[6,48,768]{2,1,0:T(8,128)(2,1)S(1)}, bf16[6,48,768]{2,1,0:T(8,128)(2,1)S(1)}, u32[]{:S(2)}, u32[]{:S(2)}) collective-permute-start(bf16[6,48,768]{2,1,0:T(8,128)(2,1)S(1)} %bitcast.49), channel_id=1, source_target_pairs={{0,16},{16,32},{32,48},{48,0},{1,17},{17,33},{33,49},{49,1},{2,18}... | collective-permute-start | bytes 1327112 | tf_op jit(solution)/shard_map/ppermute | solution.py:21
  129.4 19.9 %collective-permute-start.39 = (bf16[5,48,768]{2,1,0:T(8,128)(2,1)S(1)}, bf16[5,48,768]{2,1,0:T(8,128)(2,1)S(1)}, u32[]{:S(2)}, u32[]{:S(2)}) collective-permute-start(bf16[5,48,768]{2,1,0:T(8,128)(2,1)S(1)} %slice.147), channel_id=1, source_target_pairs={{0,16},{16,32},{32,48},{48,0},{1,17},{17,33},{33,49},{49,1},{2,18}... | collective-permute-start | bytes 1105928 | tf_op jit(solution)/shard_map/ppermute | solution.py:21
  129.9 21.2 %collective-permute-start.29 = (bf16[6,48,768]{2,1,0:T(8,128)(2,1)S(1)}, bf16[6,48,768]{2,1,0:T(8,128)(2,1)S(1)}, u32[]{:S(2)}, u32[]{:S(2)}) collective-permute-start(bf16[6,48,768]{2,1,0:T(8,128)(2,1)S(1)} %bitcast.50), channel_id=1, source_target_pairs={{0,48},{16,0},{32,16},{48,32},{1,49},{17,1},{33,17},{49,33},{2,50}... | collective-permute-start | bytes 1327112 | tf_op jit(solution)/shard_map/ppermute | solution.py:21
  132.3 17.1 %collective-permute-start.38 = (bf16[5,48,768]{2,1,0:T(8,128)(2,1)S(1)}, bf16[5,48,768]{2,1,0:T(8,128)(2,1)S(1)}, u32[]{:S(2)}, u32[]{:S(2)}) collective-permute-start(bf16[5,48,768]{2,1,0:T(8,128)(2,1)S(1)} %slice.146), channel_id=1, source_target_pairs={{0,48},{16,0},{32,16},{48,32},{1,49},{17,1},{33,17},{49,33},{2,50}... | collective-permute-start | bytes 1105928 | tf_op jit(solution)/shard_map/ppermute | solution.py:21
  133.7 30.6 %collective-permute-start.42 = (bf16[10,48,768]{2,1,0:T(8,128)(2,1)S(1)}, bf16[10,48,768]{2,1,0:T(8,128)(2,1)S(1)}, u32[]{:S(2)}, u32[]{:S(2)}) collective-permute-start(bf16[10,48,768]{2,1,0:T(8,128)(2,1)S(1)} %collective-permute-done.28.__.refs_7_), channel_id=1, source_target_pairs={{0,1},{1,0},{2,3},{3,2},{4,5},{5,4},{6,7},{7,6},{8,9},{9,8},{10,11... | collective-permute-start | bytes 2211848 | tf_op jit(solution)/shard_map/ppermute | solution.py:25
  141.4 23.7 %collective-permute-start.41 = (bf16[10,48,768]{2,1,0:T(8,128)(2,1)S(1)}, bf16[10,48,768]{2,1,0:T(8,128)(2,1)S(1)}, u32[]{:S(2)}, u32[]{:S(2)}) collective-permute-start(bf16[10,48,768]{2,1,0:T(8,128)(2,1)S(1)} %collective-permute-done.27._.refs_6_), channel_id=1, source_target_pairs={{0,1},{1,0},{2,3},{3,2},{4,5},{5,4},{6,7},{7,6},{8,9},{9,8},{10,11... | collective-permute-start | bytes 2211848 | tf_op jit(solution)/shard_map/ppermute | solution.py:25
  149.3 15.0 %collective-permute-start.44 = (bf16[5,48,768]{2,1,0:T(8,128)(2,1)S(1)}, bf16[5,48,768]{2,1,0:T(8,128)(2,1)S(1)}, u32[]{:S(2)}, u32[]{:S(2)}) collective-permute-start(bf16[5,48,768]{2,1,0:T(8,128)(2,1)S(1)} %collective-permute-done.39.refs_9_), channel_id=1, source_target_pairs={{0,1},{1,0},{2,3},{3,2},{4,5},{5,4},{6,7},{7,6},{8,9},{9,8},{10,11... | collective-permute-start | bytes 1105928 | tf_op jit(solution)/shard_map/ppermute | solution.py:25
  151.1 13.8 %collective-permute-start.43 = (bf16[5,48,768]{2,1,0:T(8,128)(2,1)S(1)}, bf16[5,48,768]{2,1,0:T(8,128)(2,1)S(1)}, u32[]{:S(2)}, u32[]{:S(2)}) collective-permute-start(bf16[5,48,768]{2,1,0:T(8,128)(2,1)S(1)} %collective-permute-done.38.refs_8_), channel_id=1, source_target_pairs={{0,1},{1,0},{2,3},{3,2},{4,5},{5,4},{6,7},{7,6},{8,9},{9,8},{10,11... | collective-permute-start | bytes 1105928 | tf_op jit(solution)/shard_map/ppermute | solution.py:25
  160.5 10.4 %collective-permute-start.33 = (bf16[6,48,768]{2,1,0:T(8,128)(2,1)S(1)}, bf16[6,48,768]{2,1,0:T(8,128)(2,1)S(1)}, u32[]{:S(2)}, u32[]{:S(2)}) collective-permute-start(bf16[6,48,768]{2,1,0:T(8,128)(2,1)S(1)} %bitcast.51), channel_id=1, source_target_pairs={{0,1},{1,0},{2,3},{3,2},{4,5},{5,4},{6,7},{7,6},{8,9},{9,8},{10,11... | collective-permute-start | bytes 1327112 | tf_op jit(solution)/shard_map/ppermute | solution.py:25
  (15 other events, 76.5 us)

commit v3 on v2

v3 whole, which is shorter than its diff:
```python
import functools
import math

import jax
import jax.numpy as jnp
from jax import lax
from jax.experimental import pallas as pl
from jax.experimental.pallas import tpu as pltpu
from jax.sharding import Mesh, PartitionSpec as P

N = 12288
BLOCK = 64
AXES = ("yl", "z", "x", "yh", "core")
F32, BF16 = jnp.float32, jnp.bfloat16
T = 768
H = T // 2
A = H
S = 48
VMEM = pl.BlockSpec(memory_space=pltpu.VMEM)


def ring(axis, step):
    return lambda a: lax.ppermute(a, axis, [(i, (i + step) % 4) for i in range(4)])


def swap(axis):
    return lambda a: lax.ppermute(a, axis, [(0, 1), (1, 0)])


def across(axis, step, other):
    first, axes = AXES.index(axis) < AXES.index(other), sorted((axis, other), key=AXES.index)
    count = 4 if axis in "xz" else 2
    at = (lambda i, o: i * 2 + o) if first else (lambda i, o: o * count + i)
    moves = [(at(i, o), at((i + step) % count, 1 - o)) for i in range(count) for o in range(2)]
    return lambda a: lax.ppermute(a, tuple(axes), moves)


def tdot(a, b):
    return lax.dot_general(a, b, (((0,), (0,)), ((), ())), preferred_element_type=F32)


def dot(a, b):
    return jnp.dot(a, b, preferred_element_type=F32)


def dot_t(a, b):
    return lax.dot_general(a, b, (((1,), (1,)), ((), ())), preferred_element_type=F32)


def params(mib):
    return pltpu.CompilerParams(vmem_limit_bytes=mib << 20)


def cost(flops, size):
    return pl.CostEstimate(flops=flops, bytes_accessed=size, transcendentals=0)


def dequant_kernel(codes, scales, out):
    factor = scales[...].T
    lane = lax.broadcasted_iota(jnp.int32, (T, 128), 1)
    for g in range(T // 128):
        both = jnp.where(lane < BLOCK, factor[:, 2 * g : 2 * g + 1], factor[:, 2 * g + 1 : 2 * g + 2])
        levels = codes[:, 128 * g : 128 * (g + 1)].astype(F32) - 7.5
        out[:, 128 * g : 128 * (g + 1)] = (levels * both).astype(BF16)


def dequant(codes, scales):
    return pl.pallas_call(
        dequant_kernel,
        out_shape=jax.ShapeDtypeStruct((T, T), BF16),
        in_specs=[VMEM, VMEM],
        out_specs=VMEM,
        compiler_params=params(12),
        cost_estimate=cost(2 * T * T, 6 * T * T),
    )(codes, scales)


def cut(full, first, count, keep, send):
    z, k = lax.axis_index("z"), lax.axis_index("core")
    for half in range(count):
        for j in range(4):
            at = half * H + lax.rem(z + j, 4) * S
            to = pl.ds((first + half) * S, S)
            keep[j, to, :] = full[pl.ds(pl.multiple_of(at + k * (4 * S), 16), S), :].astype(BF16)
            send[j, to, :] = full[pl.ds(pl.multiple_of(at + (1 - k) * (4 * S), 16), S), :].astype(BF16)


def gram_kernel0(own, keep, send, full):
    full[...] = tdot(own[...], own[...])
    cut(full, 0, 2, keep, send)


def gram_kernel1(own, near1, far, _, __, ___, keep, send, full):
    turned = near1[...].T
    full[...] = dot(turned, own[...])
    cut(full, 0, 2, keep, send)
    full[...] = dot(turned, far[...])
    cut(full, 2, 2, keep, send)
    h = lax.axis_index("yh")

    @pl.when(h == 0)
    def _():
        full[0:H, :] = tdot(far[:, 0:H], own[...])

    @pl.when(h != 0)
    def _():
        full[0:H, :] = tdot(own[:, H:T], far[...])

    cut(full, 4, 1, keep, send)


def gram_kernel2(own, far, near2a, near2b, _, keep, send, full):
    low = lax.axis_index("x") < 2
    for i, other in enumerate((own, far)):

        @pl.when(low)
        def _():
            full[0:H, :] = tdot(near2a[:, 0:H], other[0:A, :]) + tdot(near2b[:, 0:H], other[A:T, :])

        @pl.when(jnp.logical_not(low))
        def _():
            full[0:H, :] = tdot(other[0:A, H:T], near2a[...]) + tdot(other[A:T, H:T], near2b[...])

        cut(full, i, 1, keep, send)


def gram(kernel, halves, tiles, later=()):
    out = jax.ShapeDtypeStruct((4, halves * S, T), BF16)
    return pl.pallas_call(
        kernel,
        out_shape=(out, out),
        in_specs=[VMEM] * (len(tiles) + len(later)),
        out_specs=(VMEM, VMEM),
        scratch_shapes=[pltpu.VMEM((T, T), F32)],
        compiler_params=params(14),
        cost_estimate=cost(halves * T * T * T, 6 * T * T),
    )(*tiles, *later)


def local(kernel, shapes, *operands):
    out = tuple(jax.ShapeDtypeStruct(shape, BF16) for shape in shapes)
    return pl.pallas_call(
        kernel,
        out_shape=out,
        in_specs=[VMEM] * len(operands),
        out_specs=(VMEM,) * len(out),
        compiler_params=params(12),
        cost_estimate=cost(0, sum(4 * math.prod(shape) for shape in shapes)),
    )(*operands)


def rows_of(value, first, count, *later):
    def kernel(src, *refs):
        refs[-1][...] = src[first : first + count]

    return local(kernel, [(count,) + value.shape[1:]], value, *later)[0]


def gate(value, *later):
    return pl.pallas_call(
        lambda *refs: None,
        out_shape=jax.ShapeDtypeStruct(value.shape, value.dtype),
        in_specs=[VMEM] * (1 + len(later)),
        out_specs=VMEM,
        input_output_aliases={0: 0},
        compiler_params=params(8),
        cost_estimate=cost(0, 0),
    )(value, *later)


def add(*values):
    total = values[0].astype(F32)
    for value in values[1:]:
        total += value.astype(F32)
    return total


def sum_z(keep, send):
    other = swap("core")(send)
    count = keep.shape[1]
    n = count // 32 * 16

    def step1(keep, other, by_up, by_down):
        by_up[...] = add(keep[2, 0:n], other[2, 0:n]).astype(BF16)
        by_down[...] = add(keep[2, n:count], other[2, n:count]).astype(BF16)

    def step2(keep, other, from_down, from_up, up, down):
        up[0:n] = add(keep[1, 0:n], other[1, 0:n], from_down[...]).astype(BF16)
        up[n:count] = add(keep[1, n:count], other[1, n:count]).astype(BF16)
        down[0:n] = add(keep[3, 0:n], other[3, 0:n]).astype(BF16)
        down[n:count] = add(keep[3, n:count], other[3, n:count], from_up[...]).astype(BF16)

    def step3(keep, other, from_down, from_up, out):
        out[...] = add(keep[0], other[0], from_down[...], from_up[...]).astype(BF16)

    up, down = local(step1, [(n, T), (count - n, T)], keep, other)
    up, down = ring("z", 1)(up), ring("z", -1)(down)
    up, down = local(step2, [(count, T)] * 2, keep, other, up, down)
    sent = up
    up, down = ring("z", 1)(up), ring("z", -1)(down)
    return local(step3, [(count, T)], keep, other, up, down)[0], sent


def line_kernel(shard0, shard1, from_x1, from_y1, shard2, from_x2, from_y2, out):
    out[0 : 2 * S] = shard0[...]
    out[2 * S : 4 * S] = shard1[0 : 2 * S]
    out[4 * S : 8 * S] = from_x1[...]
    out[8 * S : 10 * S] = from_y1[0 : 2 * S]
    high = (lax.axis_index("x") >= 2).astype(jnp.int32)
    for at, swapped, mine, theirs in (
        (10, lax.axis_index("yh"), shard1[4 * S : 5 * S], from_y1[2 * S : 3 * S]),
        (12, high, shard2[0:S], from_x2[0:S]),
        (14, high, from_y2[...], from_x2[S : 2 * S]),
    ):
        out[pl.ds(pl.multiple_of((at + swapped) * S, S), S)] = mine
        out[pl.ds(pl.multiple_of((at + 1 - swapped) * S, S), S)] = theirs


RANGES = ((0, 0, 16), (1, 0, 16), (3, 0, 16), (2, 0, 8), (2, 8, 8))


def product_kernel(plan, *refs):
    x, h, z, k = (lax.axis_index(axis) for axis in ("x", "yh", "z", "core"))
    refs = list(refs)
    tiles = [[refs.pop(0) for _ in range(parts)] for _, parts, _ in plan]
    slices = [refs.pop(0) for _ in range(2 * len(RANGES))]
    out, gram_out, g, g_sem, acc = refs

    g_copies = []
    for c in range(2):
        for j, start, size in RANGES:
            core = k if c == 0 else 1 - k
            at = pl.multiple_of(core * (4 * S) + lax.rem(z + j, 4) * S, 16)
            n = len(g_copies)
            g_copies.append(pltpu.make_async_copy(slices[n], g.at[pl.ds(start, size), pl.ds(at, S)], g_sem.at[n]))
    for copy in g_copies:
        copy.start()
    for copy in g_copies:
        copy.wait()

    def tile(t):
        return g[2 * t : 2 * t + 2].reshape(T, T)

    def is_turned(turn):
        return {"no": z < 0, "yes": z >= 0, "h": h != 0, "x": x >= 2}[turn]

    for t, (_, _, turn) in enumerate(plan):
        turned = is_turned(turn)

        def add(multiply):
            at = 0
            for part in tiles[t]:
                rows = slice(at, at + part.shape[0])
                value = multiply(part[...], tile(t))
                if t > 0:
                    acc[rows, :] += value
                else:
                    acc[rows, :] = value
                at += part.shape[0]

        if turn != "yes":

            @pl.when(jnp.logical_not(turned))
            def _():
                add(dot)

        if turn != "no":

            @pl.when(turned)
            def _():
                add(dot_t)

    out[...] = (1.5 * tiles[0][0][...].astype(F32) - 0.5 * acc[...]).astype(BF16)
    line = lax.axis_index("yl") * 4 + z
    dx, dh = lax.rem(line // 2 - x + 4, 4), lax.rem(line + h, 2)
    for t, ((ax, ah), _, turn) in enumerate(plan):
        mine, turned = (dx == ax) & (dh == ah), is_turned(turn)
        if turn != "yes":

            @pl.when(mine & jnp.logical_not(turned))
            def _():
                gram_out[...] = g[2 * t + k]

        if turn != "no":
            for side in range(2):

                @pl.when(mine & turned & (k == side))
                def _():
                    gram_out[...] = g[2 * t : 2 * t + 2, :, side * H : (side + 1) * H].reshape(T, H).T


def product(plan, slices):
    tiles = [part for _, source, _ in plan for part in source]
    shape = tuple((d, len(source), turn) for d, source, turn in plan)
    return pl.pallas_call(
        functools.partial(product_kernel, shape),
        out_shape=(jax.ShapeDtypeStruct((T, T), BF16), jax.ShapeDtypeStruct((H, T), BF16)),
        in_specs=[VMEM] * (len(tiles) + len(slices)),
        out_specs=(VMEM, VMEM),
        scratch_shapes=[
            pltpu.VMEM((16, H, T), BF16),
            pltpu.SemaphoreType.DMA((len(slices),)),
            pltpu.VMEM((T, T), F32),
        ],
        compiler_params=params(26),
        cost_estimate=cost(16 * T * T * T, 36 * T * T),
    )(*tiles, *slices)


def sum_yl(total):
    total = total.astype(F32) + swap("yl")(total).astype(F32)
    return (total * (1.0 / N)).astype(BF16)


def spread(shard, later):
    n = shard.shape[0] // 2
    one, three = ring("z", -1)(shard), ring("z", 1)(shard)
    mine = [shard, one, three]
    mine += [ring("z", -1)(rows_of(one, 0, n, *later)), ring("z", 1)(rows_of(three, n, n, *later))]
    return mine + [swap("core")(a) for a in mine]


def body(quant_codes, block_scales):
    own = dequant(quant_codes, block_scales)

    near1 = ring("x", -1)(own)
    near3 = ring("x", 1)(own)
    far = swap("yh")(own)
    total0, _ = sum_z(*gram(gram_kernel0, 2, [own]))
    down, up = rows_of(near1, 0, H, total0), rows_of(near3, H, H, total0)
    near2 = (ring("x", -1)(down), ring("x", 1)(up))

    total1, sent = sum_z(*gram(gram_kernel1, 5, [own, near1, far], [total0, down, up]))
    total2, _ = sum_z(*gram(gram_kernel2, 2, [own, far, *near2], [sent]))
    shard0, shard1, shard2 = sum_yl(total0), sum_yl(total1), sum_yl(total2)
    from_x1 = ring("x", 1)(shard1[: 4 * S])
    from_y1 = swap("yh")(shard1[2 * S :])
    from_x2 = ring("x", 2)(shard2)
    from_y2 = swap("yh")(shard2[S:])
    line = local(line_kernel, [(16 * S, T)], shard0, shard1, from_x1, from_y1, shard2, from_x2, from_y2)[0]

    def stack(top, bottom, _, out):
        out[0:H] = top[...]
        out[H:T] = bottom[...]

    again = rows_of(far, 0, T, line)
    far1, far3 = ring("x", -1)(again), ring("x", 1)(again)
    far2 = swap("yh")(local(stack, [(T, T)], *near2, line)[0])
    slices = spread(line.reshape(16, S, T), (far1, far2, far3))

    plan = (
        ((0, 0), (own,), "no"),
        ((1, 0), (near1,), "no"),
        ((3, 0), (near3,), "yes"),
        ((3, 1), (far3,), "yes"),
        ((1, 1), (far1,), "no"),
        ((0, 1), (far,), "h"),
        ((2, 0), near2, "x"),
        ((2, 1), (far2,), "x"),
    )
    return product(plan, slices)


def solution(mesh):
    split = Mesh(mesh.devices.reshape(2, 4, 4, 2, 2), AXES)
    line, side = ("yl", "z", "core"), ("x", "yh")
    return jax.shard_map(
        body,
        mesh=split,
        in_specs=(P(line, side), P(side, line)),
        out_specs=(P(line, side), P(line, side)),
        check_vma=False,
    )
```

time: 177 us -> 161 us (0.910)
  waiting for transfers between devices: 89.7 us -> 70.7 us
  starting transfers between devices: 63.2 us -> 66.6 us
    ppermute x27 -> x24, waiting for transfers between devices: 80.9 us -> 40.9 us  [ring(): lax.ppermute(a, axis, [(i, (i + step) % 4) for i in range(4)])]
    ppermute x18 -> x15, waiting for transfers between devices: 8.74 us -> 29.8 us  [swap(): return lambda a: lax.ppermute(a, axis, [(0, 1), (1, 0)])]
    ppermute x27 -> x24, starting transfers between devices: 32.8 us -> 36.8 us  [ring(): lax.ppermute(a, axis, [(i, (i + step) % 4) for i in range(4)])]
    ppermute x18 -> x15, starting transfers between devices: 30.4 us -> 29.8 us  [swap(): return lambda a: lax.ppermute(a, axis, [(0, 1), (1, 0)])]
    pallas_call x7 -> x17, Pallas kernels: 11.6 us -> 12 us  [the longest x1 10.7 us: product(): pl.pallas_call(functools.partial(product_kernel, shape), out_shape=(jax.S...]
  transfers between devices with their start and end apart: 45 -> 39, of which waited for: 19 -> 19; matrix products, arithmetic and copies ran while one was open for 1% -> 0% of each run, Pallas kernels for 3% -> 1%
where the time goes in v3:
time: 161 us
  waiting for transfers between devices  70.7 us (44%)
  starting transfers between devices  66.6 us (41%)
  Pallas kernels  19.6 us (12%)
  local copies, waits for them, and re-layouts  2.5 us (2%)
    ppermute x24, waiting for transfers between devices, ring(): lax.ppermute(a, axis, [(i, (i + step) % 4) for i in range(4)])  40.9 us
    ppermute x24, starting transfers between devices, ring(): lax.ppermute(a, axis, [(i, (i + step) % 4) for i in range(4)])  36.8 us
    ppermute x15, waiting for transfers between devices, swap(): return lambda a: lax.ppermute(a, axis, [(0, 1), (1, 0)])  29.8 us
    ppermute x15, starting transfers between devices, swap(): return lambda a: lax.ppermute(a, axis, [(0, 1), (1, 0)])  29.8 us
    pallas_call x1, Pallas kernels, product(): pl.pallas_call(functools.partial(product_kernel, shape), out_shape=(jax.S...  10.7 us
    pallas_call x3, Pallas kernels, gram(): pl.pallas_call(kernel, out_shape=(out, out), in_specs=[VMEM] * (len(tiles...  6.12 us
  transfers between devices with their start and end apart: 39, of which 19 were waited for; matrix products, arithmetic and copies ran while one was open for 0% of the time, Pallas kernels for 1%

profile of v3, /device:TPU:1, one launch (start us, length us, event | category | flops | bytes accessed | tf_op | source)
XLA Modules:
  0.0 160.6 jit_solution(7870273764407276296)
XLA Ops:
  4.5 2.1 %collective-permute-start.1 = (bf16[768,768]{1,0:T(8,128)(2,1)S(1)}, bf16[768,768]{1,0:T(8,128)(2,1)S(1)}, u32[]{:S(2)}, u32[]{:S(2)}) collective-permute-start(bf16[768,768]{1,0:T(8,128)(2,1)S(1)} %shard_map.41.own.refs_0_), channel_id=1, source_target_pairs={{0,4},{4,8},{8,12},{12,0},{1,5},{5,9},{9,13},{13,1},{2,6},{6,10},{... | collective-permute-start | bytes 3538952 | tf_op jit(solution)/shard_map/ppermute | solution.py:23
  8.0 3.0 %collective-permute-start.2 = (bf16[768,768]{1,0:T(8,128)(2,1)S(1)}, bf16[768,768]{1,0:T(8,128)(2,1)S(1)}, u32[]{:S(2)}, u32[]{:S(2)}) collective-permute-start(bf16[768,768]{1,0:T(8,128)(2,1)S(1)} %shard_map.41.own.refs_0_), channel_id=1, source_target_pairs={{0,2},{2,0},{1,3},{3,1},{4,6},{6,4},{5,7},{7,5},{8,10},{10,8},{9,1... | collective-permute-start | bytes 3538952 | tf_op jit(solution)/shard_map/ppermute | solution.py:27
  17.3 2.2 %collective-permute-start.5 = (bf16[48,768]{1,0:T(8,128)(2,1)S(1)}, bf16[48,768]{1,0:T(8,128)(2,1)S(1)}, u32[]{:S(2)}, u32[]{:S(2)}) collective-permute-start(bf16[48,768]{1,0:T(8,128)(2,1)S(1)} %get-tuple-element.23), channel_id=1, source_target_pairs={{0,48},{16,0},{32,16},{48,32},{1,49},{17,1},{33,17},{49,33},{2,50}... | collective-permute-start | bytes 221192 | tf_op jit(solution)/shard_map/ppermute | solution.py:23
  19.5 2.3 %collective-permute-done.4.from_down = bf16[48,768]{1,0:T(8,128)(2,1)S(1)} collective-permute-done((bf16[48,768]{1,0:T(8,128)(2,1)S(1)}, bf16[48,768]{1,0:T(8,128)(2,1)S(1)}, u32[]{:S(2)}, u32[]{:S(2)}) %collective-permute-start.4) | collective-permute-done | bytes 73760 | tf_op jit(solution)/shard_map/ppermute | solution.py:23
  22.6 2.0 %collective-permute-start.7 = (bf16[96,768]{1,0:T(8,128)(2,1)S(1)}, bf16[96,768]{1,0:T(8,128)(2,1)S(1)}, u32[]{:S(2)}, u32[]{:S(2)}) collective-permute-start(bf16[96,768]{1,0:T(8,128)(2,1)S(1)} %get-tuple-element.25), channel_id=1, source_target_pairs={{0,48},{16,0},{32,16},{48,32},{1,49},{17,1},{33,17},{49,33},{2,50}... | collective-permute-start | bytes 442376 | tf_op jit(solution)/shard_map/ppermute | solution.py:23
  24.6 3.0 %collective-permute-done.6.from_down = bf16[96,768]{1,0:T(8,128)(2,1)S(1)} collective-permute-done((bf16[96,768]{1,0:T(8,128)(2,1)S(1)}, bf16[96,768]{1,0:T(8,128)(2,1)S(1)}, u32[]{:S(2)}, u32[]{:S(2)}) %collective-permute-start.6) | collective-permute-done | bytes 147488 | tf_op jit(solution)/shard_map/ppermute | solution.py:23
  27.7 5.5 %collective-permute-done.1.src.refs_2_ = bf16[768,768]{1,0:T(8,128)(2,1)S(1)} collective-permute-done((bf16[768,768]{1,0:T(8,128)(2,1)S(1)}, bf16[768,768]{1,0:T(8,128)(2,1)S(1)}, u32[]{:S(2)}, u32[]{:S(2)}) %collective-permute-start.1) | collective-permute-done | bytes 1179680 | tf_op jit(solution)/shard_map/ppermute | solution.py:23
  33.3 2.6 %collective-permute-done.2.far.src.refs_5_ = bf16[768,768]{1,0:T(8,128)(2,1)S(1)} collective-permute-done((bf16[768,768]{1,0:T(8,128)(2,1)S(1)}, bf16[768,768]{1,0:T(8,128)(2,1)S(1)}, u32[]{:S(2)}, u32[]{:S(2)}) %collective-permute-start.2) | collective-permute-done | bytes 1179680 | tf_op jit(solution)/shard_map/ppermute | solution.py:27
  35.8 3.0 %shard_map.48 = (bf16[4,240,768]{2,1,0:T(8,128)(2,1)S(1)}, bf16[4,240,768]{2,1,0:T(8,128)(2,1)S(1)}) custom-call(bf16[768,768]{1,0:T(8,128)(2,1)S(1)} %shard_map.41.own.refs_0_, bf16[768,768]{1,0:T(8,128)(2,1)S(1)} %collective-permute-done.src.near1.refs_1_, bf16[768,768]{1,0:T(8,128)(2,1)S(1)} %collective-permute-done.2.far.src.refs_5_, ...), custom_call_target="tpu_custom_call" | custom-call | flops 2264924160 | bytes 3538944 | tf_op jit(solution)/shard_map/pallas_call | solution.py:129
  38.8 2.2 %collective-permute-start.9 = (bf16[4,240,768]{2,1,0:T(8,128)(2,1)S(1)}, bf16[4,240,768]{2,1,0:T(8,128)(2,1)S(1)}, u32[]{:S(2)}, u32[]{:S(2)}) collective-permute-start(bf16[4,240,768]{2,1,0:T(8,128)(2,1)S(1)} %get-tuple-element.27), channel_id=1, source_target_pairs={{0,1},{1,0},{2,3},{3,2},{4,5},{5,4},{6,7},{7,6},{8,9},{9,8},{10,11... | collective-permute-start | bytes 4423688 | tf_op jit(solution)/shard_map/ppermute | solution.py:27
  41.1 2.6 %collective-permute-start.17 = (bf16[384,768]{1,0:T(8,128)(2,1)S(1)}, bf16[384,768]{1,0:T(8,128)(2,1)S(1)}, u32[]{:S(2)}, u32[]{:S(2)}) collective-permute-start(bf16[384,768]{1,0:T(8,128)(2,1)S(1)} %shard_map.46.__), channel_id=1, source_target_pairs={{0,12},{4,0},{8,4},{12,8},{1,13},{5,1},{9,5},{13,9},{2,14},{6,2},{... | collective-permute-start | bytes 1769480 | tf_op jit(solution)/shard_map/ppermute | solution.py:23
  44.0 3.9 %collective-permute-start.11 = (bf16[128,768]{1,0:T(8,128)(2,1)S(1)}, bf16[128,768]{1,0:T(8,128)(2,1)S(1)}, u32[]{:S(2)}, u32[]{:S(2)}) collective-permute-start(bf16[128,768]{1,0:T(8,128)(2,1)S(1)} %get-tuple-element.29), channel_id=1, source_target_pairs={{0,48},{16,0},{32,16},{48,32},{1,49},{17,1},{33,17},{49,33},{2,50}... | collective-permute-start | bytes 589832 | tf_op jit(solution)/shard_map/ppermute | solution.py:23
  47.9 6.4 %collective-permute-done.10.from_down = bf16[112,768]{1,0:T(8,128)(2,1)S(1)} collective-permute-done((bf16[112,768]{1,0:T(8,128)(2,1)S(1)}, bf16[112,768]{1,0:T(8,128)(2,1)S(1)}, u32[]{:S(2)}, u32[]{:S(2)}) %collective-permute-start.10) | collective-permute-done | bytes 172064 | tf_op jit(solution)/shard_map/ppermute | solution.py:23
  54.5 2.6 %collective-permute-done.18.near2b.bottom.refs_7_ = bf16[384,768]{1,0:T(8,128)(2,1)S(1)} collective-permute-done((bf16[384,768]{1,0:T(8,128)(2,1)S(1)}, bf16[384,768]{1,0:T(8,128)(2,1)S(1)}, u32[]{:S(2)}, u32[]{:S(2)}) %collective-permute-start.18) | collective-permute-done | bytes 589856 | tf_op jit(solution)/shard_map/ppermute | solution.py:23
  57.1 1.9 %shard_map.52 = (bf16[4,96,768]{2,1,0:T(8,128)(2,1)S(1)}, bf16[4,96,768]{2,1,0:T(8,128)(2,1)S(1)}) custom-call(bf16[768,768]{1,0:T(8,128)(2,1)S(1)} %shard_map.41.own.refs_0_, bf16[768,768]{1,0:T(8,128)(2,1)S(1)} %collective-permute-done.2.far.src.refs_5_, bf16[384,768]{1,0:T(8,128)(2,1)S(1)} %collective-permute-done.17.near2a.top.refs_6_, ...), custom_call_target="tpu_custom_call" | custom-call | flops 905969664 | bytes 3538944 | tf_op jit(solution)/shard_map/pallas_call | solution.py:129
  60.0 3.8 %collective-permute-start.13 = (bf16[240,768]{1,0:T(8,128)(2,1)S(1)}, bf16[240,768]{1,0:T(8,128)(2,1)S(1)}, u32[]{:S(2)}, u32[]{:S(2)}) collective-permute-start(bf16[240,768]{1,0:T(8,128)(2,1)S(1)} %get-tuple-element.31), channel_id=1, source_target_pairs={{0,48},{16,0},{32,16},{48,32},{1,49},{17,1},{33,17},{49,33},{2,50}... | collective-permute-start | bytes 1105928 | tf_op jit(solution)/shard_map/ppermute | solution.py:23
  63.8 7.9 %collective-permute-done.13.from_up = bf16[240,768]{1,0:T(8,128)(2,1)S(1)} collective-permute-done((bf16[240,768]{1,0:T(8,128)(2,1)S(1)}, bf16[240,768]{1,0:T(8,128)(2,1)S(1)}, u32[]{:S(2)}, u32[]{:S(2)}) %collective-permute-start.13) | collective-permute-done | bytes 368672 | tf_op jit(solution)/shard_map/ppermute | solution.py:23
  71.8 3.1 %collective-permute-done.12.from_down = bf16[240,768]{1,0:T(8,128)(2,1)S(1)} collective-permute-done((bf16[240,768]{1,0:T(8,128)(2,1)S(1)}, bf16[240,768]{1,0:T(8,128)(2,1)S(1)}, u32[]{:S(2)}, u32[]{:S(2)}) %collective-permute-start.12) | collective-permute-done | bytes 368672 | tf_op jit(solution)/shard_map/ppermute | solution.py:23
  76.5 2.7 %collective-permute-start.21 = (bf16[48,768]{1,0:T(8,128)(2,1)S(1)}, bf16[48,768]{1,0:T(8,128)(2,1)S(1)}, u32[]{:S(2)}, u32[]{:S(2)}) collective-permute-start(bf16[48,768]{1,0:T(8,128)(2,1)S(1)} %get-tuple-element.35), channel_id=1, source_target_pairs={{0,48},{16,0},{32,16},{48,32},{1,49},{17,1},{33,17},{49,33},{2,50}... | collective-permute-start | bytes 221192 | tf_op jit(solution)/shard_map/ppermute | solution.py:23
  81.1 2.7 %collective-permute-start.23 = (bf16[96,768]{1,0:T(8,128)(2,1)S(1)}, bf16[96,768]{1,0:T(8,128)(2,1)S(1)}, u32[]{:S(2)}, u32[]{:S(2)}) collective-permute-start(bf16[96,768]{1,0:T(8,128)(2,1)S(1)} %get-tuple-element.37), channel_id=1, source_target_pairs={{0,48},{16,0},{32,16},{48,32},{1,49},{17,1},{33,17},{49,33},{2,50}... | collective-permute-start | bytes 442376 | tf_op jit(solution)/shard_map/ppermute | solution.py:23
  84.0 2.3 %collective-permute-done.22.from_down = bf16[96,768]{1,0:T(8,128)(2,1)S(1)} collective-permute-done((bf16[96,768]{1,0:T(8,128)(2,1)S(1)}, bf16[96,768]{1,0:T(8,128)(2,1)S(1)}, u32[]{:S(2)}, u32[]{:S(2)}) %collective-permute-start.22) | collective-permute-done | bytes 147488 | tf_op jit(solution)/shard_map/ppermute | solution.py:23
  86.8 3.0 %collective-permute-start.16 = (bf16[144,768]{1,0:T(8,128)(2,1)S(1)}, bf16[144,768]{1,0:T(8,128)(2,1)S(1)}, u32[]{:S(2)}, u32[]{:S(2)}) collective-permute-start(bf16[144,768]{1,0:T(8,128)(2,1)S(1)} %slice.13), channel_id=1, source_target_pairs={{0,2},{2,0},{1,3},{3,1},{4,6},{6,4},{5,7},{7,5},{8,10},{10,8},{9,1... | collective-permute-start | bytes 663560 | tf_op jit(solution)/shard_map/ppermute | solution.py:27
  91.4 2.4 %collective-permute-start.25 = (bf16[96,768]{1,0:T(8,128)(2,1)S(1)}, bf16[96,768]{1,0:T(8,128)(2,1)S(1)}, u32[]{:S(2)}, u32[]{:S(2)}) collective-permute-start(bf16[96,768]{1,0:T(8,128)(2,1)S(1)} %multiply_convert_fusion.1.shard2), channel_id=1, source_target_pairs={{0,8},{4,12},{8,0},{12,4},{1,9},{5,13},{9,1},{13,5},{2,10},{6,14},... | collective-permute-start | bytes 442376 | tf_op jit(solution)/shard_map/ppermute | solution.py:23
  97.3 2.4 %collective-permute-done.26.from_y2 = bf16[48,768]{1,0:T(8,128)(2,1)S(1)} collective-permute-done((bf16[48,768]{1,0:T(8,128)(2,1)S(1)}, bf16[48,768]{1,0:T(8,128)(2,1)S(1)}, u32[]{:S(2)}, u32[]{:S(2)}) %collective-permute-start.26) | collective-permute-done | bytes 73760 | tf_op jit(solution)/shard_map/ppermute | solution.py:27
  103.3 3.3 %collective-permute-start.30 = (bf16[16,48,768]{2,1,0:T(8,128)(2,1)S(1)}, bf16[16,48,768]{2,1,0:T(8,128)(2,1)S(1)}, u32[]{:S(2)}, u32[]{:S(2)}) collective-permute-start(bf16[16,48,768]{2,1,0:T(8,128)(2,1)S(1)} %bitcast.2), channel_id=1, source_target_pairs={{0,48},{16,0},{32,16},{48,32},{1,49},{17,1},{33,17},{49,33},{2,50}... | collective-permute-start | bytes 3538952 | tf_op jit(solution)/shard_map/ppermute | solution.py:23
  106.6 17.2 %collective-permute-done.29.refs_1_.refs_8_ = bf16[768,768]{1,0:T(8,128)(2,1)S(1)} collective-permute-done((bf16[768,768]{1,0:T(8,128)(2,1)S(1)}, bf16[768,768]{1,0:T(8,128)(2,1)S(1)}, u32[]{:S(2)}, u32[]{:S(2)}) %collective-permute-start.29) | collective-permute-done | bytes 1179680 | tf_op jit(solution)/shard_map/ppermute | solution.py:27
  123.8 6.1 %collective-permute-start.34 = (bf16[16,48,768]{2,1,0:T(8,128)(2,1)S(1)}, bf16[16,48,768]{2,1,0:T(8,128)(2,1)S(1)}, u32[]{:S(2)}, u32[]{:S(2)}) collective-permute-start(bf16[16,48,768]{2,1,0:T(8,128)(2,1)S(1)} %bitcast.3), channel_id=1, source_target_pairs={{0,1},{1,0},{2,3},{3,2},{4,5},{5,4},{6,7},{7,6},{8,9},{9,8},{10,11... | collective-permute-start | bytes 3538952 | tf_op jit(solution)/shard_map/ppermute | solution.py:27
  131.1 2.0 %collective-permute-start.32 = (bf16[8,48,768]{2,1,0:T(8,128)(2,1)S(1)}, bf16[8,48,768]{2,1,0:T(8,128)(2,1)S(1)}, u32[]{:S(2)}, u32[]{:S(2)}) collective-permute-start(bf16[8,48,768]{2,1,0:T(8,128)(2,1)S(1)} %shard_map.59), channel_id=1, source_target_pairs={{0,48},{16,0},{32,16},{48,32},{1,49},{17,1},{33,17},{49,33},{2,50}... | collective-permute-start | bytes 1769480 | tf_op jit(solution)/shard_map/ppermute | solution.py:23
  133.1 3.9 %collective-permute-start.36 = (bf16[16,48,768]{2,1,0:T(8,128)(2,1)S(1)}, bf16[16,48,768]{2,1,0:T(8,128)(2,1)S(1)}, u32[]{:S(2)}, u32[]{:S(2)}) collective-permute-start(bf16[16,48,768]{2,1,0:T(8,128)(2,1)S(1)} %collective-permute-done.31.src.refs_11_), channel_id=1, source_target_pairs={{0,1},{1,0},{2,3},{3,2},{4,5},{5,4},{6,7},{7,6},{8,9},{9,8},{10,11... | collective-permute-start | bytes 3538952 | tf_op jit(solution)/shard_map/ppermute | solution.py:27
  137.0 6.0 %collective-permute-done.33.refs_13_ = bf16[8,48,768]{2,1,0:T(8,128)(2,1)S(1)} collective-permute-done((bf16[8,48,768]{2,1,0:T(8,128)(2,1)S(1)}, bf16[8,48,768]{2,1,0:T(8,128)(2,1)S(1)}, u32[]{:S(2)}, u32[]{:S(2)}) %collective-permute-start.33) | collective-permute-done | bytes 589856 | tf_op jit(solution)/shard_map/ppermute | solution.py:23
  143.0 4.3 %collective-permute-start.38 = (bf16[8,48,768]{2,1,0:T(8,128)(2,1)S(1)}, bf16[8,48,768]{2,1,0:T(8,128)(2,1)S(1)}, u32[]{:S(2)}, u32[]{:S(2)}) collective-permute-start(bf16[8,48,768]{2,1,0:T(8,128)(2,1)S(1)} %collective-permute-done.33.refs_13_), channel_id=1, source_target_pairs={{0,1},{1,0},{2,3},{3,2},{4,5},{5,4},{6,7},{7,6},{8,9},{9,8},{10,11... | collective-permute-start | bytes 1769480 | tf_op jit(solution)/shard_map/ppermute | solution.py:27
  149.7 10.7 %shard_map.61 = (bf16[768,768]{1,0:T(8,128)(2,1)}, bf16[384,768]{1,0:T(8,128)(2,1)}) custom-call(bf16[768,768]{1,0:T(8,128)(2,1)S(1)} %shard_map.41.own.refs_0_, bf16[768,768]{1,0:T(8,128)(2,1)S(1)} %collective-permute-done.src.near1.refs_1_, bf16[768,768]{1,0:T(8,128)(2,1)S(1)} %collective-permute-done.1.src.refs_2_, ...), custom_call_target="tpu_custom_call" | custom-call | flops 7247757312 | bytes 21233664 | tf_op jit(solution)/shard_map/pallas_call | solution.py:295
  (77 shorter events, 30.6 us)
Async XLA Ops:
  4.5 28.6 %collective-permute-start.1 = (bf16[768,768]{1,0:T(8,128)(2,1)S(1)}, bf16[768,768]{1,0:T(8,128)(2,1)S(1)}, u32[]{:S(2)}, u32[]{:S(2)}) collective-permute-start(bf16[768,768]{1,0:T(8,128)(2,1)S(1)} %shard_map.41.own.refs_0_), channel_id=1, source_target_pairs={{0,4},{4,8},{8,12},{12,0},{1,5},{5,9},{9,13},{13,1},{2,6},{6,10},{... | collective-permute-start | bytes 3538952 | tf_op jit(solution)/shard_map/ppermute | solution.py:23
  6.7 26.6 %collective-permute-start = (bf16[768,768]{1,0:T(8,128)(2,1)S(1)}, bf16[768,768]{1,0:T(8,128)(2,1)S(1)}, u32[]{:S(2)}, u32[]{:S(2)}) collective-permute-start(bf16[768,768]{1,0:T(8,128)(2,1)S(1)} %shard_map.41.own.refs_0_), channel_id=1, source_target_pairs={{0,12},{4,0},{8,4},{12,8},{1,13},{5,1},{9,5},{13,9},{2,14},{6,2},{... | collective-permute-start | bytes 3538952 | tf_op jit(solution)/shard_map/ppermute | solution.py:23
  8.0 27.8 %collective-permute-start.2 = (bf16[768,768]{1,0:T(8,128)(2,1)S(1)}, bf16[768,768]{1,0:T(8,128)(2,1)S(1)}, u32[]{:S(2)}, u32[]{:S(2)}) collective-permute-start(bf16[768,768]{1,0:T(8,128)(2,1)S(1)} %shard_map.41.own.refs_0_), channel_id=1, source_target_pairs={{0,2},{2,0},{1,3},{3,1},{4,6},{6,4},{5,7},{7,5},{8,10},{10,8},{9,1... | collective-permute-start | bytes 3538952 | tf_op jit(solution)/shard_map/ppermute | solution.py:27
  15.5 6.2 %collective-permute-start.4 = (bf16[48,768]{1,0:T(8,128)(2,1)S(1)}, bf16[48,768]{1,0:T(8,128)(2,1)S(1)}, u32[]{:S(2)}, u32[]{:S(2)}) collective-permute-start(bf16[48,768]{1,0:T(8,128)(2,1)S(1)} %get-tuple-element.22), channel_id=1, source_target_pairs={{0,16},{16,32},{32,48},{48,0},{1,17},{17,33},{33,49},{49,1},{2,18}... | collective-permute-start | bytes 221192 | tf_op jit(solution)/shard_map/ppermute | solution.py:23
  21.8 5.8 %collective-permute-start.6 = (bf16[96,768]{1,0:T(8,128)(2,1)S(1)}, bf16[96,768]{1,0:T(8,128)(2,1)S(1)}, u32[]{:S(2)}, u32[]{:S(2)}) collective-permute-start(bf16[96,768]{1,0:T(8,128)(2,1)S(1)} %get-tuple-element.24), channel_id=1, source_target_pairs={{0,16},{16,32},{32,48},{48,0},{1,17},{17,33},{33,49},{49,1},{2,18}... | collective-permute-start | bytes 442376 | tf_op jit(solution)/shard_map/ppermute | solution.py:23
  38.8 5.1 %collective-permute-start.9 = (bf16[4,240,768]{2,1,0:T(8,128)(2,1)S(1)}, bf16[4,240,768]{2,1,0:T(8,128)(2,1)S(1)}, u32[]{:S(2)}, u32[]{:S(2)}) collective-permute-start(bf16[4,240,768]{2,1,0:T(8,128)(2,1)S(1)} %get-tuple-element.27), channel_id=1, source_target_pairs={{0,1},{1,0},{2,3},{3,2},{4,5},{5,4},{6,7},{7,6},{8,9},{9,8},{10,11... | collective-permute-start | bytes 4423688 | tf_op jit(solution)/shard_map/ppermute | solution.py:27
  41.0 16.1 %collective-permute-start.18 = (bf16[384,768]{1,0:T(8,128)(2,1)S(1)}, bf16[384,768]{1,0:T(8,128)(2,1)S(1)}, u32[]{:S(2)}, u32[]{:S(2)}) collective-permute-start(bf16[384,768]{1,0:T(8,128)(2,1)S(1)} %shard_map.47.___), channel_id=1, source_target_pairs={{0,4},{4,8},{8,12},{12,0},{1,5},{5,9},{9,13},{13,1},{2,6},{6,10},{... | collective-permute-start | bytes 1769480 | tf_op jit(solution)/shard_map/ppermute | solution.py:23
  41.1 16.0 %collective-permute-start.17 = (bf16[384,768]{1,0:T(8,128)(2,1)S(1)}, bf16[384,768]{1,0:T(8,128)(2,1)S(1)}, u32[]{:S(2)}, u32[]{:S(2)}) collective-permute-start(bf16[384,768]{1,0:T(8,128)(2,1)S(1)} %shard_map.46.__), channel_id=1, source_target_pairs={{0,12},{4,0},{8,4},{12,8},{1,13},{5,1},{9,5},{13,9},{2,14},{6,2},{... | collective-permute-start | bytes 1769480 | tf_op jit(solution)/shard_map/ppermute | solution.py:23
  44.0 10.3 %collective-permute-start.11 = (bf16[128,768]{1,0:T(8,128)(2,1)S(1)}, bf16[128,768]{1,0:T(8,128)(2,1)S(1)}, u32[]{:S(2)}, u32[]{:S(2)}) collective-permute-start(bf16[128,768]{1,0:T(8,128)(2,1)S(1)} %get-tuple-element.29), channel_id=1, source_target_pairs={{0,48},{16,0},{32,16},{48,32},{1,49},{17,1},{33,17},{49,33},{2,50}... | collective-permute-start | bytes 589832 | tf_op jit(solution)/shard_map/ppermute | solution.py:23
  47.9 6.4 %collective-permute-start.10 = (bf16[112,768]{1,0:T(8,128)(2,1)S(1)}, bf16[112,768]{1,0:T(8,128)(2,1)S(1)}, u32[]{:S(2)}, u32[]{:S(2)}) collective-permute-start(bf16[112,768]{1,0:T(8,128)(2,1)S(1)} %get-tuple-element.28), channel_id=1, source_target_pairs={{0,16},{16,32},{32,48},{48,0},{1,17},{17,33},{33,49},{49,1},{2,18}... | collective-permute-start | bytes 516104 | tf_op jit(solution)/shard_map/ppermute | solution.py:23
  59.0 17.4 %collective-permute-start.19 = (bf16[4,96,768]{2,1,0:T(8,128)(2,1)S(1)}, bf16[4,96,768]{2,1,0:T(8,128)(2,1)S(1)}, u32[]{:S(2)}, u32[]{:S(2)}) collective-permute-start(bf16[4,96,768]{2,1,0:T(8,128)(2,1)S(1)} %get-tuple-element.33), channel_id=1, source_target_pairs={{0,1},{1,0},{2,3},{3,2},{4,5},{5,4},{6,7},{7,6},{8,9},{9,8},{10,11... | collective-permute-start | bytes 1769480 | tf_op jit(solution)/shard_map/ppermute | solution.py:27
  60.0 11.8 %collective-permute-start.13 = (bf16[240,768]{1,0:T(8,128)(2,1)S(1)}, bf16[240,768]{1,0:T(8,128)(2,1)S(1)}, u32[]{:S(2)}, u32[]{:S(2)}) collective-permute-start(bf16[240,768]{1,0:T(8,128)(2,1)S(1)} %get-tuple-element.31), channel_id=1, source_target_pairs={{0,48},{16,0},{32,16},{48,32},{1,49},{17,1},{33,17},{49,33},{2,50}... | collective-permute-start | bytes 1105928 | tf_op jit(solution)/shard_map/ppermute | solution.py:23
  63.8 11.0 %collective-permute-start.12 = (bf16[240,768]{1,0:T(8,128)(2,1)S(1)}, bf16[240,768]{1,0:T(8,128)(2,1)S(1)}, u32[]{:S(2)}, u32[]{:S(2)}) collective-permute-start(bf16[240,768]{1,0:T(8,128)(2,1)S(1)} %get-tuple-element.30._), channel_id=1, source_target_pairs={{0,16},{16,32},{32,48},{48,0},{1,17},{17,33},{33,49},{49,1},{2,18}... | collective-permute-start | bytes 1105928 | tf_op jit(solution)/shard_map/ppermute | solution.py:23
  75.0 11.6 %collective-permute-start.14 = (bf16[240,768]{1,0:T(8,128)(2,1)S(1)}, bf16[240,768]{1,0:T(8,128)(2,1)S(1)}, u32[]{:S(2)}, u32[]{:S(2)}) collective-permute-start(bf16[240,768]{1,0:T(8,128)(2,1)S(1)} %shard_map.51), channel_id=1, source_target_pairs={{0,64},{64,0},{1,65},{65,1},{2,66},{66,2},{3,67},{67,3},{4,68},{68... | collective-permute-start | bytes 1105928 | tf_op jit(solution)/shard_map/ppermute | solution.py:27
  81.0 5.3 %collective-permute-start.22 = (bf16[96,768]{1,0:T(8,128)(2,1)S(1)}, bf16[96,768]{1,0:T(8,128)(2,1)S(1)}, u32[]{:S(2)}, u32[]{:S(2)}) collective-permute-start(bf16[96,768]{1,0:T(8,128)(2,1)S(1)} %get-tuple-element.36), channel_id=1, source_target_pairs={{0,16},{16,32},{32,48},{48,0},{1,17},{17,33},{33,49},{49,1},{2,18}... | collective-permute-start | bytes 442376 | tf_op jit(solution)/shard_map/ppermute | solution.py:23
  81.1 5.2 %collective-permute-start.23 = (bf16[96,768]{1,0:T(8,128)(2,1)S(1)}, bf16[96,768]{1,0:T(8,128)(2,1)S(1)}, u32[]{:S(2)}, u32[]{:S(2)}) collective-permute-start(bf16[96,768]{1,0:T(8,128)(2,1)S(1)} %get-tuple-element.37), channel_id=1, source_target_pairs={{0,48},{16,0},{32,16},{48,32},{1,49},{17,1},{33,17},{49,33},{2,50}... | collective-permute-start | bytes 442376 | tf_op jit(solution)/shard_map/ppermute | solution.py:23
  83.9 11.5 %collective-permute-start.8 = (bf16[96,768]{1,0:T(8,128)(2,1)S(1)}, bf16[96,768]{1,0:T(8,128)(2,1)S(1)}, u32[]{:S(2)}, u32[]{:S(2)}) collective-permute-start(bf16[96,768]{1,0:T(8,128)(2,1)S(1)} %shard_map.45.refs_0_._), channel_id=1, source_target_pairs={{0,64},{64,0},{1,65},{65,1},{2,66},{66,2},{3,67},{67,3},{4,68},{68... | collective-permute-start | bytes 442376 | tf_op jit(solution)/shard_map/ppermute | solution.py:27
  86.8 10.5 %collective-permute-start.16 = (bf16[144,768]{1,0:T(8,128)(2,1)S(1)}, bf16[144,768]{1,0:T(8,128)(2,1)S(1)}, u32[]{:S(2)}, u32[]{:S(2)}) collective-permute-start(bf16[144,768]{1,0:T(8,128)(2,1)S(1)} %slice.13), channel_id=1, source_target_pairs={{0,2},{2,0},{1,3},{3,1},{4,6},{6,4},{5,7},{7,5},{8,10},{10,8},{9,1... | collective-permute-start | bytes 663560 | tf_op jit(solution)/shard_map/ppermute | solution.py:27
  89.8 9.9 %collective-permute-start.15 = (bf16[192,768]{1,0:T(8,128)(2,1)S(1)}, bf16[192,768]{1,0:T(8,128)(2,1)S(1)}, u32[]{:S(2)}, u32[]{:S(2)}) collective-permute-start(bf16[192,768]{1,0:T(8,128)(2,1)S(1)} %slice.12), channel_id=1, source_target_pairs={{0,4},{4,8},{8,12},{12,0},{1,5},{5,9},{9,13},{13,1},{2,6},{6,10},{... | collective-permute-start | bytes 884744 | tf_op jit(solution)/shard_map/ppermute | solution.py:23
  91.4 8.3 %collective-permute-start.25 = (bf16[96,768]{1,0:T(8,128)(2,1)S(1)}, bf16[96,768]{1,0:T(8,128)(2,1)S(1)}, u32[]{:S(2)}, u32[]{:S(2)}) collective-permute-start(bf16[96,768]{1,0:T(8,128)(2,1)S(1)} %multiply_convert_fusion.1.shard2), channel_id=1, source_target_pairs={{0,8},{4,12},{8,0},{12,4},{1,9},{5,13},{9,1},{13,5},{2,10},{6,14},... | collective-permute-start | bytes 442376 | tf_op jit(solution)/shard_map/ppermute | solution.py:23
  93.8 5.9 %collective-permute-start.26 = (bf16[48,768]{1,0:T(8,128)(2,1)S(1)}, bf16[48,768]{1,0:T(8,128)(2,1)S(1)}, u32[]{:S(2)}, u32[]{:S(2)}) collective-permute-start(bf16[48,768]{1,0:T(8,128)(2,1)S(1)} %slice.14), channel_id=1, source_target_pairs={{0,2},{2,0},{1,3},{3,1},{4,6},{6,4},{5,7},{7,5},{8,10},{10,8},{9,1... | collective-permute-start | bytes 221192 | tf_op jit(solution)/shard_map/ppermute | solution.py:27
  99.8 23.9 %collective-permute-start.29 = (bf16[768,768]{1,0:T(8,128)(2,1)S(1)}, bf16[768,768]{1,0:T(8,128)(2,1)S(1)}, u32[]{:S(2)}, u32[]{:S(2)}) collective-permute-start(bf16[768,768]{1,0:T(8,128)(2,1)S(1)} %shard_map.58), channel_id=1, source_target_pairs={{0,2},{2,0},{1,3},{3,1},{4,6},{6,4},{5,7},{7,5},{8,10},{10,8},{9,1... | collective-permute-start | bytes 3538952 | tf_op jit(solution)/shard_map/ppermute | solution.py:27
  101.5 28.4 %collective-permute-start.28 = (bf16[768,768]{1,0:T(8,128)(2,1)S(1)}, bf16[768,768]{1,0:T(8,128)(2,1)S(1)}, u32[]{:S(2)}, u32[]{:S(2)}) collective-permute-start(bf16[768,768]{1,0:T(8,128)(2,1)S(1)} %shard_map.57), channel_id=1, source_target_pairs={{0,12},{4,0},{8,4},{12,8},{1,13},{5,1},{9,5},{13,9},{2,14},{6,2},{... | collective-permute-start | bytes 3538952 | tf_op jit(solution)/shard_map/ppermute | solution.py:23
  102.9 26.9 %collective-permute-start.27 = (bf16[768,768]{1,0:T(8,128)(2,1)S(1)}, bf16[768,768]{1,0:T(8,128)(2,1)S(1)}, u32[]{:S(2)}, u32[]{:S(2)}) collective-permute-start(bf16[768,768]{1,0:T(8,128)(2,1)S(1)} %shard_map.57), channel_id=1, source_target_pairs={{0,4},{4,8},{8,12},{12,0},{1,5},{5,9},{9,13},{13,1},{2,6},{6,10},{... | collective-permute-start | bytes 3538952 | tf_op jit(solution)/shard_map/ppermute | solution.py:23
  103.0 26.8 %collective-permute-start.31 = (bf16[16,48,768]{2,1,0:T(8,128)(2,1)S(1)}, bf16[16,48,768]{2,1,0:T(8,128)(2,1)S(1)}, u32[]{:S(2)}, u32[]{:S(2)}) collective-permute-start(bf16[16,48,768]{2,1,0:T(8,128)(2,1)S(1)} %bitcast.1), channel_id=1, source_target_pairs={{0,16},{16,32},{32,48},{48,0},{1,17},{17,33},{33,49},{49,1},{2,18}... | collective-permute-start | bytes 3538952 | tf_op jit(solution)/shard_map/ppermute | solution.py:23
  103.3 27.8 %collective-permute-start.30 = (bf16[16,48,768]{2,1,0:T(8,128)(2,1)S(1)}, bf16[16,48,768]{2,1,0:T(8,128)(2,1)S(1)}, u32[]{:S(2)}, u32[]{:S(2)}) collective-permute-start(bf16[16,48,768]{2,1,0:T(8,128)(2,1)S(1)} %bitcast.2), channel_id=1, source_target_pairs={{0,48},{16,0},{32,16},{48,32},{1,49},{17,1},{33,17},{49,33},{2,50}... | collective-permute-start | bytes 3538952 | tf_op jit(solution)/shard_map/ppermute | solution.py:23
  123.8 23.5 %collective-permute-start.34 = (bf16[16,48,768]{2,1,0:T(8,128)(2,1)S(1)}, bf16[16,48,768]{2,1,0:T(8,128)(2,1)S(1)}, u32[]{:S(2)}, u32[]{:S(2)}) collective-permute-start(bf16[16,48,768]{2,1,0:T(8,128)(2,1)S(1)} %bitcast.3), channel_id=1, source_target_pairs={{0,1},{1,0},{2,3},{3,2},{4,5},{5,4},{6,7},{7,6},{8,9},{9,8},{10,11... | collective-permute-start | bytes 3538952 | tf_op jit(solution)/shard_map/ppermute | solution.py:27
  129.9 13.1 %collective-permute-start.33 = (bf16[8,48,768]{2,1,0:T(8,128)(2,1)S(1)}, bf16[8,48,768]{2,1,0:T(8,128)(2,1)S(1)}, u32[]{:S(2)}, u32[]{:S(2)}) collective-permute-start(bf16[8,48,768]{2,1,0:T(8,128)(2,1)S(1)} %shard_map.60), channel_id=1, source_target_pairs={{0,16},{16,32},{32,48},{48,0},{1,17},{17,33},{33,49},{49,1},{2,18}... | collective-permute-start | bytes 1769480 | tf_op jit(solution)/shard_map/ppermute | solution.py:23
  131.1 16.1 %collective-permute-start.32 = (bf16[8,48,768]{2,1,0:T(8,128)(2,1)S(1)}, bf16[8,48,768]{2,1,0:T(8,128)(2,1)S(1)}, u32[]{:S(2)}, u32[]{:S(2)}) collective-permute-start(bf16[8,48,768]{2,1,0:T(8,128)(2,1)S(1)} %shard_map.59), channel_id=1, source_target_pairs={{0,48},{16,0},{32,16},{48,32},{1,49},{17,1},{33,17},{49,33},{2,50}... | collective-permute-start | bytes 1769480 | tf_op jit(solution)/shard_map/ppermute | solution.py:23
  133.1 16.6 %collective-permute-start.36 = (bf16[16,48,768]{2,1,0:T(8,128)(2,1)S(1)}, bf16[16,48,768]{2,1,0:T(8,128)(2,1)S(1)}, u32[]{:S(2)}, u32[]{:S(2)}) collective-permute-start(bf16[16,48,768]{2,1,0:T(8,128)(2,1)S(1)} %collective-permute-done.31.src.refs_11_), channel_id=1, source_target_pairs={{0,1},{1,0},{2,3},{3,2},{4,5},{5,4},{6,7},{7,6},{8,9},{9,8},{10,11... | collective-permute-start | bytes 3538952 | tf_op jit(solution)/shard_map/ppermute | solution.py:27
  137.0 12.8 %collective-permute-start.35 = (bf16[16,48,768]{2,1,0:T(8,128)(2,1)S(1)}, bf16[16,48,768]{2,1,0:T(8,128)(2,1)S(1)}, u32[]{:S(2)}, u32[]{:S(2)}) collective-permute-start(bf16[16,48,768]{2,1,0:T(8,128)(2,1)S(1)} %collective-permute-done.30.src.refs_10_), channel_id=1, source_target_pairs={{0,1},{1,0},{2,3},{3,2},{4,5},{5,4},{6,7},{7,6},{8,9},{9,8},{10,11... | collective-permute-start | bytes 3538952 | tf_op jit(solution)/shard_map/ppermute | solution.py:27
  143.0 5.9 %collective-permute-start.38 = (bf16[8,48,768]{2,1,0:T(8,128)(2,1)S(1)}, bf16[8,48,768]{2,1,0:T(8,128)(2,1)S(1)}, u32[]{:S(2)}, u32[]{:S(2)}) collective-permute-start(bf16[8,48,768]{2,1,0:T(8,128)(2,1)S(1)} %collective-permute-done.33.refs_13_), channel_id=1, source_target_pairs={{0,1},{1,0},{2,3},{3,2},{4,5},{5,4},{6,7},{7,6},{8,9},{9,8},{10,11... | collective-permute-start | bytes 1769480 | tf_op jit(solution)/shard_map/ppermute | solution.py:27
  (9 other events, 31.5 us)

commit v4 on v3

--- a/solution.py
+++ b/solution.py
@@ -1,4 +1,3 @@
-import functools
 import math
 
 import jax
@@ -175,7 +174,7 @@
     return total
 
 
-def sum_z(keep, send):
+def sum_z_in_steps(keep, send):
     other = swap("core")(send)
     count = keep.shape[1]
     n = count // 32 * 16
@@ -196,21 +195,36 @@
     up, down = local(step1, [(n, T), (count - n, T)], keep, other)
     up, down = ring("z", 1)(up), ring("z", -1)(down)
     up, down = local(step2, [(count, T)] * 2, keep, other, up, down)
-    sent = up
     up, down = ring("z", 1)(up), ring("z", -1)(down)
-    return local(step3, [(count, T)], keep, other, up, down)[0], sent
-
-
-def line_kernel(shard0, shard1, from_x1, from_y1, shard2, from_x2, from_y2, out):
+    return local(step3, [(count, T)], keep, other, up, down)[0]
+
+
+def sum_z(keep, send):
+    other = swap("core")(send)
+    shape = keep.shape[1:]
+
+    def step1(keep, other, *parts):
+        for j, part in enumerate(parts):
+            part[...] = add(keep[j + 1], other[j + 1]).astype(BF16)
+
+    def step2(keep, other, one, three, two, out):
+        out[...] = add(keep[0], other[0], one[...], three[...], two[...]).astype(BF16)
+
+    parts = local(step1, [shape] * 3, keep, other)
+    got = [ring("z", j)(parts[j - 1]) for j in (1, 3, 2)]
+    return local(step2, [shape], keep, other, *got)[0]
+
+
+def line_kernel(shard0, shard1, from_x1, shard2, from_x2, from_y, out):
     out[0 : 2 * S] = shard0[...]
     out[2 * S : 4 * S] = shard1[0 : 2 * S]
-    out[4 * S : 8 * S] = from_x1[...]
-    out[8 * S : 10 * S] = from_y1[0 : 2 * S]
+    out[4 * S : 6 * S] = from_y[0 : 2 * S]
+    out[6 * S : 10 * S] = from_x1[...]
     high = (lax.axis_index("x") >= 2).astype(jnp.int32)
     for at, swapped, mine, theirs in (
-        (10, lax.axis_index("yh"), shard1[4 * S : 5 * S], from_y1[2 * S : 3 * S]),
+        (10, lax.axis_index("yh"), shard1[4 * S : 5 * S], from_y[2 * S : 3 * S]),
         (12, high, shard2[0:S], from_x2[0:S]),
-        (14, high, from_y2[...], from_x2[S : 2 * S]),
+        (14, high, from_y[3 * S : 4 * S], from_x2[S : 2 * S]),
     ):
         out[pl.ds(pl.multiple_of((at + swapped) * S, S), S)] = mine
         out[pl.ds(pl.multiple_of((at + 1 - swapped) * S, S), S)] = theirs
@@ -219,12 +233,21 @@
 RANGES = ((0, 0, 16), (1, 0, 16), (3, 0, 16), (2, 0, 8), (2, 8, 8))
 
 
-def product_kernel(plan, *refs):
+TILES = (
+    ((0, 0), "no"),
+    ((1, 0), "no"),
+    ((1, 1), "no"),
+    ((3, 0), "yes"),
+    ((3, 1), "yes"),
+    ((0, 1), "h"),
+    ((2, 0), "x"),
+    ((2, 1), "x"),
+)
+
+
+def product_kernel(own, near1, far1, near3, far3, far, near2a, near2b, far2, *refs):
     x, h, z, k = (lax.axis_index(axis) for axis in ("x", "yh", "z", "core"))
-    refs = list(refs)
-    tiles = [[refs.pop(0) for _ in range(parts)] for _, parts, _ in plan]
-    slices = [refs.pop(0) for _ in range(2 * len(RANGES))]
-    out, gram_out, g, g_sem, acc = refs
+    slices, (out, gram_out, g, g_sem, acc) = refs[:10], refs[10:]
 
     g_copies = []
     for c in range(2):
@@ -238,43 +261,42 @@
     for copy in g_copies:
         copy.wait()
 
-    def tile(t):
-        return g[2 * t : 2 * t + 2].reshape(T, T)
-
-    def is_turned(turn):
-        return {"no": z < 0, "yes": z >= 0, "h": h != 0, "x": x >= 2}[turn]
-
-    for t, (_, _, turn) in enumerate(plan):
-        turned = is_turned(turn)
-
-        def add(multiply):
-            at = 0
-            for part in tiles[t]:
-                rows = slice(at, at + part.shape[0])
-                value = multiply(part[...], tile(t))
-                if t > 0:
-                    acc[rows, :] += value
-                else:
-                    acc[rows, :] = value
-                at += part.shape[0]
-
-        if turn != "yes":
-
-            @pl.when(jnp.logical_not(turned))
-            def _():
-                add(dot)
-
-        if turn != "no":
-
-            @pl.when(turned)
-            def _():
-                add(dot_t)
-
-    out[...] = (1.5 * tiles[0][0][...].astype(F32) - 0.5 * acc[...]).astype(BF16)
+    def tiles(first, count):
+        return g[2 * first : 2 * (first + count)].reshape(count * T, T)
+
+    def beside(parts):
+        return jnp.concatenate(parts, axis=1)
+
+    def either(turned, straight_way, turned_way):
+        pl.when(jnp.logical_not(turned))(straight_way)
+        pl.when(turned)(turned_way)
+
+    def far_straight():
+        acc[...] = dot(far[...], tiles(5, 1))
+
+    def far_turned():
+        acc[...] = dot_t(far[...], tiles(5, 1))
+
+    either(h != 0, far_straight, far_turned)
+    acc[...] += dot(beside([own[...], near1[...], far1[...]]), tiles(0, 3))
+    acc[...] += dot_t(beside([near3[...], far3[...]]), beside([tiles(3, 1), tiles(4, 1)]))
+
+    def finish(multiply, factor):
+        for i, near2 in enumerate((near2a, near2b)):
+            rows = slice(i * H, (i + 1) * H)
+            total = acc[rows, :] + multiply(beside([near2[...], far2[rows, :]]), factor)
+            out[rows, :] = (1.5 * own[rows, :].astype(F32) - 0.5 * total).astype(BF16)
+
+    either(
+        x >= 2,
+        lambda: finish(dot, tiles(6, 2)),
+        lambda: finish(dot_t, beside([tiles(6, 1), tiles(7, 1)])),
+    )
+
     line = lax.axis_index("yl") * 4 + z
     dx, dh = lax.rem(line // 2 - x + 4, 4), lax.rem(line + h, 2)
-    for t, ((ax, ah), _, turn) in enumerate(plan):
-        mine, turned = (dx == ax) & (dh == ah), is_turned(turn)
+    for t, ((ax, ah), turn) in enumerate(TILES):
+        mine, turned = (dx == ax) & (dh == ah), {"no": z < 0, "yes": z >= 0, "h": h != 0, "x": x >= 2}[turn]
         if turn != "yes":
 
             @pl.when(mine & jnp.logical_not(turned))
@@ -289,22 +311,21 @@
                     gram_out[...] = g[2 * t : 2 * t + 2, :, side * H : (side + 1) * H].reshape(T, H).T
 
 
-def product(plan, slices):
-    tiles = [part for _, source, _ in plan for part in source]
-    shape = tuple((d, len(source), turn) for d, source, turn in plan)
-    return pl.pallas_call(
-        functools.partial(product_kernel, shape),
+def product(tiles, slices):
+    operands = [*tiles, *slices]
+    return pl.pallas_call(
+        product_kernel,
         out_shape=(jax.ShapeDtypeStruct((T, T), BF16), jax.ShapeDtypeStruct((H, T), BF16)),
-        in_specs=[VMEM] * (len(tiles) + len(slices)),
+        in_specs=[VMEM] * len(operands),
         out_specs=(VMEM, VMEM),
         scratch_shapes=[
             pltpu.VMEM((16, H, T), BF16),
             pltpu.SemaphoreType.DMA((len(slices),)),
             pltpu.VMEM((T, T), F32),
         ],
-        compiler_params=params(26),
+        compiler_params=params(30),
         cost_estimate=cost(16 * T * T * T, 36 * T * T),
-    )(*tiles, *slices)
+    )(*operands)
 
 
 def sum_yl(total):
@@ -326,18 +347,22 @@
     near1 = ring("x", -1)(own)
     near3 = ring("x", 1)(own)
     far = swap("yh")(own)
-    total0, _ = sum_z(*gram(gram_kernel0, 2, [own]))
+    total0 = sum_z_in_steps(*gram(gram_kernel0, 2, [own]))
     down, up = rows_of(near1, 0, H, total0), rows_of(near3, H, H, total0)
     near2 = (ring("x", -1)(down), ring("x", 1)(up))
 
-    total1, sent = sum_z(*gram(gram_kernel1, 5, [own, near1, far], [total0, down, up]))
-    total2, _ = sum_z(*gram(gram_kernel2, 2, [own, far, *near2], [sent]))
+    total1 = sum_z(*gram(gram_kernel1, 5, [own, near1, far], [total0, down, up]))
+    total2 = sum_z(*gram(gram_kernel2, 2, [own, far, *near2], [total1]))
     shard0, shard1, shard2 = sum_yl(total0), sum_yl(total1), sum_yl(total2)
     from_x1 = ring("x", 1)(shard1[: 4 * S])
-    from_y1 = swap("yh")(shard1[2 * S :])
     from_x2 = ring("x", 2)(shard2)
-    from_y2 = swap("yh")(shard2[S:])
-    line = local(line_kernel, [(16 * S, T)], shard0, shard1, from_x1, from_y1, shard2, from_x2, from_y2)[0]
+
+    def to_y(first, second, out):
+        out[0 : 3 * S] = first[2 * S : 5 * S]
+        out[3 * S : 4 * S] = second[S : 2 * S]
+
+    from_y = swap("yh")(local(to_y, [(4 * S, T)], shard1, shard2)[0])
+    line = local(line_kernel, [(16 * S, T)], shard0, shard1, from_x1, shard2, from_x2, from_y)[0]
 
     def stack(top, bottom, _, out):
         out[0:H] = top[...]
@@ -348,17 +373,7 @@
     far2 = swap("yh")(local(stack, [(T, T)], *near2, line)[0])
     slices = spread(line.reshape(16, S, T), (far1, far2, far3))
 
-    plan = (
-        ((0, 0), (own,), "no"),
-        ((1, 0), (near1,), "no"),
-        ((3, 0), (near3,), "yes"),
-        ((3, 1), (far3,), "yes"),
-        ((1, 1), (far1,), "no"),
-        ((0, 1), (far,), "h"),
-        ((2, 0), near2, "x"),
-        ((2, 1), (far2,), "x"),
-    )
-    return product(plan, slices)
+    return product([own, near1, far1, near3, far3, far, *near2, far2], slices)
 
 
 def solution(mesh):

time: 161 us -> 154 us (0.957)
  starting transfers between devices: 66.6 us -> 61.3 us
    ppermute x24 -> x22, starting transfers between devices: 36.8 us -> 30.7 us  [ring(): lax.ppermute(a, axis, [(i, (i + step) % 4) for i in range(4)])]
    ppermute x15 -> x14, waiting for transfers between devices: 29.8 us -> 28.1 us  [swap(): return lambda a: lax.ppermute(a, axis, [(0, 1), (1, 0)])]
    ppermute x15 -> x14, starting transfers between devices: 29.8 us -> 30.7 us  [swap(): return lambda a: lax.ppermute(a, axis, [(0, 1), (1, 0)])]
    ppermute x24 -> x22, waiting for transfers between devices: 40.9 us -> 41.1 us  [ring(): lax.ppermute(a, axis, [(i, (i + step) % 4) for i in range(4)])]
  transfers between devices with their start and end apart: 39 -> 36, of which waited for: 19 -> 18; matrix products, arithmetic and copies ran while one was open for 0% -> 0% of each run, Pallas kernels for 1% -> 2%
where the time goes in v4:
time: 154 us; the launch traced here: 153 us
  waiting for transfers between devices  69.2 us (45%)
  starting transfers between devices  61.3 us (40%)
  Pallas kernels  19.1 us (12%)
  local copies, waits for them, and re-layouts  2.48 us (2%)
    ppermute x22, waiting for transfers between devices, ring(): lax.ppermute(a, axis, [(i, (i + step) % 4) for i in range(4)])  41.1 us
    ppermute x14, starting transfers between devices, swap(): return lambda a: lax.ppermute(a, axis, [(0, 1), (1, 0)])  30.7 us
    ppermute x22, starting transfers between devices, ring(): lax.ppermute(a, axis, [(i, (i + step) % 4) for i in range(4)])  30.7 us
    ppermute x14, waiting for transfers between devices, swap(): return lambda a: lax.ppermute(a, axis, [(0, 1), (1, 0)])  28.1 us
    pallas_call x1, Pallas kernels, product(): pl.pallas_call(product_kernel, out_shape=(jax.ShapeDtypeStruct((T, T), BF...  10.2 us
    pallas_call x3, Pallas kernels, gram(): pl.pallas_call(kernel, out_shape=(out, out), in_specs=[VMEM] * (len(tiles...  6.14 us
  transfers between devices with their start and end apart: 36, of which 18 were waited for; matrix products, arithmetic and copies ran while one was open for 0% of the time, Pallas kernels for 2%

profile of v4, /device:TPU:1, one launch (start us, length us, event | category | flops | bytes accessed | tf_op | source)
XLA Modules:
  0.0 153.3 jit_solution(12565557586394174949)
XLA Ops:
  4.5 2.1 %collective-permute-start.8 = (bf16[768,768]{1,0:T(8,128)(2,1)S(1)}, bf16[768,768]{1,0:T(8,128)(2,1)S(1)}, u32[]{:S(2)}, u32[]{:S(2)}) collective-permute-start(bf16[768,768]{1,0:T(8,128)(2,1)S(1)} %shard_map.41.own), channel_id=1, source_target_pairs={{0,4},{4,8},{8,12},{12,0},{1,5},{5,9},{9,13},{13,1},{2,6},{6,10},{... | collective-permute-start | bytes 3538952 | tf_op jit(solution)/shard_map/ppermute | solution.py:22
  8.0 3.0 %collective-permute-start.1 = (bf16[768,768]{1,0:T(8,128)(2,1)S(1)}, bf16[768,768]{1,0:T(8,128)(2,1)S(1)}, u32[]{:S(2)}, u32[]{:S(2)}) collective-permute-start(bf16[768,768]{1,0:T(8,128)(2,1)S(1)} %shard_map.41.own), channel_id=1, source_target_pairs={{0,2},{2,0},{1,3},{3,1},{4,6},{6,4},{5,7},{7,5},{8,10},{10,8},{9,1... | collective-permute-start | bytes 3538952 | tf_op jit(solution)/shard_map/ppermute | solution.py:26
  15.5 1.7 %collective-permute-start.3 = (bf16[48,768]{1,0:T(8,128)(2,1)S(1)}, bf16[48,768]{1,0:T(8,128)(2,1)S(1)}, u32[]{:S(2)}, u32[]{:S(2)}) collective-permute-start(bf16[48,768]{1,0:T(8,128)(2,1)S(1)} %get-tuple-element.20), channel_id=1, source_target_pairs={{0,16},{16,32},{32,48},{48,0},{1,17},{17,33},{33,49},{49,1},{2,18}... | collective-permute-start | bytes 221192 | tf_op jit(solution)/shard_map/ppermute | solution.py:22
  17.3 2.2 %collective-permute-start.4 = (bf16[48,768]{1,0:T(8,128)(2,1)S(1)}, bf16[48,768]{1,0:T(8,128)(2,1)S(1)}, u32[]{:S(2)}, u32[]{:S(2)}) collective-permute-start(bf16[48,768]{1,0:T(8,128)(2,1)S(1)} %get-tuple-element.21), channel_id=1, source_target_pairs={{0,48},{16,0},{32,16},{48,32},{1,49},{17,1},{33,17},{49,33},{2,50}... | collective-permute-start | bytes 221192 | tf_op jit(solution)/shard_map/ppermute | solution.py:22
  19.5 2.3 %collective-permute-done.3.from_down = bf16[48,768]{1,0:T(8,128)(2,1)S(1)} collective-permute-done((bf16[48,768]{1,0:T(8,128)(2,1)S(1)}, bf16[48,768]{1,0:T(8,128)(2,1)S(1)}, u32[]{:S(2)}, u32[]{:S(2)}) %collective-permute-start.3) | collective-permute-done | bytes 73760 | tf_op jit(solution)/shard_map/ppermute | solution.py:22
  22.6 2.0 %collective-permute-start.6 = (bf16[96,768]{1,0:T(8,128)(2,1)S(1)}, bf16[96,768]{1,0:T(8,128)(2,1)S(1)}, u32[]{:S(2)}, u32[]{:S(2)}) collective-permute-start(bf16[96,768]{1,0:T(8,128)(2,1)S(1)} %get-tuple-element.23), channel_id=1, source_target_pairs={{0,48},{16,0},{32,16},{48,32},{1,49},{17,1},{33,17},{49,33},{2,50}... | collective-permute-start | bytes 442376 | tf_op jit(solution)/shard_map/ppermute | solution.py:22
  24.6 3.0 %collective-permute-done.5.from_down = bf16[96,768]{1,0:T(8,128)(2,1)S(1)} collective-permute-done((bf16[96,768]{1,0:T(8,128)(2,1)S(1)}, bf16[96,768]{1,0:T(8,128)(2,1)S(1)}, u32[]{:S(2)}, u32[]{:S(2)}) %collective-permute-start.5) | collective-permute-done | bytes 147488 | tf_op jit(solution)/shard_map/ppermute | solution.py:22
  27.7 5.5 %collective-permute-done.8.src.near3 = bf16[768,768]{1,0:T(8,128)(2,1)S(1)} collective-permute-done((bf16[768,768]{1,0:T(8,128)(2,1)S(1)}, bf16[768,768]{1,0:T(8,128)(2,1)S(1)}, u32[]{:S(2)}, u32[]{:S(2)}) %collective-permute-start.8) | collective-permute-done | bytes 1179680 | tf_op jit(solution)/shard_map/ppermute | solution.py:22
  33.3 2.6 %collective-permute-done.1.far.src = bf16[768,768]{1,0:T(8,128)(2,1)S(1)} collective-permute-done((bf16[768,768]{1,0:T(8,128)(2,1)S(1)}, bf16[768,768]{1,0:T(8,128)(2,1)S(1)}, u32[]{:S(2)}, u32[]{:S(2)}) %collective-permute-start.1) | collective-permute-done | bytes 1179680 | tf_op jit(solution)/shard_map/ppermute | solution.py:26
  35.8 3.0 %shard_map.48 = (bf16[4,240,768]{2,1,0:T(8,128)(2,1)S(1)}, bf16[4,240,768]{2,1,0:T(8,128)(2,1)S(1)}) custom-call(bf16[768,768]{1,0:T(8,128)(2,1)S(1)} %shard_map.41.own, bf16[768,768]{1,0:T(8,128)(2,1)S(1)} %collective-permute-done.src.near1, bf16[768,768]{1,0:T(8,128)(2,1)S(1)} %collective-permute-done.1.far.src, bf16[96,768]{1,0:T(8,128)(2,1)S(1)} %shard_map.45.refs_0_._, ...), custom_call_target="tpu_custom_call" | custom-call | flops 2264924160 | bytes 3538944 | tf_op jit(solution)/shard_map/pallas_call | solution.py:128
  38.8 2.2 %collective-permute-start.9 = (bf16[4,240,768]{2,1,0:T(8,128)(2,1)S(1)}, bf16[4,240,768]{2,1,0:T(8,128)(2,1)S(1)}, u32[]{:S(2)}, u32[]{:S(2)}) collective-permute-start(bf16[4,240,768]{2,1,0:T(8,128)(2,1)S(1)} %get-tuple-element.25), channel_id=1, source_target_pairs={{0,1},{1,0},{2,3},{3,2},{4,5},{5,4},{6,7},{7,6},{8,9},{9,8},{10,11... | collective-permute-start | bytes 4423688 | tf_op jit(solution)/shard_map/ppermute | solution.py:26
  41.1 2.6 %collective-permute-start.15 = (bf16[384,768]{1,0:T(8,128)(2,1)S(1)}, bf16[384,768]{1,0:T(8,128)(2,1)S(1)}, u32[]{:S(2)}, u32[]{:S(2)}) collective-permute-start(bf16[384,768]{1,0:T(8,128)(2,1)S(1)} %shard_map.46.__), channel_id=1, source_target_pairs={{0,12},{4,0},{8,4},{12,8},{1,13},{5,1},{9,5},{13,9},{2,14},{6,2},{... | collective-permute-start | bytes 1769480 | tf_op jit(solution)/shard_map/ppermute | solution.py:22
  44.2 1.8 %collective-permute-start.10 = (bf16[240,768]{1,0:T(8,128)(2,1)S(1)}, bf16[240,768]{1,0:T(8,128)(2,1)S(1)}, u32[]{:S(2)}, u32[]{:S(2)}) collective-permute-start(bf16[240,768]{1,0:T(8,128)(2,1)S(1)} %get-tuple-element.26), channel_id=1, source_target_pairs={{0,16},{16,32},{32,48},{48,0},{1,17},{17,33},{33,49},{49,1},{2,18}... | collective-permute-start | bytes 1105928 | tf_op jit(solution)/shard_map/ppermute | solution.py:22
  45.9 2.2 %collective-permute-start.11 = (bf16[240,768]{1,0:T(8,128)(2,1)S(1)}, bf16[240,768]{1,0:T(8,128)(2,1)S(1)}, u32[]{:S(2)}, u32[]{:S(2)}) collective-permute-start(bf16[240,768]{1,0:T(8,128)(2,1)S(1)} %get-tuple-element.27), channel_id=1, source_target_pairs={{0,48},{16,0},{32,16},{48,32},{1,49},{17,1},{33,17},{49,33},{2,50}... | collective-permute-start | bytes 1105928 | tf_op jit(solution)/shard_map/ppermute | solution.py:22
  49.3 7.3 %collective-permute-done.10.one = bf16[240,768]{1,0:T(8,128)(2,1)S(1)} collective-permute-done((bf16[240,768]{1,0:T(8,128)(2,1)S(1)}, bf16[240,768]{1,0:T(8,128)(2,1)S(1)}, u32[]{:S(2)}, u32[]{:S(2)}) %collective-permute-start.10) | collective-permute-done | bytes 368672 | tf_op jit(solution)/shard_map/ppermute | solution.py:22
  56.6 8.8 %collective-permute-done.12.two = bf16[240,768]{1,0:T(8,128)(2,1)S(1)} collective-permute-done((bf16[240,768]{1,0:T(8,128)(2,1)S(1)}, bf16[240,768]{1,0:T(8,128)(2,1)S(1)}, u32[]{:S(2)}, u32[]{:S(2)}) %collective-permute-start.12) | collective-permute-done | bytes 368672 | tf_op jit(solution)/shard_map/ppermute | solution.py:22
  65.6 1.9 %shard_map.51 = (bf16[4,96,768]{2,1,0:T(8,128)(2,1)S(1)}, bf16[4,96,768]{2,1,0:T(8,128)(2,1)S(1)}) custom-call(bf16[768,768]{1,0:T(8,128)(2,1)S(1)} %shard_map.41.own, bf16[768,768]{1,0:T(8,128)(2,1)S(1)} %collective-permute-done.1.far.src, bf16[384,768]{1,0:T(8,128)(2,1)S(1)} %collective-permute-done.15.near2a.top, ...), custom_call_target="tpu_custom_call" | custom-call | flops 905969664 | bytes 3538944 | tf_op jit(solution)/shard_map/pallas_call | solution.py:128
  71.6 1.8 %collective-permute-start.19 = (bf16[96,768]{1,0:T(8,128)(2,1)S(1)}, bf16[96,768]{1,0:T(8,128)(2,1)S(1)}, u32[]{:S(2)}, u32[]{:S(2)}) collective-permute-start(bf16[96,768]{1,0:T(8,128)(2,1)S(1)} %get-tuple-element.32), channel_id=1, source_target_pairs={{0,48},{16,0},{32,16},{48,32},{1,49},{17,1},{33,17},{49,33},{2,50}... | collective-permute-start | bytes 442376 | tf_op jit(solution)/shard_map/ppermute | solution.py:22
  74.8 2.2 %collective-permute-done.18.one = bf16[96,768]{1,0:T(8,128)(2,1)S(1)} collective-permute-done((bf16[96,768]{1,0:T(8,128)(2,1)S(1)}, bf16[96,768]{1,0:T(8,128)(2,1)S(1)}, u32[]{:S(2)}, u32[]{:S(2)}) %collective-permute-start.18) | collective-permute-done | bytes 147488 | tf_op jit(solution)/shard_map/ppermute | solution.py:22
  77.0 2.9 %collective-permute-done.20.two = bf16[96,768]{1,0:T(8,128)(2,1)S(1)} collective-permute-done((bf16[96,768]{1,0:T(8,128)(2,1)S(1)}, bf16[96,768]{1,0:T(8,128)(2,1)S(1)}, u32[]{:S(2)}, u32[]{:S(2)}) %collective-permute-start.20) | collective-permute-done | bytes 147488 | tf_op jit(solution)/shard_map/ppermute | solution.py:22
  81.6 2.5 %collective-permute-done.21 = bf16[96,768]{1,0:T(8,128)(2,1)S(1)} collective-permute-done((bf16[96,768]{1,0:T(8,128)(2,1)S(1)}, bf16[96,768]{1,0:T(8,128)(2,1)S(1)}, u32[]{:S(2)}, u32[]{:S(2)}) %collective-permute-start.21) | collective-permute-done | bytes 147488 | tf_op jit(solution)/shard_map/ppermute | solution.py:26
  84.1 3.0 %collective-permute-start.23 = (bf16[192,768]{1,0:T(8,128)(2,1)S(1)}, bf16[192,768]{1,0:T(8,128)(2,1)S(1)}, u32[]{:S(2)}, u32[]{:S(2)}) collective-permute-start(bf16[192,768]{1,0:T(8,128)(2,1)S(1)} %shard_map.54), channel_id=1, source_target_pairs={{0,2},{2,0},{1,3},{3,1},{4,6},{6,4},{5,7},{7,5},{8,10},{10,8},{9,1... | collective-permute-start | bytes 884744 | tf_op jit(solution)/shard_map/ppermute | solution.py:26
  89.4 3.8 %collective-permute-done.22.from_x2 = bf16[96,768]{1,0:T(8,128)(2,1)S(1)} collective-permute-done((bf16[96,768]{1,0:T(8,128)(2,1)S(1)}, bf16[96,768]{1,0:T(8,128)(2,1)S(1)}, u32[]{:S(2)}, u32[]{:S(2)}) %collective-permute-start.22) | collective-permute-done | bytes 147488 | tf_op jit(solution)/shard_map/ppermute | solution.py:22
  95.1 2.7 %collective-permute-start.24 = (bf16[768,768]{1,0:T(8,128)(2,1)S(1)}, bf16[768,768]{1,0:T(8,128)(2,1)S(1)}, u32[]{:S(2)}, u32[]{:S(2)}) collective-permute-start(bf16[768,768]{1,0:T(8,128)(2,1)S(1)} %shard_map.56), channel_id=1, source_target_pairs={{0,12},{4,0},{8,4},{12,8},{1,13},{5,1},{9,5},{13,9},{2,14},{6,2},{... | collective-permute-start | bytes 3538952 | tf_op jit(solution)/shard_map/ppermute | solution.py:22
  98.7 1.7 %collective-permute-start.27 = (bf16[16,48,768]{2,1,0:T(8,128)(2,1)S(1)}, bf16[16,48,768]{2,1,0:T(8,128)(2,1)S(1)}, u32[]{:S(2)}, u32[]{:S(2)}) collective-permute-start(bf16[16,48,768]{2,1,0:T(8,128)(2,1)S(1)} %bitcast.2), channel_id=1, source_target_pairs={{0,48},{16,0},{32,16},{48,32},{1,49},{17,1},{33,17},{49,33},{2,50}... | collective-permute-start | bytes 3538952 | tf_op jit(solution)/shard_map/ppermute | solution.py:22
  100.5 18.4 %collective-permute-done.26.refs_1_.far2 = bf16[768,768]{1,0:T(8,128)(2,1)S(1)} collective-permute-done((bf16[768,768]{1,0:T(8,128)(2,1)S(1)}, bf16[768,768]{1,0:T(8,128)(2,1)S(1)}, u32[]{:S(2)}, u32[]{:S(2)}) %collective-permute-start.26) | collective-permute-done | bytes 1179680 | tf_op jit(solution)/shard_map/ppermute | solution.py:26
  118.9 4.5 %collective-permute-start.31 = (bf16[16,48,768]{2,1,0:T(8,128)(2,1)S(1)}, bf16[16,48,768]{2,1,0:T(8,128)(2,1)S(1)}, u32[]{:S(2)}, u32[]{:S(2)}) collective-permute-start(bf16[16,48,768]{2,1,0:T(8,128)(2,1)S(1)} %bitcast.3), channel_id=1, source_target_pairs={{0,1},{1,0},{2,3},{3,2},{4,5},{5,4},{6,7},{7,6},{8,9},{9,8},{10,11... | collective-permute-start | bytes 3538952 | tf_op jit(solution)/shard_map/ppermute | solution.py:26
  124.5 1.8 %collective-permute-start.29 = (bf16[8,48,768]{2,1,0:T(8,128)(2,1)S(1)}, bf16[8,48,768]{2,1,0:T(8,128)(2,1)S(1)}, u32[]{:S(2)}, u32[]{:S(2)}) collective-permute-start(bf16[8,48,768]{2,1,0:T(8,128)(2,1)S(1)} %shard_map.58), channel_id=1, source_target_pairs={{0,48},{16,0},{32,16},{48,32},{1,49},{17,1},{33,17},{49,33},{2,50}... | collective-permute-start | bytes 1769480 | tf_op jit(solution)/shard_map/ppermute | solution.py:22
  126.3 4.6 %collective-permute-start.33 = (bf16[16,48,768]{2,1,0:T(8,128)(2,1)S(1)}, bf16[16,48,768]{2,1,0:T(8,128)(2,1)S(1)}, u32[]{:S(2)}, u32[]{:S(2)}) collective-permute-start(bf16[16,48,768]{2,1,0:T(8,128)(2,1)S(1)} %collective-permute-done.28.src.refs_2_), channel_id=1, source_target_pairs={{0,1},{1,0},{2,3},{3,2},{4,5},{5,4},{6,7},{7,6},{8,9},{9,8},{10,11... | collective-permute-start | bytes 3538952 | tf_op jit(solution)/shard_map/ppermute | solution.py:26
  130.8 4.7 %collective-permute-done.30.refs_4_ = bf16[8,48,768]{2,1,0:T(8,128)(2,1)S(1)} collective-permute-done((bf16[8,48,768]{2,1,0:T(8,128)(2,1)S(1)}, bf16[8,48,768]{2,1,0:T(8,128)(2,1)S(1)}, u32[]{:S(2)}, u32[]{:S(2)}) %collective-permute-start.30) | collective-permute-done | bytes 589856 | tf_op jit(solution)/shard_map/ppermute | solution.py:22
  135.5 4.9 %collective-permute-start.35 = (bf16[8,48,768]{2,1,0:T(8,128)(2,1)S(1)}, bf16[8,48,768]{2,1,0:T(8,128)(2,1)S(1)}, u32[]{:S(2)}, u32[]{:S(2)}) collective-permute-start(bf16[8,48,768]{2,1,0:T(8,128)(2,1)S(1)} %collective-permute-done.30.refs_4_), channel_id=1, source_target_pairs={{0,1},{1,0},{2,3},{3,2},{4,5},{5,4},{6,7},{7,6},{8,9},{9,8},{10,11... | collective-permute-start | bytes 1769480 | tf_op jit(solution)/shard_map/ppermute | solution.py:26
  142.9 10.2 %shard_map.60 = (bf16[768,768]{1,0:T(8,128)(2,1)}, bf16[384,768]{1,0:T(8,128)(2,1)}) custom-call(bf16[768,768]{1,0:T(8,128)(2,1)S(1)} %shard_map.41.own, bf16[768,768]{1,0:T(8,128)(2,1)S(1)} %collective-permute-done.src.near1, bf16[768,768]{1,0:T(8,128)(2,1)S(1)} %collective-permute-done.24.refs_0_.far1, ...), custom_call_target="tpu_custom_call" | custom-call | flops 7247757312 | bytes 21233664 | tf_op jit(solution)/shard_map/pallas_call | solution.py:316
  (68 shorter events, 28.6 us)
Async XLA Ops:
  4.5 28.6 %collective-permute-start.8 = (bf16[768,768]{1,0:T(8,128)(2,1)S(1)}, bf16[768,768]{1,0:T(8,128)(2,1)S(1)}, u32[]{:S(2)}, u32[]{:S(2)}) collective-permute-start(bf16[768,768]{1,0:T(8,128)(2,1)S(1)} %shard_map.41.own), channel_id=1, source_target_pairs={{0,4},{4,8},{8,12},{12,0},{1,5},{5,9},{9,13},{13,1},{2,6},{6,10},{... | collective-permute-start | bytes 3538952 | tf_op jit(solution)/shard_map/ppermute | solution.py:22
  6.7 26.6 %collective-permute-start = (bf16[768,768]{1,0:T(8,128)(2,1)S(1)}, bf16[768,768]{1,0:T(8,128)(2,1)S(1)}, u32[]{:S(2)}, u32[]{:S(2)}) collective-permute-start(bf16[768,768]{1,0:T(8,128)(2,1)S(1)} %shard_map.41.own), channel_id=1, source_target_pairs={{0,12},{4,0},{8,4},{12,8},{1,13},{5,1},{9,5},{13,9},{2,14},{6,2},{... | collective-permute-start | bytes 3538952 | tf_op jit(solution)/shard_map/ppermute | solution.py:22
  8.0 27.8 %collective-permute-start.1 = (bf16[768,768]{1,0:T(8,128)(2,1)S(1)}, bf16[768,768]{1,0:T(8,128)(2,1)S(1)}, u32[]{:S(2)}, u32[]{:S(2)}) collective-permute-start(bf16[768,768]{1,0:T(8,128)(2,1)S(1)} %shard_map.41.own), channel_id=1, source_target_pairs={{0,2},{2,0},{1,3},{3,1},{4,6},{6,4},{5,7},{7,5},{8,10},{10,8},{9,1... | collective-permute-start | bytes 3538952 | tf_op jit(solution)/shard_map/ppermute | solution.py:26
  15.5 6.2 %collective-permute-start.3 = (bf16[48,768]{1,0:T(8,128)(2,1)S(1)}, bf16[48,768]{1,0:T(8,128)(2,1)S(1)}, u32[]{:S(2)}, u32[]{:S(2)}) collective-permute-start(bf16[48,768]{1,0:T(8,128)(2,1)S(1)} %get-tuple-element.20), channel_id=1, source_target_pairs={{0,16},{16,32},{32,48},{48,0},{1,17},{17,33},{33,49},{49,1},{2,18}... | collective-permute-start | bytes 221192 | tf_op jit(solution)/shard_map/ppermute | solution.py:22
  17.3 4.5 %collective-permute-start.4 = (bf16[48,768]{1,0:T(8,128)(2,1)S(1)}, bf16[48,768]{1,0:T(8,128)(2,1)S(1)}, u32[]{:S(2)}, u32[]{:S(2)}) collective-permute-start(bf16[48,768]{1,0:T(8,128)(2,1)S(1)} %get-tuple-element.21), channel_id=1, source_target_pairs={{0,48},{16,0},{32,16},{48,32},{1,49},{17,1},{33,17},{49,33},{2,50}... | collective-permute-start | bytes 221192 | tf_op jit(solution)/shard_map/ppermute | solution.py:22
  21.8 5.8 %collective-permute-start.5 = (bf16[96,768]{1,0:T(8,128)(2,1)S(1)}, bf16[96,768]{1,0:T(8,128)(2,1)S(1)}, u32[]{:S(2)}, u32[]{:S(2)}) collective-permute-start(bf16[96,768]{1,0:T(8,128)(2,1)S(1)} %get-tuple-element.22), channel_id=1, source_target_pairs={{0,16},{16,32},{32,48},{48,0},{1,17},{17,33},{33,49},{49,1},{2,18}... | collective-permute-start | bytes 442376 | tf_op jit(solution)/shard_map/ppermute | solution.py:22
  22.6 5.0 %collective-permute-start.6 = (bf16[96,768]{1,0:T(8,128)(2,1)S(1)}, bf16[96,768]{1,0:T(8,128)(2,1)S(1)}, u32[]{:S(2)}, u32[]{:S(2)}) collective-permute-start(bf16[96,768]{1,0:T(8,128)(2,1)S(1)} %get-tuple-element.23), channel_id=1, source_target_pairs={{0,48},{16,0},{32,16},{48,32},{1,49},{17,1},{33,17},{49,33},{2,50}... | collective-permute-start | bytes 442376 | tf_op jit(solution)/shard_map/ppermute | solution.py:22
  38.8 5.1 %collective-permute-start.9 = (bf16[4,240,768]{2,1,0:T(8,128)(2,1)S(1)}, bf16[4,240,768]{2,1,0:T(8,128)(2,1)S(1)}, u32[]{:S(2)}, u32[]{:S(2)}) collective-permute-start(bf16[4,240,768]{2,1,0:T(8,128)(2,1)S(1)} %get-tuple-element.25), channel_id=1, source_target_pairs={{0,1},{1,0},{2,3},{3,2},{4,5},{5,4},{6,7},{7,6},{8,9},{9,8},{10,11... | collective-permute-start | bytes 4423688 | tf_op jit(solution)/shard_map/ppermute | solution.py:26
  41.0 24.6 %collective-permute-start.16 = (bf16[384,768]{1,0:T(8,128)(2,1)S(1)}, bf16[384,768]{1,0:T(8,128)(2,1)S(1)}, u32[]{:S(2)}, u32[]{:S(2)}) collective-permute-start(bf16[384,768]{1,0:T(8,128)(2,1)S(1)} %shard_map.47.___), channel_id=1, source_target_pairs={{0,4},{4,8},{8,12},{12,0},{1,5},{5,9},{9,13},{13,1},{2,6},{6,10},{... | collective-permute-start | bytes 1769480 | tf_op jit(solution)/shard_map/ppermute | solution.py:22
  41.1 24.6 %collective-permute-start.15 = (bf16[384,768]{1,0:T(8,128)(2,1)S(1)}, bf16[384,768]{1,0:T(8,128)(2,1)S(1)}, u32[]{:S(2)}, u32[]{:S(2)}) collective-permute-start(bf16[384,768]{1,0:T(8,128)(2,1)S(1)} %shard_map.46.__), channel_id=1, source_target_pairs={{0,12},{4,0},{8,4},{12,8},{1,13},{5,1},{9,5},{13,9},{2,14},{6,2},{... | collective-permute-start | bytes 1769480 | tf_op jit(solution)/shard_map/ppermute | solution.py:22
  44.2 12.5 %collective-permute-start.10 = (bf16[240,768]{1,0:T(8,128)(2,1)S(1)}, bf16[240,768]{1,0:T(8,128)(2,1)S(1)}, u32[]{:S(2)}, u32[]{:S(2)}) collective-permute-start(bf16[240,768]{1,0:T(8,128)(2,1)S(1)} %get-tuple-element.26), channel_id=1, source_target_pairs={{0,16},{16,32},{32,48},{48,0},{1,17},{17,33},{33,49},{49,1},{2,18}... | collective-permute-start | bytes 1105928 | tf_op jit(solution)/shard_map/ppermute | solution.py:22
  45.9 10.7 %collective-permute-start.11 = (bf16[240,768]{1,0:T(8,128)(2,1)S(1)}, bf16[240,768]{1,0:T(8,128)(2,1)S(1)}, u32[]{:S(2)}, u32[]{:S(2)}) collective-permute-start(bf16[240,768]{1,0:T(8,128)(2,1)S(1)} %get-tuple-element.27), channel_id=1, source_target_pairs={{0,48},{16,0},{32,16},{48,32},{1,49},{17,1},{33,17},{49,33},{2,50}... | collective-permute-start | bytes 1105928 | tf_op jit(solution)/shard_map/ppermute | solution.py:22
  48.1 17.3 %collective-permute-start.12 = (bf16[240,768]{1,0:T(8,128)(2,1)S(1)}, bf16[240,768]{1,0:T(8,128)(2,1)S(1)}, u32[]{:S(2)}, u32[]{:S(2)}) collective-permute-start(bf16[240,768]{1,0:T(8,128)(2,1)S(1)} %get-tuple-element.28), channel_id=1, source_target_pairs={{0,32},{16,48},{32,0},{48,16},{1,33},{17,49},{33,1},{49,17},{2,34}... | collective-permute-start | bytes 1105928 | tf_op jit(solution)/shard_map/ppermute | solution.py:22
  68.9 12.4 %collective-permute-start.13 = (bf16[240,768]{1,0:T(8,128)(2,1)S(1)}, bf16[240,768]{1,0:T(8,128)(2,1)S(1)}, u32[]{:S(2)}, u32[]{:S(2)}) collective-permute-start(bf16[240,768]{1,0:T(8,128)(2,1)S(1)} %shard_map.50._), channel_id=1, source_target_pairs={{0,64},{64,0},{1,65},{65,1},{2,66},{66,2},{3,67},{67,3},{4,68},{68... | collective-permute-start | bytes 1105928 | tf_op jit(solution)/shard_map/ppermute | solution.py:26
  70.7 6.3 %collective-permute-start.18 = (bf16[96,768]{1,0:T(8,128)(2,1)S(1)}, bf16[96,768]{1,0:T(8,128)(2,1)S(1)}, u32[]{:S(2)}, u32[]{:S(2)}) collective-permute-start(bf16[96,768]{1,0:T(8,128)(2,1)S(1)} %get-tuple-element.31), channel_id=1, source_target_pairs={{0,16},{16,32},{32,48},{48,0},{1,17},{17,33},{33,49},{49,1},{2,18}... | collective-permute-start | bytes 442376 | tf_op jit(solution)/shard_map/ppermute | solution.py:22
  71.6 5.4 %collective-permute-start.19 = (bf16[96,768]{1,0:T(8,128)(2,1)S(1)}, bf16[96,768]{1,0:T(8,128)(2,1)S(1)}, u32[]{:S(2)}, u32[]{:S(2)}) collective-permute-start(bf16[96,768]{1,0:T(8,128)(2,1)S(1)} %get-tuple-element.32), channel_id=1, source_target_pairs={{0,48},{16,0},{32,16},{48,32},{1,49},{17,1},{33,17},{49,33},{2,50}... | collective-permute-start | bytes 442376 | tf_op jit(solution)/shard_map/ppermute | solution.py:22
  73.4 6.5 %collective-permute-start.20 = (bf16[96,768]{1,0:T(8,128)(2,1)S(1)}, bf16[96,768]{1,0:T(8,128)(2,1)S(1)}, u32[]{:S(2)}, u32[]{:S(2)}) collective-permute-start(bf16[96,768]{1,0:T(8,128)(2,1)S(1)} %get-tuple-element.33), channel_id=1, source_target_pairs={{0,32},{16,48},{32,0},{48,16},{1,33},{17,49},{33,1},{49,17},{2,34}... | collective-permute-start | bytes 442376 | tf_op jit(solution)/shard_map/ppermute | solution.py:22
  73.5 15.2 %collective-permute-start.7 = (bf16[96,768]{1,0:T(8,128)(2,1)S(1)}, bf16[96,768]{1,0:T(8,128)(2,1)S(1)}, u32[]{:S(2)}, u32[]{:S(2)}) collective-permute-start(bf16[96,768]{1,0:T(8,128)(2,1)S(1)} %shard_map.45.refs_0_._), channel_id=1, source_target_pairs={{0,64},{64,0},{1,65},{65,1},{2,66},{66,2},{3,67},{67,3},{4,68},{68... | collective-permute-start | bytes 442376 | tf_op jit(solution)/shard_map/ppermute | solution.py:26
  81.5 7.9 %collective-permute-start.14 = (bf16[192,768]{1,0:T(8,128)(2,1)S(1)}, bf16[192,768]{1,0:T(8,128)(2,1)S(1)}, u32[]{:S(2)}, u32[]{:S(2)}) collective-permute-start(bf16[192,768]{1,0:T(8,128)(2,1)S(1)} %slice.4), channel_id=1, source_target_pairs={{0,4},{4,8},{8,12},{12,0},{1,5},{5,9},{9,13},{13,1},{2,6},{6,10},{... | collective-permute-start | bytes 884744 | tf_op jit(solution)/shard_map/ppermute | solution.py:22
  84.1 9.1 %collective-permute-start.23 = (bf16[192,768]{1,0:T(8,128)(2,1)S(1)}, bf16[192,768]{1,0:T(8,128)(2,1)S(1)}, u32[]{:S(2)}, u32[]{:S(2)}) collective-permute-start(bf16[192,768]{1,0:T(8,128)(2,1)S(1)} %shard_map.54), channel_id=1, source_target_pairs={{0,2},{2,0},{1,3},{3,1},{4,6},{6,4},{5,7},{7,5},{8,10},{10,8},{9,1... | collective-permute-start | bytes 884744 | tf_op jit(solution)/shard_map/ppermute | solution.py:26
  87.1 6.1 %collective-permute-start.22 = (bf16[96,768]{1,0:T(8,128)(2,1)S(1)}, bf16[96,768]{1,0:T(8,128)(2,1)S(1)}, u32[]{:S(2)}, u32[]{:S(2)}) collective-permute-start(bf16[96,768]{1,0:T(8,128)(2,1)S(1)} %multiply_convert_fusion.1.second.shard2), channel_id=1, source_target_pairs={{0,8},{4,12},{8,0},{12,4},{1,9},{5,13},{9,1},{13,5},{2,10},{6,14},... | collective-permute-start | bytes 442376 | tf_op jit(solution)/shard_map/ppermute | solution.py:22
  93.4 25.5 %collective-permute-start.26 = (bf16[768,768]{1,0:T(8,128)(2,1)S(1)}, bf16[768,768]{1,0:T(8,128)(2,1)S(1)}, u32[]{:S(2)}, u32[]{:S(2)}) collective-permute-start(bf16[768,768]{1,0:T(8,128)(2,1)S(1)} %shard_map.57), channel_id=1, source_target_pairs={{0,2},{2,0},{1,3},{3,1},{4,6},{6,4},{5,7},{7,5},{8,10},{10,8},{9,1... | collective-permute-start | bytes 3538952 | tf_op jit(solution)/shard_map/ppermute | solution.py:26
  95.0 28.3 %collective-permute-start.25 = (bf16[768,768]{1,0:T(8,128)(2,1)S(1)}, bf16[768,768]{1,0:T(8,128)(2,1)S(1)}, u32[]{:S(2)}, u32[]{:S(2)}) collective-permute-start(bf16[768,768]{1,0:T(8,128)(2,1)S(1)} %shard_map.56), channel_id=1, source_target_pairs={{0,4},{4,8},{8,12},{12,0},{1,5},{5,9},{9,13},{13,1},{2,6},{6,10},{... | collective-permute-start | bytes 3538952 | tf_op jit(solution)/shard_map/ppermute | solution.py:22
  95.1 28.2 %collective-permute-start.24 = (bf16[768,768]{1,0:T(8,128)(2,1)S(1)}, bf16[768,768]{1,0:T(8,128)(2,1)S(1)}, u32[]{:S(2)}, u32[]{:S(2)}) collective-permute-start(bf16[768,768]{1,0:T(8,128)(2,1)S(1)} %shard_map.56), channel_id=1, source_target_pairs={{0,12},{4,0},{8,4},{12,8},{1,13},{5,1},{9,5},{13,9},{2,14},{6,2},{... | collective-permute-start | bytes 3538952 | tf_op jit(solution)/shard_map/ppermute | solution.py:22
  97.8 25.6 %collective-permute-start.28 = (bf16[16,48,768]{2,1,0:T(8,128)(2,1)S(1)}, bf16[16,48,768]{2,1,0:T(8,128)(2,1)S(1)}, u32[]{:S(2)}, u32[]{:S(2)}) collective-permute-start(bf16[16,48,768]{2,1,0:T(8,128)(2,1)S(1)} %bitcast.1), channel_id=1, source_target_pairs={{0,16},{16,32},{32,48},{48,0},{1,17},{17,33},{33,49},{49,1},{2,18}... | collective-permute-start | bytes 3538952 | tf_op jit(solution)/shard_map/ppermute | solution.py:22
  98.7 25.7 %collective-permute-start.27 = (bf16[16,48,768]{2,1,0:T(8,128)(2,1)S(1)}, bf16[16,48,768]{2,1,0:T(8,128)(2,1)S(1)}, u32[]{:S(2)}, u32[]{:S(2)}) collective-permute-start(bf16[16,48,768]{2,1,0:T(8,128)(2,1)S(1)} %bitcast.2), channel_id=1, source_target_pairs={{0,48},{16,0},{32,16},{48,32},{1,49},{17,1},{33,17},{49,33},{2,50}... | collective-permute-start | bytes 3538952 | tf_op jit(solution)/shard_map/ppermute | solution.py:22
  118.9 21.6 %collective-permute-start.31 = (bf16[16,48,768]{2,1,0:T(8,128)(2,1)S(1)}, bf16[16,48,768]{2,1,0:T(8,128)(2,1)S(1)}, u32[]{:S(2)}, u32[]{:S(2)}) collective-permute-start(bf16[16,48,768]{2,1,0:T(8,128)(2,1)S(1)} %bitcast.3), channel_id=1, source_target_pairs={{0,1},{1,0},{2,3},{3,2},{4,5},{5,4},{6,7},{7,6},{8,9},{9,8},{10,11... | collective-permute-start | bytes 3538952 | tf_op jit(solution)/shard_map/ppermute | solution.py:26
  123.4 12.1 %collective-permute-start.30 = (bf16[8,48,768]{2,1,0:T(8,128)(2,1)S(1)}, bf16[8,48,768]{2,1,0:T(8,128)(2,1)S(1)}, u32[]{:S(2)}, u32[]{:S(2)}) collective-permute-start(bf16[8,48,768]{2,1,0:T(8,128)(2,1)S(1)} %shard_map.59), channel_id=1, source_target_pairs={{0,16},{16,32},{32,48},{48,0},{1,17},{17,33},{33,49},{49,1},{2,18}... | collective-permute-start | bytes 1769480 | tf_op jit(solution)/shard_map/ppermute | solution.py:22
  124.5 16.0 %collective-permute-start.29 = (bf16[8,48,768]{2,1,0:T(8,128)(2,1)S(1)}, bf16[8,48,768]{2,1,0:T(8,128)(2,1)S(1)}, u32[]{:S(2)}, u32[]{:S(2)}) collective-permute-start(bf16[8,48,768]{2,1,0:T(8,128)(2,1)S(1)} %shard_map.58), channel_id=1, source_target_pairs={{0,48},{16,0},{32,16},{48,32},{1,49},{17,1},{33,17},{49,33},{2,50}... | collective-permute-start | bytes 1769480 | tf_op jit(solution)/shard_map/ppermute | solution.py:22
  126.3 15.8 %collective-permute-start.33 = (bf16[16,48,768]{2,1,0:T(8,128)(2,1)S(1)}, bf16[16,48,768]{2,1,0:T(8,128)(2,1)S(1)}, u32[]{:S(2)}, u32[]{:S(2)}) collective-permute-start(bf16[16,48,768]{2,1,0:T(8,128)(2,1)S(1)} %collective-permute-done.28.src.refs_2_), channel_id=1, source_target_pairs={{0,1},{1,0},{2,3},{3,2},{4,5},{5,4},{6,7},{7,6},{8,9},{9,8},{10,11... | collective-permute-start | bytes 3538952 | tf_op jit(solution)/shard_map/ppermute | solution.py:26
  130.8 12.1 %collective-permute-start.32 = (bf16[16,48,768]{2,1,0:T(8,128)(2,1)S(1)}, bf16[16,48,768]{2,1,0:T(8,128)(2,1)S(1)}, u32[]{:S(2)}, u32[]{:S(2)}) collective-permute-start(bf16[16,48,768]{2,1,0:T(8,128)(2,1)S(1)} %collective-permute-done.27.src.refs_1_), channel_id=1, source_target_pairs={{0,1},{1,0},{2,3},{3,2},{4,5},{5,4},{6,7},{7,6},{8,9},{9,8},{10,11... | collective-permute-start | bytes 3538952 | tf_op jit(solution)/shard_map/ppermute | solution.py:26
  135.5 6.6 %collective-permute-start.35 = (bf16[8,48,768]{2,1,0:T(8,128)(2,1)S(1)}, bf16[8,48,768]{2,1,0:T(8,128)(2,1)S(1)}, u32[]{:S(2)}, u32[]{:S(2)}) collective-permute-start(bf16[8,48,768]{2,1,0:T(8,128)(2,1)S(1)} %collective-permute-done.30.refs_4_), channel_id=1, source_target_pairs={{0,1},{1,0},{2,3},{3,2},{4,5},{5,4},{6,7},{7,6},{8,9},{9,8},{10,11... | collective-permute-start | bytes 1769480 | tf_op jit(solution)/shard_map/ppermute | solution.py:26
  (6 other events, 15.2 us)

commit v5 on v4

--- a/solution.py
+++ b/solution.py
@@ -16,6 +16,7 @@
 A = H
 S = 48
 VMEM = pl.BlockSpec(memory_space=pltpu.VMEM)
+ANY = pl.BlockSpec(memory_space=pl.ANY)
 
 
 def ring(axis, step):
@@ -247,7 +248,7 @@
 
 def product_kernel(own, near1, far1, near3, far3, far, near2a, near2b, far2, *refs):
     x, h, z, k = (lax.axis_index(axis) for axis in ("x", "yh", "z", "core"))
-    slices, (out, gram_out, g, g_sem, acc) = refs[:10], refs[10:]
+    slices, (out_far, gram_far, g, g_sem, acc, out, gram_out, sems) = refs[:10], refs[10:]
 
     g_copies = []
     for c in range(2):
@@ -271,6 +272,29 @@
         pl.when(jnp.logical_not(turned))(straight_way)
         pl.when(turned)(turned_way)
 
+    line = lax.axis_index("yl") * 4 + z
+    dx, dh = lax.rem(line // 2 - x + 4, 4), lax.rem(line + h, 2)
+    for t, ((ax, ah), turn) in enumerate(TILES):
+        mine, turned = (dx == ax) & (dh == ah), {"no": z < 0, "yes": z >= 0, "h": h != 0, "x": x >= 2}[turn]
+        if turn != "yes":
+
+            @pl.when(mine & jnp.logical_not(turned))
+            def _():
+                gram_out[...] = g[2 * t + k]
+
+        if turn != "no":
+            for side in range(2):
+
+                @pl.when(mine & turned & (k == side))
+                def _():
+                    gram_out[...] = g[2 * t : 2 * t + 2, :, side * H : (side + 1) * H].reshape(T, H).T
+
+    copies = [pltpu.make_async_copy(gram_out, gram_far, sems.at[2])]
+    for i in range(2):
+        rows = pl.ds(i * H, H)
+        copies.append(pltpu.make_async_copy(out.at[rows], out_far.at[rows], sems.at[i]))
+    copies[0].start()
+
     def far_straight():
         acc[...] = dot(far[...], tiles(5, 1))
 
@@ -286,29 +310,15 @@
             rows = slice(i * H, (i + 1) * H)
             total = acc[rows, :] + multiply(beside([near2[...], far2[rows, :]]), factor)
             out[rows, :] = (1.5 * own[rows, :].astype(F32) - 0.5 * total).astype(BF16)
+            copies[1 + i].start()
 
     either(
         x >= 2,
         lambda: finish(dot, tiles(6, 2)),
         lambda: finish(dot_t, beside([tiles(6, 1), tiles(7, 1)])),
     )
-
-    line = lax.axis_index("yl") * 4 + z
-    dx, dh = lax.rem(line // 2 - x + 4, 4), lax.rem(line + h, 2)
-    for t, ((ax, ah), turn) in enumerate(TILES):
-        mine, turned = (dx == ax) & (dh == ah), {"no": z < 0, "yes": z >= 0, "h": h != 0, "x": x >= 2}[turn]
-        if turn != "yes":
-
-            @pl.when(mine & jnp.logical_not(turned))
-            def _():
-                gram_out[...] = g[2 * t + k]
-
-        if turn != "no":
-            for side in range(2):
-
-                @pl.when(mine & turned & (k == side))
-                def _():
-                    gram_out[...] = g[2 * t : 2 * t + 2, :, side * H : (side + 1) * H].reshape(T, H).T
+    for copy in copies:
+        copy.wait()
 
 
 def product(tiles, slices):
@@ -317,11 +327,14 @@
         product_kernel,
         out_shape=(jax.ShapeDtypeStruct((T, T), BF16), jax.ShapeDtypeStruct((H, T), BF16)),
         in_specs=[VMEM] * len(operands),
-        out_specs=(VMEM, VMEM),
+        out_specs=(ANY, ANY),
         scratch_shapes=[
             pltpu.VMEM((16, H, T), BF16),
             pltpu.SemaphoreType.DMA((len(slices),)),
             pltpu.VMEM((T, T), F32),
+            pltpu.VMEM((T, T), BF16),
+            pltpu.VMEM((H, T), BF16),
+            pltpu.SemaphoreType.DMA((3,)),
         ],
         compiler_params=params(30),
         cost_estimate=cost(16 * T * T * T, 36 * T * T),
@@ -333,14 +346,6 @@
     return (total * (1.0 / N)).astype(BF16)
 
 
-def spread(shard, later):
-    n = shard.shape[0] // 2
-    one, three = ring("z", -1)(shard), ring("z", 1)(shard)
-    mine = [shard, one, three]
-    mine += [ring("z", -1)(rows_of(one, 0, n, *later)), ring("z", 1)(rows_of(three, n, n, *later))]
-    return mine + [swap("core")(a) for a in mine]
-
-
 def body(quant_codes, block_scales):
     own = dequant(quant_codes, block_scales)
 
@@ -348,7 +353,7 @@
     near3 = ring("x", 1)(own)
     far = swap("yh")(own)
     total0 = sum_z_in_steps(*gram(gram_kernel0, 2, [own]))
-    down, up = rows_of(near1, 0, H, total0), rows_of(near3, H, H, total0)
+    down, up = rows_of(near1, 0, H, total0, far), rows_of(near3, H, H, total0, far)
     near2 = (ring("x", -1)(down), ring("x", 1)(up))
 
     total1 = sum_z(*gram(gram_kernel1, 5, [own, near1, far], [total0, down, up]))
@@ -371,8 +376,12 @@
     again = rows_of(far, 0, T, line)
     far1, far3 = ring("x", -1)(again), ring("x", 1)(again)
     far2 = swap("yh")(local(stack, [(T, T)], *near2, line)[0])
-    slices = spread(line.reshape(16, S, T), (far1, far2, far3))
-
+    line = line.reshape(16, S, T)
+    one, three = ring("z", -1)(line), ring("z", 1)(line)
+    two = [ring("z", -1)(rows_of(one, 0, 8)), ring("z", 1)(rows_of(three, 8, 8))]
+    two = [gate(a, far1, far2, far3) for a in two]
+    mine = [line, one, three, *two]
+    slices = mine + [swap("core")(a) for a in mine]
     return product([own, near1, far1, near3, far3, far, *near2, far2], slices)
 
 

time: 154 us -> 153 us (level)
  starting transfers between devices: 61.3 us -> 50.7 us
  waiting for transfers between devices: 69.2 us -> 79.4 us
    ppermute x22, waiting for transfers between devices: 41.1 us -> 70.3 us  [ring(): lax.ppermute(a, axis, [(i, (i + step) % 4) for i in range(4)])]
    ppermute x14, waiting for transfers between devices: 28.1 us -> 9.11 us  [swap(): return lambda a: lax.ppermute(a, axis, [(0, 1), (1, 0)])]
    ppermute x14, starting transfers between devices: 30.7 us -> 17.8 us  [swap(): return lambda a: lax.ppermute(a, axis, [(0, 1), (1, 0)])]
    ppermute x22, starting transfers between devices: 30.7 us -> 32.9 us  [ring(): lax.ppermute(a, axis, [(i, (i + step) % 4) for i in range(4)])]
  transfers between devices with their start and end apart: 36 -> 36, of which waited for: 18 -> 19; matrix products, arithmetic and copies ran while one was open for 0% -> 0% of each run, Pallas kernels for 2% -> 2%
where the time goes in v5:
time: 153 us
  waiting for transfers between devices  79.4 us (52%)
  starting transfers between devices  50.7 us (33%)
  Pallas kernels  18.7 us (12%)
  local copies, waits for them, and re-layouts  2.48 us (2%)
    ppermute x22, waiting for transfers between devices, ring(): lax.ppermute(a, axis, [(i, (i + step) % 4) for i in range(4)])  70.3 us
    ppermute x22, starting transfers between devices, ring(): lax.ppermute(a, axis, [(i, (i + step) % 4) for i in range(4)])  32.9 us
    ppermute x14, starting transfers between devices, swap(): return lambda a: lax.ppermute(a, axis, [(0, 1), (1, 0)])  17.8 us
    pallas_call x1, Pallas kernels, product(): pl.pallas_call(product_kernel, out_shape=(jax.ShapeDtypeStruct((T, T), BF...  9.86 us
    ppermute x14, waiting for transfers between devices, swap(): return lambda a: lax.ppermute(a, axis, [(0, 1), (1, 0)])  9.11 us
    pallas_call x3, Pallas kernels, gram(): pl.pallas_call(kernel, out_shape=(out, out), in_specs=[VMEM] * (len(tiles...  6.14 us
  transfers between devices with their start and end apart: 36, of which 19 were waited for; matrix products, arithmetic and copies ran while one was open for 0% of the time, Pallas kernels for 2%

profile of v5, /device:TPU:1, one launch (start us, length us, event | category | flops | bytes accessed | tf_op | source)
XLA Modules:
  0.0 152.6 jit_solution(16672907512071889450)
XLA Ops:
  0.6 1.7 %copy-done = s32[768,768]{1,0:T(8,128)S(1)} copy-done((s32[768,768]{1,0:T(8,128)S(1)}, s32[768,768]{1,0:T(8,128)}, u32[]{:S(2)}) %copy-start) | copy-done | bytes 2359320
  4.5 2.1 %collective-permute-start.8 = (bf16[768,768]{1,0:T(8,128)(2,1)S(1)}, bf16[768,768]{1,0:T(8,128)(2,1)S(1)}, u32[]{:S(2)}, u32[]{:S(2)}) collective-permute-start(bf16[768,768]{1,0:T(8,128)(2,1)S(1)} %shard_map.41.own), channel_id=1, source_target_pairs={{0,4},{4,8},{8,12},{12,0},{1,5},{5,9},{9,13},{13,1},{2,6},{6,10},{... | collective-permute-start | bytes 3538952 | tf_op jit(solution)/shard_map/ppermute | solution.py:23
  6.7 2.9 %collective-permute-start.1 = (bf16[768,768]{1,0:T(8,128)(2,1)S(1)}, bf16[768,768]{1,0:T(8,128)(2,1)S(1)}, u32[]{:S(2)}, u32[]{:S(2)}) collective-permute-start(bf16[768,768]{1,0:T(8,128)(2,1)S(1)} %shard_map.41.own), channel_id=1, source_target_pairs={{0,2},{2,0},{1,3},{3,1},{4,6},{6,4},{5,7},{7,5},{8,10},{10,8},{9,1... | collective-permute-start | bytes 3538952 | tf_op jit(solution)/shard_map/ppermute | solution.py:27
  12.3 1.6 %collective-permute-start.2 = (bf16[4,96,768]{2,1,0:T(8,128)(2,1)S(1)}, bf16[4,96,768]{2,1,0:T(8,128)(2,1)S(1)}, u32[]{:S(2)}, u32[]{:S(2)}) collective-permute-start(bf16[4,96,768]{2,1,0:T(8,128)(2,1)S(1)} %get-tuple-element.19), channel_id=1, source_target_pairs={{0,1},{1,0},{2,3},{3,2},{4,5},{5,4},{6,7},{7,6},{8,9},{9,8},{10,11... | collective-permute-start | bytes 1769480 | tf_op jit(solution)/shard_map/ppermute | solution.py:27
  13.9 1.6 %collective-permute-done.2.other = bf16[4,96,768]{2,1,0:T(8,128)(2,1)S(1)} collective-permute-done((bf16[4,96,768]{2,1,0:T(8,128)(2,1)S(1)}, bf16[4,96,768]{2,1,0:T(8,128)(2,1)S(1)}, u32[]{:S(2)}, u32[]{:S(2)}) %collective-permute-start.2) | collective-permute-done | bytes 589856 | tf_op jit(solution)/shard_map/ppermute | solution.py:27
  15.5 1.7 %collective-permute-start.3 = (bf16[48,768]{1,0:T(8,128)(2,1)S(1)}, bf16[48,768]{1,0:T(8,128)(2,1)S(1)}, u32[]{:S(2)}, u32[]{:S(2)}) collective-permute-start(bf16[48,768]{1,0:T(8,128)(2,1)S(1)} %get-tuple-element.20), channel_id=1, source_target_pairs={{0,16},{16,32},{32,48},{48,0},{1,17},{17,33},{33,49},{49,1},{2,18}... | collective-permute-start | bytes 221192 | tf_op jit(solution)/shard_map/ppermute | solution.py:23
  17.3 2.2 %collective-permute-start.4 = (bf16[48,768]{1,0:T(8,128)(2,1)S(1)}, bf16[48,768]{1,0:T(8,128)(2,1)S(1)}, u32[]{:S(2)}, u32[]{:S(2)}) collective-permute-start(bf16[48,768]{1,0:T(8,128)(2,1)S(1)} %get-tuple-element.21), channel_id=1, source_target_pairs={{0,48},{16,0},{32,16},{48,32},{1,49},{17,1},{33,17},{49,33},{2,50}... | collective-permute-start | bytes 221192 | tf_op jit(solution)/shard_map/ppermute | solution.py:23
  19.5 2.3 %collective-permute-done.3.from_down = bf16[48,768]{1,0:T(8,128)(2,1)S(1)} collective-permute-done((bf16[48,768]{1,0:T(8,128)(2,1)S(1)}, bf16[48,768]{1,0:T(8,128)(2,1)S(1)}, u32[]{:S(2)}, u32[]{:S(2)}) %collective-permute-start.3) | collective-permute-done | bytes 73760 | tf_op jit(solution)/shard_map/ppermute | solution.py:23
  22.6 2.0 %collective-permute-start.6 = (bf16[96,768]{1,0:T(8,128)(2,1)S(1)}, bf16[96,768]{1,0:T(8,128)(2,1)S(1)}, u32[]{:S(2)}, u32[]{:S(2)}) collective-permute-start(bf16[96,768]{1,0:T(8,128)(2,1)S(1)} %get-tuple-element.23), channel_id=1, source_target_pairs={{0,48},{16,0},{32,16},{48,32},{1,49},{17,1},{33,17},{49,33},{2,50}... | collective-permute-start | bytes 442376 | tf_op jit(solution)/shard_map/ppermute | solution.py:23
  24.6 3.0 %collective-permute-done.5.from_down = bf16[96,768]{1,0:T(8,128)(2,1)S(1)} collective-permute-done((bf16[96,768]{1,0:T(8,128)(2,1)S(1)}, bf16[96,768]{1,0:T(8,128)(2,1)S(1)}, u32[]{:S(2)}, u32[]{:S(2)}) %collective-permute-start.5) | collective-permute-done | bytes 147488 | tf_op jit(solution)/shard_map/ppermute | solution.py:23
  27.7 5.5 %collective-permute-done.8.src.near3 = bf16[768,768]{1,0:T(8,128)(2,1)S(1)} collective-permute-done((bf16[768,768]{1,0:T(8,128)(2,1)S(1)}, bf16[768,768]{1,0:T(8,128)(2,1)S(1)}, u32[]{:S(2)}, u32[]{:S(2)}) %collective-permute-start.8) | collective-permute-done | bytes 1179680 | tf_op jit(solution)/shard_map/ppermute | solution.py:23
  35.8 3.0 %shard_map.48 = (bf16[4,240,768]{2,1,0:T(8,128)(2,1)S(1)}, bf16[4,240,768]{2,1,0:T(8,128)(2,1)S(1)}) custom-call(bf16[768,768]{1,0:T(8,128)(2,1)S(1)} %shard_map.41.own, bf16[768,768]{1,0:T(8,128)(2,1)S(1)} %collective-permute-done.src.near1, bf16[768,768]{1,0:T(8,128)(2,1)S(1)} %collective-permute-done.1.refs_1_.far.src, ...), custom_call_target="tpu_custom_call" | custom-call | flops 2264924160 | bytes 3538944 | tf_op jit(solution)/shard_map/pallas_call | solution.py:129
  38.8 2.2 %collective-permute-start.9 = (bf16[4,240,768]{2,1,0:T(8,128)(2,1)S(1)}, bf16[4,240,768]{2,1,0:T(8,128)(2,1)S(1)}, u32[]{:S(2)}, u32[]{:S(2)}) collective-permute-start(bf16[4,240,768]{2,1,0:T(8,128)(2,1)S(1)} %get-tuple-element.25), channel_id=1, source_target_pairs={{0,1},{1,0},{2,3},{3,2},{4,5},{5,4},{6,7},{7,6},{8,9},{9,8},{10,11... | collective-permute-start | bytes 4423688 | tf_op jit(solution)/shard_map/ppermute | solution.py:27
  44.2 1.7 %collective-permute-start.10 = (bf16[240,768]{1,0:T(8,128)(2,1)S(1)}, bf16[240,768]{1,0:T(8,128)(2,1)S(1)}, u32[]{:S(2)}, u32[]{:S(2)}) collective-permute-start(bf16[240,768]{1,0:T(8,128)(2,1)S(1)} %get-tuple-element.26), channel_id=1, source_target_pairs={{0,16},{16,32},{32,48},{48,0},{1,17},{17,33},{33,49},{49,1},{2,18}... | collective-permute-start | bytes 1105928 | tf_op jit(solution)/shard_map/ppermute | solution.py:23
  45.9 2.2 %collective-permute-start.11 = (bf16[240,768]{1,0:T(8,128)(2,1)S(1)}, bf16[240,768]{1,0:T(8,128)(2,1)S(1)}, u32[]{:S(2)}, u32[]{:S(2)}) collective-permute-start(bf16[240,768]{1,0:T(8,128)(2,1)S(1)} %get-tuple-element.27), channel_id=1, source_target_pairs={{0,48},{16,0},{32,16},{48,32},{1,49},{17,1},{33,17},{49,33},{2,50}... | collective-permute-start | bytes 1105928 | tf_op jit(solution)/shard_map/ppermute | solution.py:23
  49.3 7.3 %collective-permute-done.10.one = bf16[240,768]{1,0:T(8,128)(2,1)S(1)} collective-permute-done((bf16[240,768]{1,0:T(8,128)(2,1)S(1)}, bf16[240,768]{1,0:T(8,128)(2,1)S(1)}, u32[]{:S(2)}, u32[]{:S(2)}) %collective-permute-start.10) | collective-permute-done | bytes 368672 | tf_op jit(solution)/shard_map/ppermute | solution.py:23
  56.6 8.8 %collective-permute-done.12.two = bf16[240,768]{1,0:T(8,128)(2,1)S(1)} collective-permute-done((bf16[240,768]{1,0:T(8,128)(2,1)S(1)}, bf16[240,768]{1,0:T(8,128)(2,1)S(1)}, u32[]{:S(2)}, u32[]{:S(2)}) %collective-permute-start.12) | collective-permute-done | bytes 368672 | tf_op jit(solution)/shard_map/ppermute | solution.py:23
  65.6 1.9 %shard_map.51 = (bf16[4,96,768]{2,1,0:T(8,128)(2,1)S(1)}, bf16[4,96,768]{2,1,0:T(8,128)(2,1)S(1)}) custom-call(bf16[768,768]{1,0:T(8,128)(2,1)S(1)} %shard_map.41.own, bf16[768,768]{1,0:T(8,128)(2,1)S(1)} %collective-permute-done.1.refs_1_.far.src, bf16[384,768]{1,0:T(8,128)(2,1)S(1)} %collective-permute-done.15.near2a.top, ...), custom_call_target="tpu_custom_call" | custom-call | flops 905969664 | bytes 3538944 | tf_op jit(solution)/shard_map/pallas_call | solution.py:129
  71.6 1.8 %collective-permute-start.19 = (bf16[96,768]{1,0:T(8,128)(2,1)S(1)}, bf16[96,768]{1,0:T(8,128)(2,1)S(1)}, u32[]{:S(2)}, u32[]{:S(2)}) collective-permute-start(bf16[96,768]{1,0:T(8,128)(2,1)S(1)} %get-tuple-element.32), channel_id=1, source_target_pairs={{0,48},{16,0},{32,16},{48,32},{1,49},{17,1},{33,17},{49,33},{2,50}... | collective-permute-start | bytes 442376 | tf_op jit(solution)/shard_map/ppermute | solution.py:23
  73.9 3.1 %collective-permute-done.18.one = bf16[96,768]{1,0:T(8,128)(2,1)S(1)} collective-permute-done((bf16[96,768]{1,0:T(8,128)(2,1)S(1)}, bf16[96,768]{1,0:T(8,128)(2,1)S(1)}, u32[]{:S(2)}, u32[]{:S(2)}) %collective-permute-start.18) | collective-permute-done | bytes 147488 | tf_op jit(solution)/shard_map/ppermute | solution.py:23
  77.0 2.9 %collective-permute-done.20.two = bf16[96,768]{1,0:T(8,128)(2,1)S(1)} collective-permute-done((bf16[96,768]{1,0:T(8,128)(2,1)S(1)}, bf16[96,768]{1,0:T(8,128)(2,1)S(1)}, u32[]{:S(2)}, u32[]{:S(2)}) %collective-permute-start.20) | collective-permute-done | bytes 147488 | tf_op jit(solution)/shard_map/ppermute | solution.py:23
  81.9 2.2 %collective-permute-done.21 = bf16[96,768]{1,0:T(8,128)(2,1)S(1)} collective-permute-done((bf16[96,768]{1,0:T(8,128)(2,1)S(1)}, bf16[96,768]{1,0:T(8,128)(2,1)S(1)}, u32[]{:S(2)}, u32[]{:S(2)}) %collective-permute-start.21) | collective-permute-done | bytes 147488 | tf_op jit(solution)/shard_map/ppermute | solution.py:27
  84.1 1.6 %collective-permute-start.23 = (bf16[192,768]{1,0:T(8,128)(2,1)S(1)}, bf16[192,768]{1,0:T(8,128)(2,1)S(1)}, u32[]{:S(2)}, u32[]{:S(2)}) collective-permute-start(bf16[192,768]{1,0:T(8,128)(2,1)S(1)} %shard_map.54), channel_id=1, source_target_pairs={{0,2},{2,0},{1,3},{3,1},{4,6},{6,4},{5,7},{7,5},{8,10},{10,8},{9,1... | collective-permute-start | bytes 884744 | tf_op jit(solution)/shard_map/ppermute | solution.py:27
  85.8 2.5 %collective-permute-start.22 = (bf16[96,768]{1,0:T(8,128)(2,1)S(1)}, bf16[96,768]{1,0:T(8,128)(2,1)S(1)}, u32[]{:S(2)}, u32[]{:S(2)}) collective-permute-start(bf16[96,768]{1,0:T(8,128)(2,1)S(1)} %multiply_convert_fusion.1.second.shard2), channel_id=1, source_target_pairs={{0,8},{4,12},{8,0},{12,4},{1,9},{5,13},{9,1},{13,5},{2,10},{6,14},... | collective-permute-start | bytes 442376 | tf_op jit(solution)/shard_map/ppermute | solution.py:23
  88.5 4.7 %collective-permute-done.22.from_x2 = bf16[96,768]{1,0:T(8,128)(2,1)S(1)} collective-permute-done((bf16[96,768]{1,0:T(8,128)(2,1)S(1)}, bf16[96,768]{1,0:T(8,128)(2,1)S(1)}, u32[]{:S(2)}, u32[]{:S(2)}) %collective-permute-start.22) | collective-permute-done | bytes 147488 | tf_op jit(solution)/shard_map/ppermute | solution.py:23
  94.3 1.8 %collective-permute-start.27 = (bf16[16,48,768]{2,1,0:T(8,128)(2,1)S(1)}, bf16[16,48,768]{2,1,0:T(8,128)(2,1)S(1)}, u32[]{:S(2)}, u32[]{:S(2)}) collective-permute-start(bf16[16,48,768]{2,1,0:T(8,128)(2,1)S(1)} %bitcast.2), channel_id=1, source_target_pairs={{0,48},{16,0},{32,16},{48,32},{1,49},{17,1},{33,17},{49,33},{2,50}... | collective-permute-start | bytes 3538952 | tf_op jit(solution)/shard_map/ppermute | solution.py:23
  97.5 2.7 %collective-permute-start.24 = (bf16[768,768]{1,0:T(8,128)(2,1)S(1)}, bf16[768,768]{1,0:T(8,128)(2,1)S(1)}, u32[]{:S(2)}, u32[]{:S(2)}) collective-permute-start(bf16[768,768]{1,0:T(8,128)(2,1)S(1)} %shard_map.56), channel_id=1, source_target_pairs={{0,12},{4,0},{8,4},{12,8},{1,13},{5,1},{9,5},{13,9},{2,14},{6,2},{... | collective-permute-start | bytes 3538952 | tf_op jit(solution)/shard_map/ppermute | solution.py:23
  100.1 19.5 %collective-permute-done.28.src.refs_2_ = bf16[16,48,768]{2,1,0:T(8,128)(2,1)S(1)} collective-permute-done((bf16[16,48,768]{2,1,0:T(8,128)(2,1)S(1)}, bf16[16,48,768]{2,1,0:T(8,128)(2,1)S(1)}, u32[]{:S(2)}, u32[]{:S(2)}) %collective-permute-start.28) | collective-permute-done | bytes 1179680 | tf_op jit(solution)/shard_map/ppermute | solution.py:23
  119.6 3.4 %collective-permute-start.31 = (bf16[16,48,768]{2,1,0:T(8,128)(2,1)S(1)}, bf16[16,48,768]{2,1,0:T(8,128)(2,1)S(1)}, u32[]{:S(2)}, u32[]{:S(2)}) collective-permute-start(bf16[16,48,768]{2,1,0:T(8,128)(2,1)S(1)} %bitcast.3), channel_id=1, source_target_pairs={{0,1},{1,0},{2,3},{3,2},{4,5},{5,4},{6,7},{7,6},{8,9},{9,8},{10,11... | collective-permute-start | bytes 3538952 | tf_op jit(solution)/shard_map/ppermute | solution.py:27
  123.2 2.7 %collective-permute-start.29 = (bf16[8,48,768]{2,1,0:T(8,128)(2,1)S(1)}, bf16[8,48,768]{2,1,0:T(8,128)(2,1)S(1)}, u32[]{:S(2)}, u32[]{:S(2)}) collective-permute-start(bf16[8,48,768]{2,1,0:T(8,128)(2,1)S(1)} %shard_map.58), channel_id=1, source_target_pairs={{0,48},{16,0},{32,16},{48,32},{1,49},{17,1},{33,17},{49,33},{2,50}... | collective-permute-start | bytes 1769480 | tf_op jit(solution)/shard_map/ppermute | solution.py:23
  127.2 12.0 %collective-permute-done.30.refs_0_ = bf16[8,48,768]{2,1,0:T(8,128)(2,1)S(1)} collective-permute-done((bf16[8,48,768]{2,1,0:T(8,128)(2,1)S(1)}, bf16[8,48,768]{2,1,0:T(8,128)(2,1)S(1)}, u32[]{:S(2)}, u32[]{:S(2)}) %collective-permute-start.30) | collective-permute-done | bytes 589856 | tf_op jit(solution)/shard_map/ppermute | solution.py:23
  142.5 9.9 %shard_map.62 = (bf16[768,768]{1,0:T(8,128)(2,1)}, bf16[384,768]{1,0:T(8,128)(2,1)}) custom-call(bf16[768,768]{1,0:T(8,128)(2,1)S(1)} %shard_map.41.own, bf16[768,768]{1,0:T(8,128)(2,1)S(1)} %collective-permute-done.src.near1, bf16[768,768]{1,0:T(8,128)(2,1)S(1)} %collective-permute-done.24.refs_1_.far1, ...), custom_call_target="tpu_custom_call" | custom-call | flops 7247757312 | bytes 21233664 | tf_op jit(solution)/shard_map/pallas_call | solution.py:326
  (70 shorter events, 27.3 us)
Async XLA Ops:
  4.5 28.6 %collective-permute-start.8 = (bf16[768,768]{1,0:T(8,128)(2,1)S(1)}, bf16[768,768]{1,0:T(8,128)(2,1)S(1)}, u32[]{:S(2)}, u32[]{:S(2)}) collective-permute-start(bf16[768,768]{1,0:T(8,128)(2,1)S(1)} %shard_map.41.own), channel_id=1, source_target_pairs={{0,4},{4,8},{8,12},{12,0},{1,5},{5,9},{9,13},{13,1},{2,6},{6,10},{... | collective-permute-start | bytes 3538952 | tf_op jit(solution)/shard_map/ppermute | solution.py:23
  6.7 28.0 %collective-permute-start.1 = (bf16[768,768]{1,0:T(8,128)(2,1)S(1)}, bf16[768,768]{1,0:T(8,128)(2,1)S(1)}, u32[]{:S(2)}, u32[]{:S(2)}) collective-permute-start(bf16[768,768]{1,0:T(8,128)(2,1)S(1)} %shard_map.41.own), channel_id=1, source_target_pairs={{0,2},{2,0},{1,3},{3,1},{4,6},{6,4},{5,7},{7,5},{8,10},{10,8},{9,1... | collective-permute-start | bytes 3538952 | tf_op jit(solution)/shard_map/ppermute | solution.py:27
  9.6 26.2 %collective-permute-start = (bf16[768,768]{1,0:T(8,128)(2,1)S(1)}, bf16[768,768]{1,0:T(8,128)(2,1)S(1)}, u32[]{:S(2)}, u32[]{:S(2)}) collective-permute-start(bf16[768,768]{1,0:T(8,128)(2,1)S(1)} %shard_map.41.own), channel_id=1, source_target_pairs={{0,12},{4,0},{8,4},{12,8},{1,13},{5,1},{9,5},{13,9},{2,14},{6,2},{... | collective-permute-start | bytes 3538952 | tf_op jit(solution)/shard_map/ppermute | solution.py:23
  15.5 6.2 %collective-permute-start.3 = (bf16[48,768]{1,0:T(8,128)(2,1)S(1)}, bf16[48,768]{1,0:T(8,128)(2,1)S(1)}, u32[]{:S(2)}, u32[]{:S(2)}) collective-permute-start(bf16[48,768]{1,0:T(8,128)(2,1)S(1)} %get-tuple-element.20), channel_id=1, source_target_pairs={{0,16},{16,32},{32,48},{48,0},{1,17},{17,33},{33,49},{49,1},{2,18}... | collective-permute-start | bytes 221192 | tf_op jit(solution)/shard_map/ppermute | solution.py:23
  17.3 4.5 %collective-permute-start.4 = (bf16[48,768]{1,0:T(8,128)(2,1)S(1)}, bf16[48,768]{1,0:T(8,128)(2,1)S(1)}, u32[]{:S(2)}, u32[]{:S(2)}) collective-permute-start(bf16[48,768]{1,0:T(8,128)(2,1)S(1)} %get-tuple-element.21), channel_id=1, source_target_pairs={{0,48},{16,0},{32,16},{48,32},{1,49},{17,1},{33,17},{49,33},{2,50}... | collective-permute-start | bytes 221192 | tf_op jit(solution)/shard_map/ppermute | solution.py:23
  21.8 5.8 %collective-permute-start.5 = (bf16[96,768]{1,0:T(8,128)(2,1)S(1)}, bf16[96,768]{1,0:T(8,128)(2,1)S(1)}, u32[]{:S(2)}, u32[]{:S(2)}) collective-permute-start(bf16[96,768]{1,0:T(8,128)(2,1)S(1)} %get-tuple-element.22), channel_id=1, source_target_pairs={{0,16},{16,32},{32,48},{48,0},{1,17},{17,33},{33,49},{49,1},{2,18}... | collective-permute-start | bytes 442376 | tf_op jit(solution)/shard_map/ppermute | solution.py:23
  22.6 5.0 %collective-permute-start.6 = (bf16[96,768]{1,0:T(8,128)(2,1)S(1)}, bf16[96,768]{1,0:T(8,128)(2,1)S(1)}, u32[]{:S(2)}, u32[]{:S(2)}) collective-permute-start(bf16[96,768]{1,0:T(8,128)(2,1)S(1)} %get-tuple-element.23), channel_id=1, source_target_pairs={{0,48},{16,0},{32,16},{48,32},{1,49},{17,1},{33,17},{49,33},{2,50}... | collective-permute-start | bytes 442376 | tf_op jit(solution)/shard_map/ppermute | solution.py:23
  38.8 5.1 %collective-permute-start.9 = (bf16[4,240,768]{2,1,0:T(8,128)(2,1)S(1)}, bf16[4,240,768]{2,1,0:T(8,128)(2,1)S(1)}, u32[]{:S(2)}, u32[]{:S(2)}) collective-permute-start(bf16[4,240,768]{2,1,0:T(8,128)(2,1)S(1)} %get-tuple-element.25), channel_id=1, source_target_pairs={{0,1},{1,0},{2,3},{3,2},{4,5},{5,4},{6,7},{7,6},{8,9},{9,8},{10,11... | collective-permute-start | bytes 4423688 | tf_op jit(solution)/shard_map/ppermute | solution.py:27
  41.1 24.6 %collective-permute-start.16 = (bf16[384,768]{1,0:T(8,128)(2,1)S(1)}, bf16[384,768]{1,0:T(8,128)(2,1)S(1)}, u32[]{:S(2)}, u32[]{:S(2)}) collective-permute-start(bf16[384,768]{1,0:T(8,128)(2,1)S(1)} %shard_map.47.___), channel_id=1, source_target_pairs={{0,4},{4,8},{8,12},{12,0},{1,5},{5,9},{9,13},{13,1},{2,6},{6,10},{... | collective-permute-start | bytes 1769480 | tf_op jit(solution)/shard_map/ppermute | solution.py:23
  42.3 23.4 %collective-permute-start.15 = (bf16[384,768]{1,0:T(8,128)(2,1)S(1)}, bf16[384,768]{1,0:T(8,128)(2,1)S(1)}, u32[]{:S(2)}, u32[]{:S(2)}) collective-permute-start(bf16[384,768]{1,0:T(8,128)(2,1)S(1)} %shard_map.46.__), channel_id=1, source_target_pairs={{0,12},{4,0},{8,4},{12,8},{1,13},{5,1},{9,5},{13,9},{2,14},{6,2},{... | collective-permute-start | bytes 1769480 | tf_op jit(solution)/shard_map/ppermute | solution.py:23
  44.2 12.4 %collective-permute-start.10 = (bf16[240,768]{1,0:T(8,128)(2,1)S(1)}, bf16[240,768]{1,0:T(8,128)(2,1)S(1)}, u32[]{:S(2)}, u32[]{:S(2)}) collective-permute-start(bf16[240,768]{1,0:T(8,128)(2,1)S(1)} %get-tuple-element.26), channel_id=1, source_target_pairs={{0,16},{16,32},{32,48},{48,0},{1,17},{17,33},{33,49},{49,1},{2,18}... | collective-permute-start | bytes 1105928 | tf_op jit(solution)/shard_map/ppermute | solution.py:23
  45.9 10.7 %collective-permute-start.11 = (bf16[240,768]{1,0:T(8,128)(2,1)S(1)}, bf16[240,768]{1,0:T(8,128)(2,1)S(1)}, u32[]{:S(2)}, u32[]{:S(2)}) collective-permute-start(bf16[240,768]{1,0:T(8,128)(2,1)S(1)} %get-tuple-element.27), channel_id=1, source_target_pairs={{0,48},{16,0},{32,16},{48,32},{1,49},{17,1},{33,17},{49,33},{2,50}... | collective-permute-start | bytes 1105928 | tf_op jit(solution)/shard_map/ppermute | solution.py:23
  48.1 17.3 %collective-permute-start.12 = (bf16[240,768]{1,0:T(8,128)(2,1)S(1)}, bf16[240,768]{1,0:T(8,128)(2,1)S(1)}, u32[]{:S(2)}, u32[]{:S(2)}) collective-permute-start(bf16[240,768]{1,0:T(8,128)(2,1)S(1)} %get-tuple-element.28), channel_id=1, source_target_pairs={{0,32},{16,48},{32,0},{48,16},{1,33},{17,49},{33,1},{49,17},{2,34}... | collective-permute-start | bytes 1105928 | tf_op jit(solution)/shard_map/ppermute | solution.py:23
  68.9 11.5 %collective-permute-start.13 = (bf16[240,768]{1,0:T(8,128)(2,1)S(1)}, bf16[240,768]{1,0:T(8,128)(2,1)S(1)}, u32[]{:S(2)}, u32[]{:S(2)}) collective-permute-start(bf16[240,768]{1,0:T(8,128)(2,1)S(1)} %shard_map.50._), channel_id=1, source_target_pairs={{0,64},{64,0},{1,65},{65,1},{2,66},{66,2},{3,67},{67,3},{4,68},{68... | collective-permute-start | bytes 1105928 | tf_op jit(solution)/shard_map/ppermute | solution.py:27
  70.7 6.3 %collective-permute-start.18 = (bf16[96,768]{1,0:T(8,128)(2,1)S(1)}, bf16[96,768]{1,0:T(8,128)(2,1)S(1)}, u32[]{:S(2)}, u32[]{:S(2)}) collective-permute-start(bf16[96,768]{1,0:T(8,128)(2,1)S(1)} %get-tuple-element.31), channel_id=1, source_target_pairs={{0,16},{16,32},{32,48},{48,0},{1,17},{17,33},{33,49},{49,1},{2,18}... | collective-permute-start | bytes 442376 | tf_op jit(solution)/shard_map/ppermute | solution.py:23
  71.6 5.4 %collective-permute-start.19 = (bf16[96,768]{1,0:T(8,128)(2,1)S(1)}, bf16[96,768]{1,0:T(8,128)(2,1)S(1)}, u32[]{:S(2)}, u32[]{:S(2)}) collective-permute-start(bf16[96,768]{1,0:T(8,128)(2,1)S(1)} %get-tuple-element.32), channel_id=1, source_target_pairs={{0,48},{16,0},{32,16},{48,32},{1,49},{17,1},{33,17},{49,33},{2,50}... | collective-permute-start | bytes 442376 | tf_op jit(solution)/shard_map/ppermute | solution.py:23
  73.4 6.5 %collective-permute-start.20 = (bf16[96,768]{1,0:T(8,128)(2,1)S(1)}, bf16[96,768]{1,0:T(8,128)(2,1)S(1)}, u32[]{:S(2)}, u32[]{:S(2)}) collective-permute-start(bf16[96,768]{1,0:T(8,128)(2,1)S(1)} %get-tuple-element.33), channel_id=1, source_target_pairs={{0,32},{16,48},{32,0},{48,16},{1,33},{17,49},{33,1},{49,17},{2,34}... | collective-permute-start | bytes 442376 | tf_op jit(solution)/shard_map/ppermute | solution.py:23
  73.5 14.7 %collective-permute-start.7 = (bf16[96,768]{1,0:T(8,128)(2,1)S(1)}, bf16[96,768]{1,0:T(8,128)(2,1)S(1)}, u32[]{:S(2)}, u32[]{:S(2)}) collective-permute-start(bf16[96,768]{1,0:T(8,128)(2,1)S(1)} %shard_map.45.refs_0_._), channel_id=1, source_target_pairs={{0,64},{64,0},{1,65},{65,1},{2,66},{66,2},{3,67},{67,3},{4,68},{68... | collective-permute-start | bytes 442376 | tf_op jit(solution)/shard_map/ppermute | solution.py:27
  80.0 4.1 %collective-permute-start.21 = (bf16[96,768]{1,0:T(8,128)(2,1)S(1)}, bf16[96,768]{1,0:T(8,128)(2,1)S(1)}, u32[]{:S(2)}, u32[]{:S(2)}) collective-permute-start(bf16[96,768]{1,0:T(8,128)(2,1)S(1)} %shard_map.53), channel_id=1, source_target_pairs={{0,64},{64,0},{1,65},{65,1},{2,66},{66,2},{3,67},{67,3},{4,68},{68... | collective-permute-start | bytes 442376 | tf_op jit(solution)/shard_map/ppermute | solution.py:27
  80.6 7.9 %collective-permute-start.14 = (bf16[192,768]{1,0:T(8,128)(2,1)S(1)}, bf16[192,768]{1,0:T(8,128)(2,1)S(1)}, u32[]{:S(2)}, u32[]{:S(2)}) collective-permute-start(bf16[192,768]{1,0:T(8,128)(2,1)S(1)} %slice.4), channel_id=1, source_target_pairs={{0,4},{4,8},{8,12},{12,0},{1,5},{5,9},{9,13},{13,1},{2,6},{6,10},{... | collective-permute-start | bytes 884744 | tf_op jit(solution)/shard_map/ppermute | solution.py:23
  84.1 9.1 %collective-permute-start.23 = (bf16[192,768]{1,0:T(8,128)(2,1)S(1)}, bf16[192,768]{1,0:T(8,128)(2,1)S(1)}, u32[]{:S(2)}, u32[]{:S(2)}) collective-permute-start(bf16[192,768]{1,0:T(8,128)(2,1)S(1)} %shard_map.54), channel_id=1, source_target_pairs={{0,2},{2,0},{1,3},{3,1},{4,6},{6,4},{5,7},{7,5},{8,10},{10,8},{9,1... | collective-permute-start | bytes 884744 | tf_op jit(solution)/shard_map/ppermute | solution.py:27
  85.8 7.4 %collective-permute-start.22 = (bf16[96,768]{1,0:T(8,128)(2,1)S(1)}, bf16[96,768]{1,0:T(8,128)(2,1)S(1)}, u32[]{:S(2)}, u32[]{:S(2)}) collective-permute-start(bf16[96,768]{1,0:T(8,128)(2,1)S(1)} %multiply_convert_fusion.1.second.shard2), channel_id=1, source_target_pairs={{0,8},{4,12},{8,0},{12,4},{1,9},{5,13},{9,1},{13,5},{2,10},{6,14},... | collective-permute-start | bytes 442376 | tf_op jit(solution)/shard_map/ppermute | solution.py:23
  93.3 26.3 %collective-permute-start.28 = (bf16[16,48,768]{2,1,0:T(8,128)(2,1)S(1)}, bf16[16,48,768]{2,1,0:T(8,128)(2,1)S(1)}, u32[]{:S(2)}, u32[]{:S(2)}) collective-permute-start(bf16[16,48,768]{2,1,0:T(8,128)(2,1)S(1)} %bitcast.1), channel_id=1, source_target_pairs={{0,16},{16,32},{32,48},{48,0},{1,17},{17,33},{33,49},{49,1},{2,18}... | collective-permute-start | bytes 3538952 | tf_op jit(solution)/shard_map/ppermute | solution.py:23
  94.3 28.7 %collective-permute-start.27 = (bf16[16,48,768]{2,1,0:T(8,128)(2,1)S(1)}, bf16[16,48,768]{2,1,0:T(8,128)(2,1)S(1)}, u32[]{:S(2)}, u32[]{:S(2)}) collective-permute-start(bf16[16,48,768]{2,1,0:T(8,128)(2,1)S(1)} %bitcast.2), channel_id=1, source_target_pairs={{0,48},{16,0},{32,16},{48,32},{1,49},{17,1},{33,17},{49,33},{2,50}... | collective-permute-start | bytes 3538952 | tf_op jit(solution)/shard_map/ppermute | solution.py:23
  96.1 27.0 %collective-permute-start.26 = (bf16[768,768]{1,0:T(8,128)(2,1)S(1)}, bf16[768,768]{1,0:T(8,128)(2,1)S(1)}, u32[]{:S(2)}, u32[]{:S(2)}) collective-permute-start(bf16[768,768]{1,0:T(8,128)(2,1)S(1)} %shard_map.57), channel_id=1, source_target_pairs={{0,2},{2,0},{1,3},{3,1},{4,6},{6,4},{5,7},{7,5},{8,10},{10,8},{9,1... | collective-permute-start | bytes 3538952 | tf_op jit(solution)/shard_map/ppermute | solution.py:27
  97.4 28.5 %collective-permute-start.25 = (bf16[768,768]{1,0:T(8,128)(2,1)S(1)}, bf16[768,768]{1,0:T(8,128)(2,1)S(1)}, u32[]{:S(2)}, u32[]{:S(2)}) collective-permute-start(bf16[768,768]{1,0:T(8,128)(2,1)S(1)} %shard_map.56), channel_id=1, source_target_pairs={{0,4},{4,8},{8,12},{12,0},{1,5},{5,9},{9,13},{13,1},{2,6},{6,10},{... | collective-permute-start | bytes 3538952 | tf_op jit(solution)/shard_map/ppermute | solution.py:23
  97.5 29.7 %collective-permute-start.24 = (bf16[768,768]{1,0:T(8,128)(2,1)S(1)}, bf16[768,768]{1,0:T(8,128)(2,1)S(1)}, u32[]{:S(2)}, u32[]{:S(2)}) collective-permute-start(bf16[768,768]{1,0:T(8,128)(2,1)S(1)} %shard_map.56), channel_id=1, source_target_pairs={{0,12},{4,0},{8,4},{12,8},{1,13},{5,1},{9,5},{13,9},{2,14},{6,2},{... | collective-permute-start | bytes 3538952 | tf_op jit(solution)/shard_map/ppermute | solution.py:23
  119.6 20.5 %collective-permute-start.31 = (bf16[16,48,768]{2,1,0:T(8,128)(2,1)S(1)}, bf16[16,48,768]{2,1,0:T(8,128)(2,1)S(1)}, u32[]{:S(2)}, u32[]{:S(2)}) collective-permute-start(bf16[16,48,768]{2,1,0:T(8,128)(2,1)S(1)} %bitcast.3), channel_id=1, source_target_pairs={{0,1},{1,0},{2,3},{3,2},{4,5},{5,4},{6,7},{7,6},{8,9},{9,8},{10,11... | collective-permute-start | bytes 3538952 | tf_op jit(solution)/shard_map/ppermute | solution.py:27
  123.0 16.2 %collective-permute-start.30 = (bf16[8,48,768]{2,1,0:T(8,128)(2,1)S(1)}, bf16[8,48,768]{2,1,0:T(8,128)(2,1)S(1)}, u32[]{:S(2)}, u32[]{:S(2)}) collective-permute-start(bf16[8,48,768]{2,1,0:T(8,128)(2,1)S(1)} %shard_map.60), channel_id=1, source_target_pairs={{0,16},{16,32},{32,48},{48,0},{1,17},{17,33},{33,49},{49,1},{2,18}... | collective-permute-start | bytes 1769480 | tf_op jit(solution)/shard_map/ppermute | solution.py:23
  123.2 16.9 %collective-permute-start.29 = (bf16[8,48,768]{2,1,0:T(8,128)(2,1)S(1)}, bf16[8,48,768]{2,1,0:T(8,128)(2,1)S(1)}, u32[]{:S(2)}, u32[]{:S(2)}) collective-permute-start(bf16[8,48,768]{2,1,0:T(8,128)(2,1)S(1)} %shard_map.58), channel_id=1, source_target_pairs={{0,48},{16,0},{32,16},{48,32},{1,49},{17,1},{33,17},{49,33},{2,50}... | collective-permute-start | bytes 1769480 | tf_op jit(solution)/shard_map/ppermute | solution.py:23
  125.9 15.8 %collective-permute-start.33 = (bf16[16,48,768]{2,1,0:T(8,128)(2,1)S(1)}, bf16[16,48,768]{2,1,0:T(8,128)(2,1)S(1)}, u32[]{:S(2)}, u32[]{:S(2)}) collective-permute-start(bf16[16,48,768]{2,1,0:T(8,128)(2,1)S(1)} %collective-permute-done.28.src.refs_2_), channel_id=1, source_target_pairs={{0,1},{1,0},{2,3},{3,2},{4,5},{5,4},{6,7},{7,6},{8,9},{9,8},{10,11... | collective-permute-start | bytes 3538952 | tf_op jit(solution)/shard_map/ppermute | solution.py:27
  127.2 15.4 %collective-permute-start.32 = (bf16[16,48,768]{2,1,0:T(8,128)(2,1)S(1)}, bf16[16,48,768]{2,1,0:T(8,128)(2,1)S(1)}, u32[]{:S(2)}, u32[]{:S(2)}) collective-permute-start(bf16[16,48,768]{2,1,0:T(8,128)(2,1)S(1)} %collective-permute-done.27.src.refs_1_), channel_id=1, source_target_pairs={{0,1},{1,0},{2,3},{3,2},{4,5},{5,4},{6,7},{7,6},{8,9},{9,8},{10,11... | collective-permute-start | bytes 3538952 | tf_op jit(solution)/shard_map/ppermute | solution.py:27
  (6 other events, 13.6 us)

commit v6 on v5

--- a/solution.py
+++ b/solution.py
@@ -90,12 +90,9 @@
     cut(full, 0, 2, keep, send)
 
 
-def gram_kernel1(own, near1, far, _, __, ___, keep, send, full):
-    turned = near1[...].T
-    full[...] = dot(turned, own[...])
+def gram_kernel1a(own, near1, far, _, __, ___, keep, send, full):
+    full[...] = tdot(near1[...], own[...])
     cut(full, 0, 2, keep, send)
-    full[...] = dot(turned, far[...])
-    cut(full, 2, 2, keep, send)
     h = lax.axis_index("yh")
 
     @pl.when(h == 0)
@@ -106,7 +103,12 @@
     def _():
         full[0:H, :] = tdot(own[:, H:T], far[...])
 
-    cut(full, 4, 1, keep, send)
+    cut(full, 2, 1, keep, send)
+
+
+def gram_kernel1b(near1, far, _, keep, send, full):
+    full[...] = tdot(near1[...], far[...])
+    cut(full, 0, 2, keep, send)
 
 
 def gram_kernel2(own, far, near2a, near2b, _, keep, send, full):
@@ -124,7 +126,7 @@
         cut(full, i, 1, keep, send)
 
 
-def gram(kernel, halves, tiles, later=()):
+def gram(kernel, halves, tiles, later=(), weight=1):
     out = jax.ShapeDtypeStruct((4, halves * S, T), BF16)
     return pl.pallas_call(
         kernel,
@@ -133,7 +135,7 @@
         out_specs=(VMEM, VMEM),
         scratch_shapes=[pltpu.VMEM((T, T), F32)],
         compiler_params=params(14),
-        cost_estimate=cost(halves * T * T * T, 6 * T * T),
+        cost_estimate=cost(weight * halves * T * T * T, weight * 6 * T * T),
     )(*tiles, *later)
 
 
@@ -200,20 +202,27 @@
     return local(step3, [(count, T)], keep, other, up, down)[0]
 
 
-def sum_z(keep, send):
-    other = swap("core")(send)
-    shape = keep.shape[1:]
-
-    def step1(keep, other, *parts):
-        for j, part in enumerate(parts):
-            part[...] = add(keep[j + 1], other[j + 1]).astype(BF16)
-
-    def step2(keep, other, one, three, two, out):
-        out[...] = add(keep[0], other[0], one[...], three[...], two[...]).astype(BF16)
-
-    parts = local(step1, [shape] * 3, keep, other)
+def sum_z(*pieces):
+    pairs = [a for keep, send, _ in pieces for a in (keep, swap("core")(send))]
+    moves = [(2 * i, *move) for i, piece in enumerate(pieces) for move in piece[2]]
+    count = len(pairs)
+    shape = (sum(move[2] for move in moves), T)
+
+    def step1(*refs):
+        for i, first, size, to in moves:
+            rows = slice(first, first + size)
+            for j, part in enumerate(refs[count:]):
+                part[to : to + size] = add(refs[i][j + 1, rows], refs[i + 1][j + 1, rows]).astype(BF16)
+
+    def step2(*refs):
+        one, three, two, out = refs[count:]
+        for i, first, size, to in moves:
+            rows, at = slice(first, first + size), slice(to, to + size)
+            out[at] = add(refs[i][0, rows], refs[i + 1][0, rows], one[at], three[at], two[at]).astype(BF16)
+
+    parts = local(step1, [shape] * 3, *pairs)
     got = [ring("z", j)(parts[j - 1]) for j in (1, 3, 2)]
-    return local(step2, [shape], keep, other, *got)[0]
+    return local(step2, [shape], *pairs, *got)[0]
 
 
 def line_kernel(shard0, shard1, from_x1, shard2, from_x2, from_y, out):
@@ -356,8 +365,10 @@
     down, up = rows_of(near1, 0, H, total0, far), rows_of(near3, H, H, total0, far)
     near2 = (ring("x", -1)(down), ring("x", 1)(up))
 
-    total1 = sum_z(*gram(gram_kernel1, 5, [own, near1, far], [total0, down, up]))
-    total2 = sum_z(*gram(gram_kernel2, 2, [own, far, *near2], [total1]))
+    piece1a = gram(gram_kernel1a, 3, [own, near1, far], [total0, down, up])
+    piece1b = gram(gram_kernel1b, 2, [near1, far], [piece1a[0]], 0)
+    total1 = sum_z((*piece1a, ((0, 2 * S, 0), (2 * S, S, 4 * S))), (*piece1b, ((0, 2 * S, 2 * S),)))
+    total2 = sum_z((*gram(gram_kernel2, 2, [own, far, *near2], [total1]), ((0, 2 * S, 0),)))
     shard0, shard1, shard2 = sum_yl(total0), sum_yl(total1), sum_yl(total2)
     from_x1 = ring("x", 1)(shard1[: 4 * S])
     from_x2 = ring("x", 2)(shard2)

time: 153 us -> 153 us (level)
    ppermute x14 -> x15, starting transfers between devices: 17.8 us -> 18.7 us  [swap(): return lambda a: lax.ppermute(a, axis, [(0, 1), (1, 0)])]
    ppermute x14 -> x15, waiting for transfers between devices: 9.11 us -> 9.76 us  [swap(): return lambda a: lax.ppermute(a, axis, [(0, 1), (1, 0)])]
    pallas_call x3 -> x4, Pallas kernels: 6.14 us -> 6.37 us  [gram(): pl.pallas_call(kernel, out_shape=(out, out), in_specs=[VMEM] * (len(tiles...]
  transfers between devices with their start and end apart: 36 -> 37, of which waited for: 19 -> 18; matrix products, arithmetic and copies ran while one was open for 0% -> 0% of each run, Pallas kernels for 2% -> 2%
where the time goes in v6:
time: 153 us; the launch traced here: 152 us
  waiting for transfers between devices  79.6 us (52%)
  starting transfers between devices  50.2 us (33%)
  Pallas kernels  19 us (12%)
  local copies, waits for them, and re-layouts  2.48 us (2%)
    ppermute x22, waiting for transfers between devices, ring(): lax.ppermute(a, axis, [(i, (i + step) % 4) for i in range(4)])  69.8 us
    ppermute x22, starting transfers between devices, ring(): lax.ppermute(a, axis, [(i, (i + step) % 4) for i in range(4)])  31.4 us
    ppermute x15, starting transfers between devices, swap(): return lambda a: lax.ppermute(a, axis, [(0, 1), (1, 0)])  18.7 us
    pallas_call x1, Pallas kernels, product(): pl.pallas_call(product_kernel, out_shape=(jax.ShapeDtypeStruct((T, T), BF...  9.86 us
    ppermute x15, waiting for transfers between devices, swap(): return lambda a: lax.ppermute(a, axis, [(0, 1), (1, 0)])  9.76 us
    pallas_call x4, Pallas kernels, gram(): pl.pallas_call(kernel, out_shape=(out, out), in_specs=[VMEM] * (len(tiles...  6.37 us
  transfers between devices with their start and end apart: 37, of which 18 were waited for; matrix products, arithmetic and copies ran while one was open for 0% of the time, Pallas kernels for 2%

profile of v6, /device:TPU:1, one launch (start us, length us, event | category | flops | bytes accessed | tf_op | source)
XLA Modules:
  0.0 152.5 jit_solution(7806647328582333318)
XLA Ops:
  0.6 1.7 %copy-done = s32[768,768]{1,0:T(8,128)S(1)} copy-done((s32[768,768]{1,0:T(8,128)S(1)}, s32[768,768]{1,0:T(8,128)}, u32[]{:S(2)}) %copy-start) | copy-done | bytes 2359320
  4.5 2.1 %collective-permute-start.8 = (bf16[768,768]{1,0:T(8,128)(2,1)S(1)}, bf16[768,768]{1,0:T(8,128)(2,1)S(1)}, u32[]{:S(2)}, u32[]{:S(2)}) collective-permute-start(bf16[768,768]{1,0:T(8,128)(2,1)S(1)} %shard_map.41.own), channel_id=1, source_target_pairs={{0,4},{4,8},{8,12},{12,0},{1,5},{5,9},{9,13},{13,1},{2,6},{6,10},{... | collective-permute-start | bytes 3538952 | tf_op jit(solution)/shard_map/ppermute | solution.py:23
  6.7 2.9 %collective-permute-start.1 = (bf16[768,768]{1,0:T(8,128)(2,1)S(1)}, bf16[768,768]{1,0:T(8,128)(2,1)S(1)}, u32[]{:S(2)}, u32[]{:S(2)}) collective-permute-start(bf16[768,768]{1,0:T(8,128)(2,1)S(1)} %shard_map.41.own), channel_id=1, source_target_pairs={{0,2},{2,0},{1,3},{3,1},{4,6},{6,4},{5,7},{7,5},{8,10},{10,8},{9,1... | collective-permute-start | bytes 3538952 | tf_op jit(solution)/shard_map/ppermute | solution.py:27
  12.3 1.6 %collective-permute-start.2 = (bf16[4,96,768]{2,1,0:T(8,128)(2,1)S(1)}, bf16[4,96,768]{2,1,0:T(8,128)(2,1)S(1)}, u32[]{:S(2)}, u32[]{:S(2)}) collective-permute-start(bf16[4,96,768]{2,1,0:T(8,128)(2,1)S(1)} %get-tuple-element.21), channel_id=1, source_target_pairs={{0,1},{1,0},{2,3},{3,2},{4,5},{5,4},{6,7},{7,6},{8,9},{9,8},{10,11... | collective-permute-start | bytes 1769480 | tf_op jit(solution)/shard_map/ppermute | solution.py:27
  13.9 1.6 %collective-permute-done.2.other = bf16[4,96,768]{2,1,0:T(8,128)(2,1)S(1)} collective-permute-done((bf16[4,96,768]{2,1,0:T(8,128)(2,1)S(1)}, bf16[4,96,768]{2,1,0:T(8,128)(2,1)S(1)}, u32[]{:S(2)}, u32[]{:S(2)}) %collective-permute-start.2) | collective-permute-done | bytes 589856 | tf_op jit(solution)/shard_map/ppermute | solution.py:27
  15.5 1.7 %collective-permute-start.3 = (bf16[48,768]{1,0:T(8,128)(2,1)S(1)}, bf16[48,768]{1,0:T(8,128)(2,1)S(1)}, u32[]{:S(2)}, u32[]{:S(2)}) collective-permute-start(bf16[48,768]{1,0:T(8,128)(2,1)S(1)} %get-tuple-element.22), channel_id=1, source_target_pairs={{0,16},{16,32},{32,48},{48,0},{1,17},{17,33},{33,49},{49,1},{2,18}... | collective-permute-start | bytes 221192 | tf_op jit(solution)/shard_map/ppermute | solution.py:23
  17.3 2.2 %collective-permute-start.4 = (bf16[48,768]{1,0:T(8,128)(2,1)S(1)}, bf16[48,768]{1,0:T(8,128)(2,1)S(1)}, u32[]{:S(2)}, u32[]{:S(2)}) collective-permute-start(bf16[48,768]{1,0:T(8,128)(2,1)S(1)} %get-tuple-element.23), channel_id=1, source_target_pairs={{0,48},{16,0},{32,16},{48,32},{1,49},{17,1},{33,17},{49,33},{2,50}... | collective-permute-start | bytes 221192 | tf_op jit(solution)/shard_map/ppermute | solution.py:23
  19.5 2.3 %collective-permute-done.3.from_down = bf16[48,768]{1,0:T(8,128)(2,1)S(1)} collective-permute-done((bf16[48,768]{1,0:T(8,128)(2,1)S(1)}, bf16[48,768]{1,0:T(8,128)(2,1)S(1)}, u32[]{:S(2)}, u32[]{:S(2)}) %collective-permute-start.3) | collective-permute-done | bytes 73760 | tf_op jit(solution)/shard_map/ppermute | solution.py:23
  22.6 2.0 %collective-permute-start.6 = (bf16[96,768]{1,0:T(8,128)(2,1)S(1)}, bf16[96,768]{1,0:T(8,128)(2,1)S(1)}, u32[]{:S(2)}, u32[]{:S(2)}) collective-permute-start(bf16[96,768]{1,0:T(8,128)(2,1)S(1)} %get-tuple-element.25), channel_id=1, source_target_pairs={{0,48},{16,0},{32,16},{48,32},{1,49},{17,1},{33,17},{49,33},{2,50}... | collective-permute-start | bytes 442376 | tf_op jit(solution)/shard_map/ppermute | solution.py:23
  24.6 3.0 %collective-permute-done.5.from_down = bf16[96,768]{1,0:T(8,128)(2,1)S(1)} collective-permute-done((bf16[96,768]{1,0:T(8,128)(2,1)S(1)}, bf16[96,768]{1,0:T(8,128)(2,1)S(1)}, u32[]{:S(2)}, u32[]{:S(2)}) %collective-permute-start.5) | collective-permute-done | bytes 147488 | tf_op jit(solution)/shard_map/ppermute | solution.py:23
  27.7 5.5 %collective-permute-done.8.src.near3 = bf16[768,768]{1,0:T(8,128)(2,1)S(1)} collective-permute-done((bf16[768,768]{1,0:T(8,128)(2,1)S(1)}, bf16[768,768]{1,0:T(8,128)(2,1)S(1)}, u32[]{:S(2)}, u32[]{:S(2)}) %collective-permute-start.8) | collective-permute-done | bytes 1179680 | tf_op jit(solution)/shard_map/ppermute | solution.py:23
  35.8 2.0 %shard_map.48 = (bf16[4,144,768]{2,1,0:T(8,128)(2,1)S(1)}, bf16[4,144,768]{2,1,0:T(8,128)(2,1)S(1)}) custom-call(bf16[768,768]{1,0:T(8,128)(2,1)S(1)} %shard_map.41.own, bf16[768,768]{1,0:T(8,128)(2,1)S(1)} %collective-permute-done.src.near1, bf16[768,768]{1,0:T(8,128)(2,1)S(1)} %collective-permute-done.1.refs_1_.far.src, ...), custom_call_target="tpu_custom_call" | custom-call | flops 1358954496 | bytes 3538944 | tf_op jit(solution)/shard_map/pallas_call | solution.py:131
  37.8 2.2 %collective-permute-start.9 = (bf16[4,144,768]{2,1,0:T(8,128)(2,1)S(1)}, bf16[4,144,768]{2,1,0:T(8,128)(2,1)S(1)}, u32[]{:S(2)}, u32[]{:S(2)}) collective-permute-start(bf16[4,144,768]{2,1,0:T(8,128)(2,1)S(1)} %get-tuple-element.27), channel_id=1, source_target_pairs={{0,1},{1,0},{2,3},{3,2},{4,5},{5,4},{6,7},{7,6},{8,9},{9,8},{10,11... | collective-permute-start | bytes 2654216 | tf_op jit(solution)/shard_map/ppermute | solution.py:27
  44.5 1.7 %collective-permute-start.11 = (bf16[240,768]{1,0:T(8,128)(2,1)S(1)}, bf16[240,768]{1,0:T(8,128)(2,1)S(1)}, u32[]{:S(2)}, u32[]{:S(2)}) collective-permute-start(bf16[240,768]{1,0:T(8,128)(2,1)S(1)} %get-tuple-element.30), channel_id=1, source_target_pairs={{0,16},{16,32},{32,48},{48,0},{1,17},{17,33},{33,49},{49,1},{2,18}... | collective-permute-start | bytes 1105928 | tf_op jit(solution)/shard_map/ppermute | solution.py:23
  46.2 2.2 %collective-permute-start.12 = (bf16[240,768]{1,0:T(8,128)(2,1)S(1)}, bf16[240,768]{1,0:T(8,128)(2,1)S(1)}, u32[]{:S(2)}, u32[]{:S(2)}) collective-permute-start(bf16[240,768]{1,0:T(8,128)(2,1)S(1)} %get-tuple-element.31), channel_id=1, source_target_pairs={{0,48},{16,0},{32,16},{48,32},{1,49},{17,1},{33,17},{49,33},{2,50}... | collective-permute-start | bytes 1105928 | tf_op jit(solution)/shard_map/ppermute | solution.py:23
  49.6 6.7 %collective-permute-done.11.refs_4_ = bf16[240,768]{1,0:T(8,128)(2,1)S(1)} collective-permute-done((bf16[240,768]{1,0:T(8,128)(2,1)S(1)}, bf16[240,768]{1,0:T(8,128)(2,1)S(1)}, u32[]{:S(2)}, u32[]{:S(2)}) %collective-permute-start.11) | collective-permute-done | bytes 368672 | tf_op jit(solution)/shard_map/ppermute | solution.py:23
  56.4 8.8 %collective-permute-done.13.refs_6_ = bf16[240,768]{1,0:T(8,128)(2,1)S(1)} collective-permute-done((bf16[240,768]{1,0:T(8,128)(2,1)S(1)}, bf16[240,768]{1,0:T(8,128)(2,1)S(1)}, u32[]{:S(2)}, u32[]{:S(2)}) %collective-permute-start.13) | collective-permute-done | bytes 368672 | tf_op jit(solution)/shard_map/ppermute | solution.py:23
  65.4 1.9 %shard_map.52 = (bf16[4,96,768]{2,1,0:T(8,128)(2,1)S(1)}, bf16[4,96,768]{2,1,0:T(8,128)(2,1)S(1)}) custom-call(bf16[768,768]{1,0:T(8,128)(2,1)S(1)} %shard_map.41.own, bf16[768,768]{1,0:T(8,128)(2,1)S(1)} %collective-permute-done.1.refs_1_.far.src, bf16[384,768]{1,0:T(8,128)(2,1)S(1)} %collective-permute-done.16.near2a.top, ...), custom_call_target="tpu_custom_call" | custom-call | flops 905969664 | bytes 3538944 | tf_op jit(solution)/shard_map/pallas_call | solution.py:131
  67.3 1.9 %collective-permute-start.18 = (bf16[4,96,768]{2,1,0:T(8,128)(2,1)S(1)}, bf16[4,96,768]{2,1,0:T(8,128)(2,1)S(1)}, u32[]{:S(2)}, u32[]{:S(2)}) collective-permute-start(bf16[4,96,768]{2,1,0:T(8,128)(2,1)S(1)} %get-tuple-element.34), channel_id=1, source_target_pairs={{0,1},{1,0},{2,3},{3,2},{4,5},{5,4},{6,7},{7,6},{8,9},{9,8},{10,11... | collective-permute-start | bytes 1769480 | tf_op jit(solution)/shard_map/ppermute | solution.py:27
  71.9 1.8 %collective-permute-start.20 = (bf16[96,768]{1,0:T(8,128)(2,1)S(1)}, bf16[96,768]{1,0:T(8,128)(2,1)S(1)}, u32[]{:S(2)}, u32[]{:S(2)}) collective-permute-start(bf16[96,768]{1,0:T(8,128)(2,1)S(1)} %get-tuple-element.36), channel_id=1, source_target_pairs={{0,48},{16,0},{32,16},{48,32},{1,49},{17,1},{33,17},{49,33},{2,50}... | collective-permute-start | bytes 442376 | tf_op jit(solution)/shard_map/ppermute | solution.py:23
  74.2 3.1 %collective-permute-done.19.refs_2_ = bf16[96,768]{1,0:T(8,128)(2,1)S(1)} collective-permute-done((bf16[96,768]{1,0:T(8,128)(2,1)S(1)}, bf16[96,768]{1,0:T(8,128)(2,1)S(1)}, u32[]{:S(2)}, u32[]{:S(2)}) %collective-permute-start.19) | collective-permute-done | bytes 147488 | tf_op jit(solution)/shard_map/ppermute | solution.py:23
  77.3 2.9 %collective-permute-done.21.refs_4_ = bf16[96,768]{1,0:T(8,128)(2,1)S(1)} collective-permute-done((bf16[96,768]{1,0:T(8,128)(2,1)S(1)}, bf16[96,768]{1,0:T(8,128)(2,1)S(1)}, u32[]{:S(2)}, u32[]{:S(2)}) %collective-permute-start.21) | collective-permute-done | bytes 147488 | tf_op jit(solution)/shard_map/ppermute | solution.py:23
  81.3 3.0 %collective-permute-done.22 = bf16[96,768]{1,0:T(8,128)(2,1)S(1)} collective-permute-done((bf16[96,768]{1,0:T(8,128)(2,1)S(1)}, bf16[96,768]{1,0:T(8,128)(2,1)S(1)}, u32[]{:S(2)}, u32[]{:S(2)}) %collective-permute-start.22) | collective-permute-done | bytes 147488 | tf_op jit(solution)/shard_map/ppermute | solution.py:27
  86.0 1.7 %collective-permute-start.23 = (bf16[96,768]{1,0:T(8,128)(2,1)S(1)}, bf16[96,768]{1,0:T(8,128)(2,1)S(1)}, u32[]{:S(2)}, u32[]{:S(2)}) collective-permute-start(bf16[96,768]{1,0:T(8,128)(2,1)S(1)} %multiply_convert_fusion.1.second.shard2), channel_id=1, source_target_pairs={{0,8},{4,12},{8,0},{12,4},{1,9},{5,13},{9,1},{13,5},{2,10},{6,14},... | collective-permute-start | bytes 442376 | tf_op jit(solution)/shard_map/ppermute | solution.py:23
  88.8 4.3 %collective-permute-done.23.from_x2 = bf16[96,768]{1,0:T(8,128)(2,1)S(1)} collective-permute-done((bf16[96,768]{1,0:T(8,128)(2,1)S(1)}, bf16[96,768]{1,0:T(8,128)(2,1)S(1)}, u32[]{:S(2)}, u32[]{:S(2)}) %collective-permute-start.23) | collective-permute-done | bytes 147488 | tf_op jit(solution)/shard_map/ppermute | solution.py:23
  94.2 1.8 %collective-permute-start.28 = (bf16[16,48,768]{2,1,0:T(8,128)(2,1)S(1)}, bf16[16,48,768]{2,1,0:T(8,128)(2,1)S(1)}, u32[]{:S(2)}, u32[]{:S(2)}) collective-permute-start(bf16[16,48,768]{2,1,0:T(8,128)(2,1)S(1)} %bitcast.2), channel_id=1, source_target_pairs={{0,48},{16,0},{32,16},{48,32},{1,49},{17,1},{33,17},{49,33},{2,50}... | collective-permute-start | bytes 3538952 | tf_op jit(solution)/shard_map/ppermute | solution.py:23
  97.6 2.7 %collective-permute-start.25 = (bf16[768,768]{1,0:T(8,128)(2,1)S(1)}, bf16[768,768]{1,0:T(8,128)(2,1)S(1)}, u32[]{:S(2)}, u32[]{:S(2)}) collective-permute-start(bf16[768,768]{1,0:T(8,128)(2,1)S(1)} %shard_map.57), channel_id=1, source_target_pairs={{0,12},{4,0},{8,4},{12,8},{1,13},{5,1},{9,5},{13,9},{2,14},{6,2},{... | collective-permute-start | bytes 3538952 | tf_op jit(solution)/shard_map/ppermute | solution.py:23
  100.3 19.1 %collective-permute-done.29.src.refs_2_ = bf16[16,48,768]{2,1,0:T(8,128)(2,1)S(1)} collective-permute-done((bf16[16,48,768]{2,1,0:T(8,128)(2,1)S(1)}, bf16[16,48,768]{2,1,0:T(8,128)(2,1)S(1)}, u32[]{:S(2)}, u32[]{:S(2)}) %collective-permute-start.29) | collective-permute-done | bytes 1179680 | tf_op jit(solution)/shard_map/ppermute | solution.py:23
  119.4 3.4 %collective-permute-start.32 = (bf16[16,48,768]{2,1,0:T(8,128)(2,1)S(1)}, bf16[16,48,768]{2,1,0:T(8,128)(2,1)S(1)}, u32[]{:S(2)}, u32[]{:S(2)}) collective-permute-start(bf16[16,48,768]{2,1,0:T(8,128)(2,1)S(1)} %bitcast.3), channel_id=1, source_target_pairs={{0,1},{1,0},{2,3},{3,2},{4,5},{5,4},{6,7},{7,6},{8,9},{9,8},{10,11... | collective-permute-start | bytes 3538952 | tf_op jit(solution)/shard_map/ppermute | solution.py:27
  123.1 2.7 %collective-permute-start.30 = (bf16[8,48,768]{2,1,0:T(8,128)(2,1)S(1)}, bf16[8,48,768]{2,1,0:T(8,128)(2,1)S(1)}, u32[]{:S(2)}, u32[]{:S(2)}) collective-permute-start(bf16[8,48,768]{2,1,0:T(8,128)(2,1)S(1)} %shard_map.59), channel_id=1, source_target_pairs={{0,48},{16,0},{32,16},{48,32},{1,49},{17,1},{33,17},{49,33},{2,50}... | collective-permute-start | bytes 1769480 | tf_op jit(solution)/shard_map/ppermute | solution.py:23
  127.2 11.9 %collective-permute-done.31.refs_0_ = bf16[8,48,768]{2,1,0:T(8,128)(2,1)S(1)} collective-permute-done((bf16[8,48,768]{2,1,0:T(8,128)(2,1)S(1)}, bf16[8,48,768]{2,1,0:T(8,128)(2,1)S(1)}, u32[]{:S(2)}, u32[]{:S(2)}) %collective-permute-start.31) | collective-permute-done | bytes 589856 | tf_op jit(solution)/shard_map/ppermute | solution.py:23
  142.4 9.9 %shard_map.63 = (bf16[768,768]{1,0:T(8,128)(2,1)}, bf16[384,768]{1,0:T(8,128)(2,1)}) custom-call(bf16[768,768]{1,0:T(8,128)(2,1)S(1)} %shard_map.41.own, bf16[768,768]{1,0:T(8,128)(2,1)S(1)} %collective-permute-done.src.near1, bf16[768,768]{1,0:T(8,128)(2,1)S(1)} %collective-permute-done.25.refs_1_.far1, ...), custom_call_target="tpu_custom_call" | custom-call | flops 7247757312 | bytes 21233664 | tf_op jit(solution)/shard_map/pallas_call | solution.py:335
  (73 shorter events, 29.1 us)
Async XLA Ops:
  4.5 28.6 %collective-permute-start.8 = (bf16[768,768]{1,0:T(8,128)(2,1)S(1)}, bf16[768,768]{1,0:T(8,128)(2,1)S(1)}, u32[]{:S(2)}, u32[]{:S(2)}) collective-permute-start(bf16[768,768]{1,0:T(8,128)(2,1)S(1)} %shard_map.41.own), channel_id=1, source_target_pairs={{0,4},{4,8},{8,12},{12,0},{1,5},{5,9},{9,13},{13,1},{2,6},{6,10},{... | collective-permute-start | bytes 3538952 | tf_op jit(solution)/shard_map/ppermute | solution.py:23
  6.7 28.0 %collective-permute-start.1 = (bf16[768,768]{1,0:T(8,128)(2,1)S(1)}, bf16[768,768]{1,0:T(8,128)(2,1)S(1)}, u32[]{:S(2)}, u32[]{:S(2)}) collective-permute-start(bf16[768,768]{1,0:T(8,128)(2,1)S(1)} %shard_map.41.own), channel_id=1, source_target_pairs={{0,2},{2,0},{1,3},{3,1},{4,6},{6,4},{5,7},{7,5},{8,10},{10,8},{9,1... | collective-permute-start | bytes 3538952 | tf_op jit(solution)/shard_map/ppermute | solution.py:27
  9.6 26.2 %collective-permute-start = (bf16[768,768]{1,0:T(8,128)(2,1)S(1)}, bf16[768,768]{1,0:T(8,128)(2,1)S(1)}, u32[]{:S(2)}, u32[]{:S(2)}) collective-permute-start(bf16[768,768]{1,0:T(8,128)(2,1)S(1)} %shard_map.41.own), channel_id=1, source_target_pairs={{0,12},{4,0},{8,4},{12,8},{1,13},{5,1},{9,5},{13,9},{2,14},{6,2},{... | collective-permute-start | bytes 3538952 | tf_op jit(solution)/shard_map/ppermute | solution.py:23
  15.5 6.2 %collective-permute-start.3 = (bf16[48,768]{1,0:T(8,128)(2,1)S(1)}, bf16[48,768]{1,0:T(8,128)(2,1)S(1)}, u32[]{:S(2)}, u32[]{:S(2)}) collective-permute-start(bf16[48,768]{1,0:T(8,128)(2,1)S(1)} %get-tuple-element.22), channel_id=1, source_target_pairs={{0,16},{16,32},{32,48},{48,0},{1,17},{17,33},{33,49},{49,1},{2,18}... | collective-permute-start | bytes 221192 | tf_op jit(solution)/shard_map/ppermute | solution.py:23
  17.3 4.5 %collective-permute-start.4 = (bf16[48,768]{1,0:T(8,128)(2,1)S(1)}, bf16[48,768]{1,0:T(8,128)(2,1)S(1)}, u32[]{:S(2)}, u32[]{:S(2)}) collective-permute-start(bf16[48,768]{1,0:T(8,128)(2,1)S(1)} %get-tuple-element.23), channel_id=1, source_target_pairs={{0,48},{16,0},{32,16},{48,32},{1,49},{17,1},{33,17},{49,33},{2,50}... | collective-permute-start | bytes 221192 | tf_op jit(solution)/shard_map/ppermute | solution.py:23
  21.8 5.8 %collective-permute-start.5 = (bf16[96,768]{1,0:T(8,128)(2,1)S(1)}, bf16[96,768]{1,0:T(8,128)(2,1)S(1)}, u32[]{:S(2)}, u32[]{:S(2)}) collective-permute-start(bf16[96,768]{1,0:T(8,128)(2,1)S(1)} %get-tuple-element.24), channel_id=1, source_target_pairs={{0,16},{16,32},{32,48},{48,0},{1,17},{17,33},{33,49},{49,1},{2,18}... | collective-permute-start | bytes 442376 | tf_op jit(solution)/shard_map/ppermute | solution.py:23
  22.6 5.0 %collective-permute-start.6 = (bf16[96,768]{1,0:T(8,128)(2,1)S(1)}, bf16[96,768]{1,0:T(8,128)(2,1)S(1)}, u32[]{:S(2)}, u32[]{:S(2)}) collective-permute-start(bf16[96,768]{1,0:T(8,128)(2,1)S(1)} %get-tuple-element.25), channel_id=1, source_target_pairs={{0,48},{16,0},{32,16},{48,32},{1,49},{17,1},{33,17},{49,33},{2,50}... | collective-permute-start | bytes 442376 | tf_op jit(solution)/shard_map/ppermute | solution.py:23
  37.8 6.4 %collective-permute-start.9 = (bf16[4,144,768]{2,1,0:T(8,128)(2,1)S(1)}, bf16[4,144,768]{2,1,0:T(8,128)(2,1)S(1)}, u32[]{:S(2)}, u32[]{:S(2)}) collective-permute-start(bf16[4,144,768]{2,1,0:T(8,128)(2,1)S(1)} %get-tuple-element.27), channel_id=1, source_target_pairs={{0,1},{1,0},{2,3},{3,2},{4,5},{5,4},{6,7},{7,6},{8,9},{9,8},{10,11... | collective-permute-start | bytes 2654216 | tf_op jit(solution)/shard_map/ppermute | solution.py:27
  41.4 24.0 %collective-permute-start.17 = (bf16[384,768]{1,0:T(8,128)(2,1)S(1)}, bf16[384,768]{1,0:T(8,128)(2,1)S(1)}, u32[]{:S(2)}, u32[]{:S(2)}) collective-permute-start(bf16[384,768]{1,0:T(8,128)(2,1)S(1)} %shard_map.47.___), channel_id=1, source_target_pairs={{0,4},{4,8},{8,12},{12,0},{1,5},{5,9},{9,13},{13,1},{2,6},{6,10},{... | collective-permute-start | bytes 1769480 | tf_op jit(solution)/shard_map/ppermute | solution.py:23
  42.7 22.7 %collective-permute-start.16 = (bf16[384,768]{1,0:T(8,128)(2,1)S(1)}, bf16[384,768]{1,0:T(8,128)(2,1)S(1)}, u32[]{:S(2)}, u32[]{:S(2)}) collective-permute-start(bf16[384,768]{1,0:T(8,128)(2,1)S(1)} %shard_map.46.__), channel_id=1, source_target_pairs={{0,12},{4,0},{8,4},{12,8},{1,13},{5,1},{9,5},{13,9},{2,14},{6,2},{... | collective-permute-start | bytes 1769480 | tf_op jit(solution)/shard_map/ppermute | solution.py:23
  44.5 11.9 %collective-permute-start.11 = (bf16[240,768]{1,0:T(8,128)(2,1)S(1)}, bf16[240,768]{1,0:T(8,128)(2,1)S(1)}, u32[]{:S(2)}, u32[]{:S(2)}) collective-permute-start(bf16[240,768]{1,0:T(8,128)(2,1)S(1)} %get-tuple-element.30), channel_id=1, source_target_pairs={{0,16},{16,32},{32,48},{48,0},{1,17},{17,33},{33,49},{49,1},{2,18}... | collective-permute-start | bytes 1105928 | tf_op jit(solution)/shard_map/ppermute | solution.py:23
  46.2 10.2 %collective-permute-start.12 = (bf16[240,768]{1,0:T(8,128)(2,1)S(1)}, bf16[240,768]{1,0:T(8,128)(2,1)S(1)}, u32[]{:S(2)}, u32[]{:S(2)}) collective-permute-start(bf16[240,768]{1,0:T(8,128)(2,1)S(1)} %get-tuple-element.31), channel_id=1, source_target_pairs={{0,48},{16,0},{32,16},{48,32},{1,49},{17,1},{33,17},{49,33},{2,50}... | collective-permute-start | bytes 1105928 | tf_op jit(solution)/shard_map/ppermute | solution.py:23
  48.4 16.7 %collective-permute-start.13 = (bf16[240,768]{1,0:T(8,128)(2,1)S(1)}, bf16[240,768]{1,0:T(8,128)(2,1)S(1)}, u32[]{:S(2)}, u32[]{:S(2)}) collective-permute-start(bf16[240,768]{1,0:T(8,128)(2,1)S(1)} %get-tuple-element.32), channel_id=1, source_target_pairs={{0,32},{16,48},{32,0},{48,16},{1,33},{17,49},{33,1},{49,17},{2,34}... | collective-permute-start | bytes 1105928 | tf_op jit(solution)/shard_map/ppermute | solution.py:23
  69.2 11.5 %collective-permute-start.14 = (bf16[240,768]{1,0:T(8,128)(2,1)S(1)}, bf16[240,768]{1,0:T(8,128)(2,1)S(1)}, u32[]{:S(2)}, u32[]{:S(2)}) collective-permute-start(bf16[240,768]{1,0:T(8,128)(2,1)S(1)} %shard_map.51._), channel_id=1, source_target_pairs={{0,64},{64,0},{1,65},{65,1},{2,66},{66,2},{3,67},{67,3},{4,68},{68... | collective-permute-start | bytes 1105928 | tf_op jit(solution)/shard_map/ppermute | solution.py:27
  70.9 6.3 %collective-permute-start.19 = (bf16[96,768]{1,0:T(8,128)(2,1)S(1)}, bf16[96,768]{1,0:T(8,128)(2,1)S(1)}, u32[]{:S(2)}, u32[]{:S(2)}) collective-permute-start(bf16[96,768]{1,0:T(8,128)(2,1)S(1)} %get-tuple-element.35), channel_id=1, source_target_pairs={{0,16},{16,32},{32,48},{48,0},{1,17},{17,33},{33,49},{49,1},{2,18}... | collective-permute-start | bytes 442376 | tf_op jit(solution)/shard_map/ppermute | solution.py:23
  71.9 5.4 %collective-permute-start.20 = (bf16[96,768]{1,0:T(8,128)(2,1)S(1)}, bf16[96,768]{1,0:T(8,128)(2,1)S(1)}, u32[]{:S(2)}, u32[]{:S(2)}) collective-permute-start(bf16[96,768]{1,0:T(8,128)(2,1)S(1)} %get-tuple-element.36), channel_id=1, source_target_pairs={{0,48},{16,0},{32,16},{48,32},{1,49},{17,1},{33,17},{49,33},{2,50}... | collective-permute-start | bytes 442376 | tf_op jit(solution)/shard_map/ppermute | solution.py:23
  73.7 6.5 %collective-permute-start.21 = (bf16[96,768]{1,0:T(8,128)(2,1)S(1)}, bf16[96,768]{1,0:T(8,128)(2,1)S(1)}, u32[]{:S(2)}, u32[]{:S(2)}) collective-permute-start(bf16[96,768]{1,0:T(8,128)(2,1)S(1)} %get-tuple-element.37), channel_id=1, source_target_pairs={{0,32},{16,48},{32,0},{48,16},{1,33},{17,49},{33,1},{49,17},{2,34}... | collective-permute-start | bytes 442376 | tf_op jit(solution)/shard_map/ppermute | solution.py:23
  73.8 13.9 %collective-permute-start.7 = (bf16[96,768]{1,0:T(8,128)(2,1)S(1)}, bf16[96,768]{1,0:T(8,128)(2,1)S(1)}, u32[]{:S(2)}, u32[]{:S(2)}) collective-permute-start(bf16[96,768]{1,0:T(8,128)(2,1)S(1)} %shard_map.45.refs_0_._), channel_id=1, source_target_pairs={{0,64},{64,0},{1,65},{65,1},{2,66},{66,2},{3,67},{67,3},{4,68},{68... | collective-permute-start | bytes 442376 | tf_op jit(solution)/shard_map/ppermute | solution.py:27
  80.3 4.1 %collective-permute-start.22 = (bf16[96,768]{1,0:T(8,128)(2,1)S(1)}, bf16[96,768]{1,0:T(8,128)(2,1)S(1)}, u32[]{:S(2)}, u32[]{:S(2)}) collective-permute-start(bf16[96,768]{1,0:T(8,128)(2,1)S(1)} %shard_map.54), channel_id=1, source_target_pairs={{0,64},{64,0},{1,65},{65,1},{2,66},{66,2},{3,67},{67,3},{4,68},{68... | collective-permute-start | bytes 442376 | tf_op jit(solution)/shard_map/ppermute | solution.py:27
  80.9 7.9 %collective-permute-start.15 = (bf16[192,768]{1,0:T(8,128)(2,1)S(1)}, bf16[192,768]{1,0:T(8,128)(2,1)S(1)}, u32[]{:S(2)}, u32[]{:S(2)}) collective-permute-start(bf16[192,768]{1,0:T(8,128)(2,1)S(1)} %slice.4), channel_id=1, source_target_pairs={{0,4},{4,8},{8,12},{12,0},{1,5},{5,9},{9,13},{13,1},{2,6},{6,10},{... | collective-permute-start | bytes 884744 | tf_op jit(solution)/shard_map/ppermute | solution.py:23
  84.4 8.7 %collective-permute-start.24 = (bf16[192,768]{1,0:T(8,128)(2,1)S(1)}, bf16[192,768]{1,0:T(8,128)(2,1)S(1)}, u32[]{:S(2)}, u32[]{:S(2)}) collective-permute-start(bf16[192,768]{1,0:T(8,128)(2,1)S(1)} %shard_map.55), channel_id=1, source_target_pairs={{0,2},{2,0},{1,3},{3,1},{4,6},{6,4},{5,7},{7,5},{8,10},{10,8},{9,1... | collective-permute-start | bytes 884744 | tf_op jit(solution)/shard_map/ppermute | solution.py:27
  86.0 7.1 %collective-permute-start.23 = (bf16[96,768]{1,0:T(8,128)(2,1)S(1)}, bf16[96,768]{1,0:T(8,128)(2,1)S(1)}, u32[]{:S(2)}, u32[]{:S(2)}) collective-permute-start(bf16[96,768]{1,0:T(8,128)(2,1)S(1)} %multiply_convert_fusion.1.second.shard2), channel_id=1, source_target_pairs={{0,8},{4,12},{8,0},{12,4},{1,9},{5,13},{9,1},{13,5},{2,10},{6,14},... | collective-permute-start | bytes 442376 | tf_op jit(solution)/shard_map/ppermute | solution.py:23
  93.2 26.2 %collective-permute-start.29 = (bf16[16,48,768]{2,1,0:T(8,128)(2,1)S(1)}, bf16[16,48,768]{2,1,0:T(8,128)(2,1)S(1)}, u32[]{:S(2)}, u32[]{:S(2)}) collective-permute-start(bf16[16,48,768]{2,1,0:T(8,128)(2,1)S(1)} %bitcast.1), channel_id=1, source_target_pairs={{0,16},{16,32},{32,48},{48,0},{1,17},{17,33},{33,49},{49,1},{2,18}... | collective-permute-start | bytes 3538952 | tf_op jit(solution)/shard_map/ppermute | solution.py:23
  94.2 28.7 %collective-permute-start.28 = (bf16[16,48,768]{2,1,0:T(8,128)(2,1)S(1)}, bf16[16,48,768]{2,1,0:T(8,128)(2,1)S(1)}, u32[]{:S(2)}, u32[]{:S(2)}) collective-permute-start(bf16[16,48,768]{2,1,0:T(8,128)(2,1)S(1)} %bitcast.2), channel_id=1, source_target_pairs={{0,48},{16,0},{32,16},{48,32},{1,49},{17,1},{33,17},{49,33},{2,50}... | collective-permute-start | bytes 3538952 | tf_op jit(solution)/shard_map/ppermute | solution.py:23
  96.0 27.0 %collective-permute-start.27 = (bf16[768,768]{1,0:T(8,128)(2,1)S(1)}, bf16[768,768]{1,0:T(8,128)(2,1)S(1)}, u32[]{:S(2)}, u32[]{:S(2)}) collective-permute-start(bf16[768,768]{1,0:T(8,128)(2,1)S(1)} %shard_map.58), channel_id=1, source_target_pairs={{0,2},{2,0},{1,3},{3,1},{4,6},{6,4},{5,7},{7,5},{8,10},{10,8},{9,1... | collective-permute-start | bytes 3538952 | tf_op jit(solution)/shard_map/ppermute | solution.py:27
  97.6 28.2 %collective-permute-start.26 = (bf16[768,768]{1,0:T(8,128)(2,1)S(1)}, bf16[768,768]{1,0:T(8,128)(2,1)S(1)}, u32[]{:S(2)}, u32[]{:S(2)}) collective-permute-start(bf16[768,768]{1,0:T(8,128)(2,1)S(1)} %shard_map.57), channel_id=1, source_target_pairs={{0,4},{4,8},{8,12},{12,0},{1,5},{5,9},{9,13},{13,1},{2,6},{6,10},{... | collective-permute-start | bytes 3538952 | tf_op jit(solution)/shard_map/ppermute | solution.py:23
  97.6 29.6 %collective-permute-start.25 = (bf16[768,768]{1,0:T(8,128)(2,1)S(1)}, bf16[768,768]{1,0:T(8,128)(2,1)S(1)}, u32[]{:S(2)}, u32[]{:S(2)}) collective-permute-start(bf16[768,768]{1,0:T(8,128)(2,1)S(1)} %shard_map.57), channel_id=1, source_target_pairs={{0,12},{4,0},{8,4},{12,8},{1,13},{5,1},{9,5},{13,9},{2,14},{6,2},{... | collective-permute-start | bytes 3538952 | tf_op jit(solution)/shard_map/ppermute | solution.py:23
  119.4 20.6 %collective-permute-start.32 = (bf16[16,48,768]{2,1,0:T(8,128)(2,1)S(1)}, bf16[16,48,768]{2,1,0:T(8,128)(2,1)S(1)}, u32[]{:S(2)}, u32[]{:S(2)}) collective-permute-start(bf16[16,48,768]{2,1,0:T(8,128)(2,1)S(1)} %bitcast.3), channel_id=1, source_target_pairs={{0,1},{1,0},{2,3},{3,2},{4,5},{5,4},{6,7},{7,6},{8,9},{9,8},{10,11... | collective-permute-start | bytes 3538952 | tf_op jit(solution)/shard_map/ppermute | solution.py:27
  122.9 16.2 %collective-permute-start.31 = (bf16[8,48,768]{2,1,0:T(8,128)(2,1)S(1)}, bf16[8,48,768]{2,1,0:T(8,128)(2,1)S(1)}, u32[]{:S(2)}, u32[]{:S(2)}) collective-permute-start(bf16[8,48,768]{2,1,0:T(8,128)(2,1)S(1)} %shard_map.61), channel_id=1, source_target_pairs={{0,16},{16,32},{32,48},{48,0},{1,17},{17,33},{33,49},{49,1},{2,18}... | collective-permute-start | bytes 1769480 | tf_op jit(solution)/shard_map/ppermute | solution.py:23
  123.1 16.9 %collective-permute-start.30 = (bf16[8,48,768]{2,1,0:T(8,128)(2,1)S(1)}, bf16[8,48,768]{2,1,0:T(8,128)(2,1)S(1)}, u32[]{:S(2)}, u32[]{:S(2)}) collective-permute-start(bf16[8,48,768]{2,1,0:T(8,128)(2,1)S(1)} %shard_map.59), channel_id=1, source_target_pairs={{0,48},{16,0},{32,16},{48,32},{1,49},{17,1},{33,17},{49,33},{2,50}... | collective-permute-start | bytes 1769480 | tf_op jit(solution)/shard_map/ppermute | solution.py:23
  125.8 16.6 %collective-permute-start.34 = (bf16[16,48,768]{2,1,0:T(8,128)(2,1)S(1)}, bf16[16,48,768]{2,1,0:T(8,128)(2,1)S(1)}, u32[]{:S(2)}, u32[]{:S(2)}) collective-permute-start(bf16[16,48,768]{2,1,0:T(8,128)(2,1)S(1)} %collective-permute-done.29.src.refs_2_), channel_id=1, source_target_pairs={{0,1},{1,0},{2,3},{3,2},{4,5},{5,4},{6,7},{7,6},{8,9},{9,8},{10,11... | collective-permute-start | bytes 3538952 | tf_op jit(solution)/shard_map/ppermute | solution.py:27
  127.2 15.2 %collective-permute-start.33 = (bf16[16,48,768]{2,1,0:T(8,128)(2,1)S(1)}, bf16[16,48,768]{2,1,0:T(8,128)(2,1)S(1)}, u32[]{:S(2)}, u32[]{:S(2)}) collective-permute-start(bf16[16,48,768]{2,1,0:T(8,128)(2,1)S(1)} %collective-permute-done.28.src.refs_1_), channel_id=1, source_target_pairs={{0,1},{1,0},{2,3},{3,2},{4,5},{5,4},{6,7},{7,6},{8,9},{9,8},{10,11... | collective-permute-start | bytes 3538952 | tf_op jit(solution)/shard_map/ppermute | solution.py:27
  (7 other events, 17.0 us)

commit v7 on v6

--- a/solution.py
+++ b/solution.py
@@ -311,8 +311,8 @@
         acc[...] = dot_t(far[...], tiles(5, 1))
 
     either(h != 0, far_straight, far_turned)
-    acc[...] += dot(beside([own[...], near1[...], far1[...]]), tiles(0, 3))
-    acc[...] += dot_t(beside([near3[...], far3[...]]), beside([tiles(3, 1), tiles(4, 1)]))
+    acc[...] += dot(beside([near1[...], far1[...]]), tiles(1, 2))
+    acc[...] += dot_t(beside([own[...], near3[...], far3[...]]), beside([tiles(0, 1), tiles(3, 1), tiles(4, 1)]))
 
     def finish(multiply, factor):
         for i, near2 in enumerate((near2a, near2b)):

time: 153 us -> 153 us (level)
  no operation moved by 1% of the time
where the time goes in v7:
time: 153 us; the launch traced here: 152 us
  waiting for transfers between devices  79.6 us (52%)
  starting transfers between devices  50.2 us (33%)
  Pallas kernels  19 us (12%)
  local copies, waits for them, and re-layouts  2.48 us (2%)
    ppermute x22, waiting for transfers between devices, ring(): lax.ppermute(a, axis, [(i, (i + step) % 4) for i in range(4)])  69.8 us
    ppermute x22, starting transfers between devices, ring(): lax.ppermute(a, axis, [(i, (i + step) % 4) for i in range(4)])  31.4 us
    ppermute x15, starting transfers between devices, swap(): return lambda a: lax.ppermute(a, axis, [(0, 1), (1, 0)])  18.7 us
    pallas_call x1, Pallas kernels, product(): pl.pallas_call(product_kernel, out_shape=(jax.ShapeDtypeStruct((T, T), BF...  9.86 us
    ppermute x15, waiting for transfers between devices, swap(): return lambda a: lax.ppermute(a, axis, [(0, 1), (1, 0)])  9.76 us
    pallas_call x4, Pallas kernels, gram(): pl.pallas_call(kernel, out_shape=(out, out), in_specs=[VMEM] * (len(tiles...  6.37 us
  transfers between devices with their start and end apart: 37, of which 18 were waited for; matrix products, arithmetic and copies ran while one was open for 0% of the time, Pallas kernels for 2%

profile of v7, /device:TPU:1, one launch (start us, length us, event | category | flops | bytes accessed | tf_op | source)
XLA Modules:
  0.0 152.5 jit_solution(14694773161509992153)
XLA Ops:
  0.6 1.7 %copy-done = s32[768,768]{1,0:T(8,128)S(1)} copy-done((s32[768,768]{1,0:T(8,128)S(1)}, s32[768,768]{1,0:T(8,128)}, u32[]{:S(2)}) %copy-start) | copy-done | bytes 2359320
  4.5 2.1 %collective-permute-start.8 = (bf16[768,768]{1,0:T(8,128)(2,1)S(1)}, bf16[768,768]{1,0:T(8,128)(2,1)S(1)}, u32[]{:S(2)}, u32[]{:S(2)}) collective-permute-start(bf16[768,768]{1,0:T(8,128)(2,1)S(1)} %shard_map.41.own), channel_id=1, source_target_pairs={{0,4},{4,8},{8,12},{12,0},{1,5},{5,9},{9,13},{13,1},{2,6},{6,10},{... | collective-permute-start | bytes 3538952 | tf_op jit(solution)/shard_map/ppermute | solution.py:23
  6.7 2.9 %collective-permute-start.1 = (bf16[768,768]{1,0:T(8,128)(2,1)S(1)}, bf16[768,768]{1,0:T(8,128)(2,1)S(1)}, u32[]{:S(2)}, u32[]{:S(2)}) collective-permute-start(bf16[768,768]{1,0:T(8,128)(2,1)S(1)} %shard_map.41.own), channel_id=1, source_target_pairs={{0,2},{2,0},{1,3},{3,1},{4,6},{6,4},{5,7},{7,5},{8,10},{10,8},{9,1... | collective-permute-start | bytes 3538952 | tf_op jit(solution)/shard_map/ppermute | solution.py:27
  12.3 1.6 %collective-permute-start.2 = (bf16[4,96,768]{2,1,0:T(8,128)(2,1)S(1)}, bf16[4,96,768]{2,1,0:T(8,128)(2,1)S(1)}, u32[]{:S(2)}, u32[]{:S(2)}) collective-permute-start(bf16[4,96,768]{2,1,0:T(8,128)(2,1)S(1)} %get-tuple-element.21), channel_id=1, source_target_pairs={{0,1},{1,0},{2,3},{3,2},{4,5},{5,4},{6,7},{7,6},{8,9},{9,8},{10,11... | collective-permute-start | bytes 1769480 | tf_op jit(solution)/shard_map/ppermute | solution.py:27
  13.9 1.6 %collective-permute-done.2.other = bf16[4,96,768]{2,1,0:T(8,128)(2,1)S(1)} collective-permute-done((bf16[4,96,768]{2,1,0:T(8,128)(2,1)S(1)}, bf16[4,96,768]{2,1,0:T(8,128)(2,1)S(1)}, u32[]{:S(2)}, u32[]{:S(2)}) %collective-permute-start.2) | collective-permute-done | bytes 589856 | tf_op jit(solution)/shard_map/ppermute | solution.py:27
  15.5 1.7 %collective-permute-start.3 = (bf16[48,768]{1,0:T(8,128)(2,1)S(1)}, bf16[48,768]{1,0:T(8,128)(2,1)S(1)}, u32[]{:S(2)}, u32[]{:S(2)}) collective-permute-start(bf16[48,768]{1,0:T(8,128)(2,1)S(1)} %get-tuple-element.22), channel_id=1, source_target_pairs={{0,16},{16,32},{32,48},{48,0},{1,17},{17,33},{33,49},{49,1},{2,18}... | collective-permute-start | bytes 221192 | tf_op jit(solution)/shard_map/ppermute | solution.py:23
  17.3 2.2 %collective-permute-start.4 = (bf16[48,768]{1,0:T(8,128)(2,1)S(1)}, bf16[48,768]{1,0:T(8,128)(2,1)S(1)}, u32[]{:S(2)}, u32[]{:S(2)}) collective-permute-start(bf16[48,768]{1,0:T(8,128)(2,1)S(1)} %get-tuple-element.23), channel_id=1, source_target_pairs={{0,48},{16,0},{32,16},{48,32},{1,49},{17,1},{33,17},{49,33},{2,50}... | collective-permute-start | bytes 221192 | tf_op jit(solution)/shard_map/ppermute | solution.py:23
  19.5 2.3 %collective-permute-done.3.from_down = bf16[48,768]{1,0:T(8,128)(2,1)S(1)} collective-permute-done((bf16[48,768]{1,0:T(8,128)(2,1)S(1)}, bf16[48,768]{1,0:T(8,128)(2,1)S(1)}, u32[]{:S(2)}, u32[]{:S(2)}) %collective-permute-start.3) | collective-permute-done | bytes 73760 | tf_op jit(solution)/shard_map/ppermute | solution.py:23
  22.6 2.0 %collective-permute-start.6 = (bf16[96,768]{1,0:T(8,128)(2,1)S(1)}, bf16[96,768]{1,0:T(8,128)(2,1)S(1)}, u32[]{:S(2)}, u32[]{:S(2)}) collective-permute-start(bf16[96,768]{1,0:T(8,128)(2,1)S(1)} %get-tuple-element.25), channel_id=1, source_target_pairs={{0,48},{16,0},{32,16},{48,32},{1,49},{17,1},{33,17},{49,33},{2,50}... | collective-permute-start | bytes 442376 | tf_op jit(solution)/shard_map/ppermute | solution.py:23
  24.6 3.0 %collective-permute-done.5.from_down = bf16[96,768]{1,0:T(8,128)(2,1)S(1)} collective-permute-done((bf16[96,768]{1,0:T(8,128)(2,1)S(1)}, bf16[96,768]{1,0:T(8,128)(2,1)S(1)}, u32[]{:S(2)}, u32[]{:S(2)}) %collective-permute-start.5) | collective-permute-done | bytes 147488 | tf_op jit(solution)/shard_map/ppermute | solution.py:23
  27.7 5.5 %collective-permute-done.8.src.near3 = bf16[768,768]{1,0:T(8,128)(2,1)S(1)} collective-permute-done((bf16[768,768]{1,0:T(8,128)(2,1)S(1)}, bf16[768,768]{1,0:T(8,128)(2,1)S(1)}, u32[]{:S(2)}, u32[]{:S(2)}) %collective-permute-start.8) | collective-permute-done | bytes 1179680 | tf_op jit(solution)/shard_map/ppermute | solution.py:23
  35.8 2.0 %shard_map.48 = (bf16[4,144,768]{2,1,0:T(8,128)(2,1)S(1)}, bf16[4,144,768]{2,1,0:T(8,128)(2,1)S(1)}) custom-call(bf16[768,768]{1,0:T(8,128)(2,1)S(1)} %shard_map.41.own, bf16[768,768]{1,0:T(8,128)(2,1)S(1)} %collective-permute-done.src.near1, bf16[768,768]{1,0:T(8,128)(2,1)S(1)} %collective-permute-done.1.refs_1_.far.src, ...), custom_call_target="tpu_custom_call" | custom-call | flops 1358954496 | bytes 3538944 | tf_op jit(solution)/shard_map/pallas_call | solution.py:131
  37.8 2.2 %collective-permute-start.9 = (bf16[4,144,768]{2,1,0:T(8,128)(2,1)S(1)}, bf16[4,144,768]{2,1,0:T(8,128)(2,1)S(1)}, u32[]{:S(2)}, u32[]{:S(2)}) collective-permute-start(bf16[4,144,768]{2,1,0:T(8,128)(2,1)S(1)} %get-tuple-element.27), channel_id=1, source_target_pairs={{0,1},{1,0},{2,3},{3,2},{4,5},{5,4},{6,7},{7,6},{8,9},{9,8},{10,11... | collective-permute-start | bytes 2654216 | tf_op jit(solution)/shard_map/ppermute | solution.py:27
  44.5 1.7 %collective-permute-start.11 = (bf16[240,768]{1,0:T(8,128)(2,1)S(1)}, bf16[240,768]{1,0:T(8,128)(2,1)S(1)}, u32[]{:S(2)}, u32[]{:S(2)}) collective-permute-start(bf16[240,768]{1,0:T(8,128)(2,1)S(1)} %get-tuple-element.30), channel_id=1, source_target_pairs={{0,16},{16,32},{32,48},{48,0},{1,17},{17,33},{33,49},{49,1},{2,18}... | collective-permute-start | bytes 1105928 | tf_op jit(solution)/shard_map/ppermute | solution.py:23
  46.2 2.2 %collective-permute-start.12 = (bf16[240,768]{1,0:T(8,128)(2,1)S(1)}, bf16[240,768]{1,0:T(8,128)(2,1)S(1)}, u32[]{:S(2)}, u32[]{:S(2)}) collective-permute-start(bf16[240,768]{1,0:T(8,128)(2,1)S(1)} %get-tuple-element.31), channel_id=1, source_target_pairs={{0,48},{16,0},{32,16},{48,32},{1,49},{17,1},{33,17},{49,33},{2,50}... | collective-permute-start | bytes 1105928 | tf_op jit(solution)/shard_map/ppermute | solution.py:23
  49.6 6.7 %collective-permute-done.11.refs_4_ = bf16[240,768]{1,0:T(8,128)(2,1)S(1)} collective-permute-done((bf16[240,768]{1,0:T(8,128)(2,1)S(1)}, bf16[240,768]{1,0:T(8,128)(2,1)S(1)}, u32[]{:S(2)}, u32[]{:S(2)}) %collective-permute-start.11) | collective-permute-done | bytes 368672 | tf_op jit(solution)/shard_map/ppermute | solution.py:23
  56.4 8.8 %collective-permute-done.13.refs_6_ = bf16[240,768]{1,0:T(8,128)(2,1)S(1)} collective-permute-done((bf16[240,768]{1,0:T(8,128)(2,1)S(1)}, bf16[240,768]{1,0:T(8,128)(2,1)S(1)}, u32[]{:S(2)}, u32[]{:S(2)}) %collective-permute-start.13) | collective-permute-done | bytes 368672 | tf_op jit(solution)/shard_map/ppermute | solution.py:23
  65.4 1.9 %shard_map.52 = (bf16[4,96,768]{2,1,0:T(8,128)(2,1)S(1)}, bf16[4,96,768]{2,1,0:T(8,128)(2,1)S(1)}) custom-call(bf16[768,768]{1,0:T(8,128)(2,1)S(1)} %shard_map.41.own, bf16[768,768]{1,0:T(8,128)(2,1)S(1)} %collective-permute-done.1.refs_1_.far.src, bf16[384,768]{1,0:T(8,128)(2,1)S(1)} %collective-permute-done.16.near2a.top, ...), custom_call_target="tpu_custom_call" | custom-call | flops 905969664 | bytes 3538944 | tf_op jit(solution)/shard_map/pallas_call | solution.py:131
  67.3 1.9 %collective-permute-start.18 = (bf16[4,96,768]{2,1,0:T(8,128)(2,1)S(1)}, bf16[4,96,768]{2,1,0:T(8,128)(2,1)S(1)}, u32[]{:S(2)}, u32[]{:S(2)}) collective-permute-start(bf16[4,96,768]{2,1,0:T(8,128)(2,1)S(1)} %get-tuple-element.34), channel_id=1, source_target_pairs={{0,1},{1,0},{2,3},{3,2},{4,5},{5,4},{6,7},{7,6},{8,9},{9,8},{10,11... | collective-permute-start | bytes 1769480 | tf_op jit(solution)/shard_map/ppermute | solution.py:27
  71.9 1.8 %collective-permute-start.20 = (bf16[96,768]{1,0:T(8,128)(2,1)S(1)}, bf16[96,768]{1,0:T(8,128)(2,1)S(1)}, u32[]{:S(2)}, u32[]{:S(2)}) collective-permute-start(bf16[96,768]{1,0:T(8,128)(2,1)S(1)} %get-tuple-element.36), channel_id=1, source_target_pairs={{0,48},{16,0},{32,16},{48,32},{1,49},{17,1},{33,17},{49,33},{2,50}... | collective-permute-start | bytes 442376 | tf_op jit(solution)/shard_map/ppermute | solution.py:23
  74.2 3.1 %collective-permute-done.19.refs_2_ = bf16[96,768]{1,0:T(8,128)(2,1)S(1)} collective-permute-done((bf16[96,768]{1,0:T(8,128)(2,1)S(1)}, bf16[96,768]{1,0:T(8,128)(2,1)S(1)}, u32[]{:S(2)}, u32[]{:S(2)}) %collective-permute-start.19) | collective-permute-done | bytes 147488 | tf_op jit(solution)/shard_map/ppermute | solution.py:23
  77.3 2.9 %collective-permute-done.21.refs_4_ = bf16[96,768]{1,0:T(8,128)(2,1)S(1)} collective-permute-done((bf16[96,768]{1,0:T(8,128)(2,1)S(1)}, bf16[96,768]{1,0:T(8,128)(2,1)S(1)}, u32[]{:S(2)}, u32[]{:S(2)}) %collective-permute-start.21) | collective-permute-done | bytes 147488 | tf_op jit(solution)/shard_map/ppermute | solution.py:23
  81.3 3.0 %collective-permute-done.22 = bf16[96,768]{1,0:T(8,128)(2,1)S(1)} collective-permute-done((bf16[96,768]{1,0:T(8,128)(2,1)S(1)}, bf16[96,768]{1,0:T(8,128)(2,1)S(1)}, u32[]{:S(2)}, u32[]{:S(2)}) %collective-permute-start.22) | collective-permute-done | bytes 147488 | tf_op jit(solution)/shard_map/ppermute | solution.py:27
  86.0 1.7 %collective-permute-start.23 = (bf16[96,768]{1,0:T(8,128)(2,1)S(1)}, bf16[96,768]{1,0:T(8,128)(2,1)S(1)}, u32[]{:S(2)}, u32[]{:S(2)}) collective-permute-start(bf16[96,768]{1,0:T(8,128)(2,1)S(1)} %multiply_convert_fusion.1.second.shard2), channel_id=1, source_target_pairs={{0,8},{4,12},{8,0},{12,4},{1,9},{5,13},{9,1},{13,5},{2,10},{6,14},... | collective-permute-start | bytes 442376 | tf_op jit(solution)/shard_map/ppermute | solution.py:23
  88.8 4.3 %collective-permute-done.23.from_x2 = bf16[96,768]{1,0:T(8,128)(2,1)S(1)} collective-permute-done((bf16[96,768]{1,0:T(8,128)(2,1)S(1)}, bf16[96,768]{1,0:T(8,128)(2,1)S(1)}, u32[]{:S(2)}, u32[]{:S(2)}) %collective-permute-start.23) | collective-permute-done | bytes 147488 | tf_op jit(solution)/shard_map/ppermute | solution.py:23
  94.2 1.8 %collective-permute-start.28 = (bf16[16,48,768]{2,1,0:T(8,128)(2,1)S(1)}, bf16[16,48,768]{2,1,0:T(8,128)(2,1)S(1)}, u32[]{:S(2)}, u32[]{:S(2)}) collective-permute-start(bf16[16,48,768]{2,1,0:T(8,128)(2,1)S(1)} %bitcast.2), channel_id=1, source_target_pairs={{0,48},{16,0},{32,16},{48,32},{1,49},{17,1},{33,17},{49,33},{2,50}... | collective-permute-start | bytes 3538952 | tf_op jit(solution)/shard_map/ppermute | solution.py:23
  97.6 2.7 %collective-permute-start.25 = (bf16[768,768]{1,0:T(8,128)(2,1)S(1)}, bf16[768,768]{1,0:T(8,128)(2,1)S(1)}, u32[]{:S(2)}, u32[]{:S(2)}) collective-permute-start(bf16[768,768]{1,0:T(8,128)(2,1)S(1)} %shard_map.57), channel_id=1, source_target_pairs={{0,12},{4,0},{8,4},{12,8},{1,13},{5,1},{9,5},{13,9},{2,14},{6,2},{... | collective-permute-start | bytes 3538952 | tf_op jit(solution)/shard_map/ppermute | solution.py:23
  100.3 19.1 %collective-permute-done.29.src.refs_2_ = bf16[16,48,768]{2,1,0:T(8,128)(2,1)S(1)} collective-permute-done((bf16[16,48,768]{2,1,0:T(8,128)(2,1)S(1)}, bf16[16,48,768]{2,1,0:T(8,128)(2,1)S(1)}, u32[]{:S(2)}, u32[]{:S(2)}) %collective-permute-start.29) | collective-permute-done | bytes 1179680 | tf_op jit(solution)/shard_map/ppermute | solution.py:23
  119.4 3.4 %collective-permute-start.32 = (bf16[16,48,768]{2,1,0:T(8,128)(2,1)S(1)}, bf16[16,48,768]{2,1,0:T(8,128)(2,1)S(1)}, u32[]{:S(2)}, u32[]{:S(2)}) collective-permute-start(bf16[16,48,768]{2,1,0:T(8,128)(2,1)S(1)} %bitcast.3), channel_id=1, source_target_pairs={{0,1},{1,0},{2,3},{3,2},{4,5},{5,4},{6,7},{7,6},{8,9},{9,8},{10,11... | collective-permute-start | bytes 3538952 | tf_op jit(solution)/shard_map/ppermute | solution.py:27
  123.1 2.7 %collective-permute-start.30 = (bf16[8,48,768]{2,1,0:T(8,128)(2,1)S(1)}, bf16[8,48,768]{2,1,0:T(8,128)(2,1)S(1)}, u32[]{:S(2)}, u32[]{:S(2)}) collective-permute-start(bf16[8,48,768]{2,1,0:T(8,128)(2,1)S(1)} %shard_map.59), channel_id=1, source_target_pairs={{0,48},{16,0},{32,16},{48,32},{1,49},{17,1},{33,17},{49,33},{2,50}... | collective-permute-start | bytes 1769480 | tf_op jit(solution)/shard_map/ppermute | solution.py:23
  127.2 11.9 %collective-permute-done.31.refs_0_ = bf16[8,48,768]{2,1,0:T(8,128)(2,1)S(1)} collective-permute-done((bf16[8,48,768]{2,1,0:T(8,128)(2,1)S(1)}, bf16[8,48,768]{2,1,0:T(8,128)(2,1)S(1)}, u32[]{:S(2)}, u32[]{:S(2)}) %collective-permute-start.31) | collective-permute-done | bytes 589856 | tf_op jit(solution)/shard_map/ppermute | solution.py:23
  142.4 9.9 %shard_map.63 = (bf16[768,768]{1,0:T(8,128)(2,1)}, bf16[384,768]{1,0:T(8,128)(2,1)}) custom-call(bf16[768,768]{1,0:T(8,128)(2,1)S(1)} %shard_map.41.own, bf16[768,768]{1,0:T(8,128)(2,1)S(1)} %collective-permute-done.src.near1, bf16[768,768]{1,0:T(8,128)(2,1)S(1)} %collective-permute-done.25.refs_1_.far1, ...), custom_call_target="tpu_custom_call" | custom-call | flops 7247757312 | bytes 21233664 | tf_op jit(solution)/shard_map/pallas_call | solution.py:335
  (73 shorter events, 29.1 us)
Async XLA Ops:
  4.5 28.6 %collective-permute-start.8 = (bf16[768,768]{1,0:T(8,128)(2,1)S(1)}, bf16[768,768]{1,0:T(8,128)(2,1)S(1)}, u32[]{:S(2)}, u32[]{:S(2)}) collective-permute-start(bf16[768,768]{1,0:T(8,128)(2,1)S(1)} %shard_map.41.own), channel_id=1, source_target_pairs={{0,4},{4,8},{8,12},{12,0},{1,5},{5,9},{9,13},{13,1},{2,6},{6,10},{... | collective-permute-start | bytes 3538952 | tf_op jit(solution)/shard_map/ppermute | solution.py:23
  6.7 28.0 %collective-permute-start.1 = (bf16[768,768]{1,0:T(8,128)(2,1)S(1)}, bf16[768,768]{1,0:T(8,128)(2,1)S(1)}, u32[]{:S(2)}, u32[]{:S(2)}) collective-permute-start(bf16[768,768]{1,0:T(8,128)(2,1)S(1)} %shard_map.41.own), channel_id=1, source_target_pairs={{0,2},{2,0},{1,3},{3,1},{4,6},{6,4},{5,7},{7,5},{8,10},{10,8},{9,1... | collective-permute-start | bytes 3538952 | tf_op jit(solution)/shard_map/ppermute | solution.py:27
  9.6 26.2 %collective-permute-start = (bf16[768,768]{1,0:T(8,128)(2,1)S(1)}, bf16[768,768]{1,0:T(8,128)(2,1)S(1)}, u32[]{:S(2)}, u32[]{:S(2)}) collective-permute-start(bf16[768,768]{1,0:T(8,128)(2,1)S(1)} %shard_map.41.own), channel_id=1, source_target_pairs={{0,12},{4,0},{8,4},{12,8},{1,13},{5,1},{9,5},{13,9},{2,14},{6,2},{... | collective-permute-start | bytes 3538952 | tf_op jit(solution)/shard_map/ppermute | solution.py:23
  15.5 6.2 %collective-permute-start.3 = (bf16[48,768]{1,0:T(8,128)(2,1)S(1)}, bf16[48,768]{1,0:T(8,128)(2,1)S(1)}, u32[]{:S(2)}, u32[]{:S(2)}) collective-permute-start(bf16[48,768]{1,0:T(8,128)(2,1)S(1)} %get-tuple-element.22), channel_id=1, source_target_pairs={{0,16},{16,32},{32,48},{48,0},{1,17},{17,33},{33,49},{49,1},{2,18}... | collective-permute-start | bytes 221192 | tf_op jit(solution)/shard_map/ppermute | solution.py:23
  17.3 4.5 %collective-permute-start.4 = (bf16[48,768]{1,0:T(8,128)(2,1)S(1)}, bf16[48,768]{1,0:T(8,128)(2,1)S(1)}, u32[]{:S(2)}, u32[]{:S(2)}) collective-permute-start(bf16[48,768]{1,0:T(8,128)(2,1)S(1)} %get-tuple-element.23), channel_id=1, source_target_pairs={{0,48},{16,0},{32,16},{48,32},{1,49},{17,1},{33,17},{49,33},{2,50}... | collective-permute-start | bytes 221192 | tf_op jit(solution)/shard_map/ppermute | solution.py:23
  21.8 5.8 %collective-permute-start.5 = (bf16[96,768]{1,0:T(8,128)(2,1)S(1)}, bf16[96,768]{1,0:T(8,128)(2,1)S(1)}, u32[]{:S(2)}, u32[]{:S(2)}) collective-permute-start(bf16[96,768]{1,0:T(8,128)(2,1)S(1)} %get-tuple-element.24), channel_id=1, source_target_pairs={{0,16},{16,32},{32,48},{48,0},{1,17},{17,33},{33,49},{49,1},{2,18}... | collective-permute-start | bytes 442376 | tf_op jit(solution)/shard_map/ppermute | solution.py:23
  22.6 5.0 %collective-permute-start.6 = (bf16[96,768]{1,0:T(8,128)(2,1)S(1)}, bf16[96,768]{1,0:T(8,128)(2,1)S(1)}, u32[]{:S(2)}, u32[]{:S(2)}) collective-permute-start(bf16[96,768]{1,0:T(8,128)(2,1)S(1)} %get-tuple-element.25), channel_id=1, source_target_pairs={{0,48},{16,0},{32,16},{48,32},{1,49},{17,1},{33,17},{49,33},{2,50}... | collective-permute-start | bytes 442376 | tf_op jit(solution)/shard_map/ppermute | solution.py:23
  37.8 6.4 %collective-permute-start.9 = (bf16[4,144,768]{2,1,0:T(8,128)(2,1)S(1)}, bf16[4,144,768]{2,1,0:T(8,128)(2,1)S(1)}, u32[]{:S(2)}, u32[]{:S(2)}) collective-permute-start(bf16[4,144,768]{2,1,0:T(8,128)(2,1)S(1)} %get-tuple-element.27), channel_id=1, source_target_pairs={{0,1},{1,0},{2,3},{3,2},{4,5},{5,4},{6,7},{7,6},{8,9},{9,8},{10,11... | collective-permute-start | bytes 2654216 | tf_op jit(solution)/shard_map/ppermute | solution.py:27
  41.4 24.0 %collective-permute-start.17 = (bf16[384,768]{1,0:T(8,128)(2,1)S(1)}, bf16[384,768]{1,0:T(8,128)(2,1)S(1)}, u32[]{:S(2)}, u32[]{:S(2)}) collective-permute-start(bf16[384,768]{1,0:T(8,128)(2,1)S(1)} %shard_map.47.___), channel_id=1, source_target_pairs={{0,4},{4,8},{8,12},{12,0},{1,5},{5,9},{9,13},{13,1},{2,6},{6,10},{... | collective-permute-start | bytes 1769480 | tf_op jit(solution)/shard_map/ppermute | solution.py:23
  42.7 22.7 %collective-permute-start.16 = (bf16[384,768]{1,0:T(8,128)(2,1)S(1)}, bf16[384,768]{1,0:T(8,128)(2,1)S(1)}, u32[]{:S(2)}, u32[]{:S(2)}) collective-permute-start(bf16[384,768]{1,0:T(8,128)(2,1)S(1)} %shard_map.46.__), channel_id=1, source_target_pairs={{0,12},{4,0},{8,4},{12,8},{1,13},{5,1},{9,5},{13,9},{2,14},{6,2},{... | collective-permute-start | bytes 1769480 | tf_op jit(solution)/shard_map/ppermute | solution.py:23
  44.5 11.9 %collective-permute-start.11 = (bf16[240,768]{1,0:T(8,128)(2,1)S(1)}, bf16[240,768]{1,0:T(8,128)(2,1)S(1)}, u32[]{:S(2)}, u32[]{:S(2)}) collective-permute-start(bf16[240,768]{1,0:T(8,128)(2,1)S(1)} %get-tuple-element.30), channel_id=1, source_target_pairs={{0,16},{16,32},{32,48},{48,0},{1,17},{17,33},{33,49},{49,1},{2,18}... | collective-permute-start | bytes 1105928 | tf_op jit(solution)/shard_map/ppermute | solution.py:23
  46.2 10.2 %collective-permute-start.12 = (bf16[240,768]{1,0:T(8,128)(2,1)S(1)}, bf16[240,768]{1,0:T(8,128)(2,1)S(1)}, u32[]{:S(2)}, u32[]{:S(2)}) collective-permute-start(bf16[240,768]{1,0:T(8,128)(2,1)S(1)} %get-tuple-element.31), channel_id=1, source_target_pairs={{0,48},{16,0},{32,16},{48,32},{1,49},{17,1},{33,17},{49,33},{2,50}... | collective-permute-start | bytes 1105928 | tf_op jit(solution)/shard_map/ppermute | solution.py:23
  48.4 16.7 %collective-permute-start.13 = (bf16[240,768]{1,0:T(8,128)(2,1)S(1)}, bf16[240,768]{1,0:T(8,128)(2,1)S(1)}, u32[]{:S(2)}, u32[]{:S(2)}) collective-permute-start(bf16[240,768]{1,0:T(8,128)(2,1)S(1)} %get-tuple-element.32), channel_id=1, source_target_pairs={{0,32},{16,48},{32,0},{48,16},{1,33},{17,49},{33,1},{49,17},{2,34}... | collective-permute-start | bytes 1105928 | tf_op jit(solution)/shard_map/ppermute | solution.py:23
  69.2 11.5 %collective-permute-start.14 = (bf16[240,768]{1,0:T(8,128)(2,1)S(1)}, bf16[240,768]{1,0:T(8,128)(2,1)S(1)}, u32[]{:S(2)}, u32[]{:S(2)}) collective-permute-start(bf16[240,768]{1,0:T(8,128)(2,1)S(1)} %shard_map.51._), channel_id=1, source_target_pairs={{0,64},{64,0},{1,65},{65,1},{2,66},{66,2},{3,67},{67,3},{4,68},{68... | collective-permute-start | bytes 1105928 | tf_op jit(solution)/shard_map/ppermute | solution.py:27
  70.9 6.3 %collective-permute-start.19 = (bf16[96,768]{1,0:T(8,128)(2,1)S(1)}, bf16[96,768]{1,0:T(8,128)(2,1)S(1)}, u32[]{:S(2)}, u32[]{:S(2)}) collective-permute-start(bf16[96,768]{1,0:T(8,128)(2,1)S(1)} %get-tuple-element.35), channel_id=1, source_target_pairs={{0,16},{16,32},{32,48},{48,0},{1,17},{17,33},{33,49},{49,1},{2,18}... | collective-permute-start | bytes 442376 | tf_op jit(solution)/shard_map/ppermute | solution.py:23
  71.9 5.4 %collective-permute-start.20 = (bf16[96,768]{1,0:T(8,128)(2,1)S(1)}, bf16[96,768]{1,0:T(8,128)(2,1)S(1)}, u32[]{:S(2)}, u32[]{:S(2)}) collective-permute-start(bf16[96,768]{1,0:T(8,128)(2,1)S(1)} %get-tuple-element.36), channel_id=1, source_target_pairs={{0,48},{16,0},{32,16},{48,32},{1,49},{17,1},{33,17},{49,33},{2,50}... | collective-permute-start | bytes 442376 | tf_op jit(solution)/shard_map/ppermute | solution.py:23
  73.7 6.5 %collective-permute-start.21 = (bf16[96,768]{1,0:T(8,128)(2,1)S(1)}, bf16[96,768]{1,0:T(8,128)(2,1)S(1)}, u32[]{:S(2)}, u32[]{:S(2)}) collective-permute-start(bf16[96,768]{1,0:T(8,128)(2,1)S(1)} %get-tuple-element.37), channel_id=1, source_target_pairs={{0,32},{16,48},{32,0},{48,16},{1,33},{17,49},{33,1},{49,17},{2,34}... | collective-permute-start | bytes 442376 | tf_op jit(solution)/shard_map/ppermute | solution.py:23
  73.8 13.9 %collective-permute-start.7 = (bf16[96,768]{1,0:T(8,128)(2,1)S(1)}, bf16[96,768]{1,0:T(8,128)(2,1)S(1)}, u32[]{:S(2)}, u32[]{:S(2)}) collective-permute-start(bf16[96,768]{1,0:T(8,128)(2,1)S(1)} %shard_map.45.refs_0_._), channel_id=1, source_target_pairs={{0,64},{64,0},{1,65},{65,1},{2,66},{66,2},{3,67},{67,3},{4,68},{68... | collective-permute-start | bytes 442376 | tf_op jit(solution)/shard_map/ppermute | solution.py:27
  80.3 4.1 %collective-permute-start.22 = (bf16[96,768]{1,0:T(8,128)(2,1)S(1)}, bf16[96,768]{1,0:T(8,128)(2,1)S(1)}, u32[]{:S(2)}, u32[]{:S(2)}) collective-permute-start(bf16[96,768]{1,0:T(8,128)(2,1)S(1)} %shard_map.54), channel_id=1, source_target_pairs={{0,64},{64,0},{1,65},{65,1},{2,66},{66,2},{3,67},{67,3},{4,68},{68... | collective-permute-start | bytes 442376 | tf_op jit(solution)/shard_map/ppermute | solution.py:27
  80.9 7.9 %collective-permute-start.15 = (bf16[192,768]{1,0:T(8,128)(2,1)S(1)}, bf16[192,768]{1,0:T(8,128)(2,1)S(1)}, u32[]{:S(2)}, u32[]{:S(2)}) collective-permute-start(bf16[192,768]{1,0:T(8,128)(2,1)S(1)} %slice.4), channel_id=1, source_target_pairs={{0,4},{4,8},{8,12},{12,0},{1,5},{5,9},{9,13},{13,1},{2,6},{6,10},{... | collective-permute-start | bytes 884744 | tf_op jit(solution)/shard_map/ppermute | solution.py:23
  84.4 8.7 %collective-permute-start.24 = (bf16[192,768]{1,0:T(8,128)(2,1)S(1)}, bf16[192,768]{1,0:T(8,128)(2,1)S(1)}, u32[]{:S(2)}, u32[]{:S(2)}) collective-permute-start(bf16[192,768]{1,0:T(8,128)(2,1)S(1)} %shard_map.55), channel_id=1, source_target_pairs={{0,2},{2,0},{1,3},{3,1},{4,6},{6,4},{5,7},{7,5},{8,10},{10,8},{9,1... | collective-permute-start | bytes 884744 | tf_op jit(solution)/shard_map/ppermute | solution.py:27
  86.0 7.1 %collective-permute-start.23 = (bf16[96,768]{1,0:T(8,128)(2,1)S(1)}, bf16[96,768]{1,0:T(8,128)(2,1)S(1)}, u32[]{:S(2)}, u32[]{:S(2)}) collective-permute-start(bf16[96,768]{1,0:T(8,128)(2,1)S(1)} %multiply_convert_fusion.1.second.shard2), channel_id=1, source_target_pairs={{0,8},{4,12},{8,0},{12,4},{1,9},{5,13},{9,1},{13,5},{2,10},{6,14},... | collective-permute-start | bytes 442376 | tf_op jit(solution)/shard_map/ppermute | solution.py:23
  93.2 26.2 %collective-permute-start.29 = (bf16[16,48,768]{2,1,0:T(8,128)(2,1)S(1)}, bf16[16,48,768]{2,1,0:T(8,128)(2,1)S(1)}, u32[]{:S(2)}, u32[]{:S(2)}) collective-permute-start(bf16[16,48,768]{2,1,0:T(8,128)(2,1)S(1)} %bitcast.1), channel_id=1, source_target_pairs={{0,16},{16,32},{32,48},{48,0},{1,17},{17,33},{33,49},{49,1},{2,18}... | collective-permute-start | bytes 3538952 | tf_op jit(solution)/shard_map/ppermute | solution.py:23
  94.2 28.7 %collective-permute-start.28 = (bf16[16,48,768]{2,1,0:T(8,128)(2,1)S(1)}, bf16[16,48,768]{2,1,0:T(8,128)(2,1)S(1)}, u32[]{:S(2)}, u32[]{:S(2)}) collective-permute-start(bf16[16,48,768]{2,1,0:T(8,128)(2,1)S(1)} %bitcast.2), channel_id=1, source_target_pairs={{0,48},{16,0},{32,16},{48,32},{1,49},{17,1},{33,17},{49,33},{2,50}... | collective-permute-start | bytes 3538952 | tf_op jit(solution)/shard_map/ppermute | solution.py:23
  96.0 27.0 %collective-permute-start.27 = (bf16[768,768]{1,0:T(8,128)(2,1)S(1)}, bf16[768,768]{1,0:T(8,128)(2,1)S(1)}, u32[]{:S(2)}, u32[]{:S(2)}) collective-permute-start(bf16[768,768]{1,0:T(8,128)(2,1)S(1)} %shard_map.58), channel_id=1, source_target_pairs={{0,2},{2,0},{1,3},{3,1},{4,6},{6,4},{5,7},{7,5},{8,10},{10,8},{9,1... | collective-permute-start | bytes 3538952 | tf_op jit(solution)/shard_map/ppermute | solution.py:27
  97.6 28.2 %collective-permute-start.26 = (bf16[768,768]{1,0:T(8,128)(2,1)S(1)}, bf16[768,768]{1,0:T(8,128)(2,1)S(1)}, u32[]{:S(2)}, u32[]{:S(2)}) collective-permute-start(bf16[768,768]{1,0:T(8,128)(2,1)S(1)} %shard_map.57), channel_id=1, source_target_pairs={{0,4},{4,8},{8,12},{12,0},{1,5},{5,9},{9,13},{13,1},{2,6},{6,10},{... | collective-permute-start | bytes 3538952 | tf_op jit(solution)/shard_map/ppermute | solution.py:23
  97.6 29.6 %collective-permute-start.25 = (bf16[768,768]{1,0:T(8,128)(2,1)S(1)}, bf16[768,768]{1,0:T(8,128)(2,1)S(1)}, u32[]{:S(2)}, u32[]{:S(2)}) collective-permute-start(bf16[768,768]{1,0:T(8,128)(2,1)S(1)} %shard_map.57), channel_id=1, source_target_pairs={{0,12},{4,0},{8,4},{12,8},{1,13},{5,1},{9,5},{13,9},{2,14},{6,2},{... | collective-permute-start | bytes 3538952 | tf_op jit(solution)/shard_map/ppermute | solution.py:23
  119.4 20.6 %collective-permute-start.32 = (bf16[16,48,768]{2,1,0:T(8,128)(2,1)S(1)}, bf16[16,48,768]{2,1,0:T(8,128)(2,1)S(1)}, u32[]{:S(2)}, u32[]{:S(2)}) collective-permute-start(bf16[16,48,768]{2,1,0:T(8,128)(2,1)S(1)} %bitcast.3), channel_id=1, source_target_pairs={{0,1},{1,0},{2,3},{3,2},{4,5},{5,4},{6,7},{7,6},{8,9},{9,8},{10,11... | collective-permute-start | bytes 3538952 | tf_op jit(solution)/shard_map/ppermute | solution.py:27
  122.9 16.2 %collective-permute-start.31 = (bf16[8,48,768]{2,1,0:T(8,128)(2,1)S(1)}, bf16[8,48,768]{2,1,0:T(8,128)(2,1)S(1)}, u32[]{:S(2)}, u32[]{:S(2)}) collective-permute-start(bf16[8,48,768]{2,1,0:T(8,128)(2,1)S(1)} %shard_map.61), channel_id=1, source_target_pairs={{0,16},{16,32},{32,48},{48,0},{1,17},{17,33},{33,49},{49,1},{2,18}... | collective-permute-start | bytes 1769480 | tf_op jit(solution)/shard_map/ppermute | solution.py:23
  123.1 16.9 %collective-permute-start.30 = (bf16[8,48,768]{2,1,0:T(8,128)(2,1)S(1)}, bf16[8,48,768]{2,1,0:T(8,128)(2,1)S(1)}, u32[]{:S(2)}, u32[]{:S(2)}) collective-permute-start(bf16[8,48,768]{2,1,0:T(8,128)(2,1)S(1)} %shard_map.59), channel_id=1, source_target_pairs={{0,48},{16,0},{32,16},{48,32},{1,49},{17,1},{33,17},{49,33},{2,50}... | collective-permute-start | bytes 1769480 | tf_op jit(solution)/shard_map/ppermute | solution.py:23
  125.8 16.6 %collective-permute-start.34 = (bf16[16,48,768]{2,1,0:T(8,128)(2,1)S(1)}, bf16[16,48,768]{2,1,0:T(8,128)(2,1)S(1)}, u32[]{:S(2)}, u32[]{:S(2)}) collective-permute-start(bf16[16,48,768]{2,1,0:T(8,128)(2,1)S(1)} %collective-permute-done.29.src.refs_2_), channel_id=1, source_target_pairs={{0,1},{1,0},{2,3},{3,2},{4,5},{5,4},{6,7},{7,6},{8,9},{9,8},{10,11... | collective-permute-start | bytes 3538952 | tf_op jit(solution)/shard_map/ppermute | solution.py:27
  127.2 15.2 %collective-permute-start.33 = (bf16[16,48,768]{2,1,0:T(8,128)(2,1)S(1)}, bf16[16,48,768]{2,1,0:T(8,128)(2,1)S(1)}, u32[]{:S(2)}, u32[]{:S(2)}) collective-permute-start(bf16[16,48,768]{2,1,0:T(8,128)(2,1)S(1)} %collective-permute-done.28.src.refs_1_), channel_id=1, source_target_pairs={{0,1},{1,0},{2,3},{3,2},{4,5},{5,4},{6,7},{7,6},{8,9},{9,8},{10,11... | collective-permute-start | bytes 3538952 | tf_op jit(solution)/shard_map/ppermute | solution.py:27
  (7 other events, 17.0 us)
